TPU v7x, 32 devices: a whole 2x2x4 slice. The times are simulated.
32 devices in a mesh: section: 2 (over x), dp: 16 (over z, y, core).
Axes of the slice: x: 2, y: 2, z: 4, core: 2. Of those that a mesh axis runs over, the one named last changes fastest.
Arguments:
- text: bfloat16 [4096, 768], P('dp', 'section'), may hold values from -6 to 6
- image: bfloat16 [64, 576, 768], P('dp', 'section'), may hold values from -6 to 6
- lengths: int32 [64], P('dp'), may hold values from 5 to 64
- self_gain: bfloat16 [2, 768], P('section', 'dp'), may hold values from 0.25 to 1.75
- self_shift: bfloat16 [2, 768], P('section', 'dp'), may hold values from -1.75 to 1.75
- heads_in: bfloat16 [2, 768, 2304], P('section', 'dp'), may hold values from -0.3125 to 0.3125
- heads_out: bfloat16 [2, 768, 768], P('section', 'dp'), may hold values from -0.21875 to 0.21875
- feed_gain: bfloat16 [2, 768], P('section', 'dp'), may hold values from 0.25 to 1.75
- feed_shift: bfloat16 [2, 768], P('section', 'dp'), may hold values from -1.75 to 1.75
- up_weight: bfloat16 [2, 768, 3072], P('section', 'dp'), may hold values from -0.21875 to 0.21875
- up_bias: bfloat16 [2, 3072], P('section', 'dp'), may hold values from -1.75 to 1.75
- down_weight: bfloat16 [2, 3072, 768], P('section', 'dp'), may hold values from -0.109375 to 0.109375
- down_bias: bfloat16 [2, 768], P('section', 'dp'), may hold values from -1.75 to 1.75
- cross_gain: bfloat16 [768], P(('section', 'dp')), may hold values from 0.25 to 1.75
- cross_shift: bfloat16 [768], P(('section', 'dp')), may hold values from -1.75 to 1.75
- cross_query: bfloat16 [768, 768], P(('section', 'dp')), may hold values from -0.3125 to 0.3125
- cross_keys: bfloat16 [768, 1536], P(('section', 'dp')), may hold values from -0.21875 to 0.21875
- cross_out: bfloat16 [768, 768], P(('section', 'dp')), may hold values from -0.4375 to 0.4375
- cotangent: bfloat16 [4096, 768], P('dp', 'section'), may hold values from -6 to 6
Outputs:
- layer_out: float32 [4096, 768], P('dp', 'section')
- text_grad: float32 [4096, 768], P('dp', 'section')
- image_grad: float32 [64, 576, 768], P('dp', 'section')
- self_gain_grad: float32 [2, 768], P('section', 'dp')
- self_shift_grad: float32 [2, 768], P('section', 'dp')
- heads_in_grad: float32 [2, 768, 2304], P('section', 'dp')
- heads_out_grad: float32 [2, 768, 768], P('section', 'dp')
- feed_gain_grad: float32 [2, 768], P('section', 'dp')
- feed_shift_grad: float32 [2, 768], P('section', 'dp')
- up_weight_grad: float32 [2, 768, 3072], P('section', 'dp')
- up_bias_grad: float32 [2, 3072], P('section', 'dp')
- down_weight_grad: float32 [2, 3072, 768], P('section', 'dp')
- down_bias_grad: float32 [2, 768], P('section', 'dp')
- cross_gain_grad: float32 [768], P(('section', 'dp'))
- cross_shift_grad: float32 [768], P(('section', 'dp'))
- cross_query_grad: float32 [768, 768], P(('section', 'dp'))
- cross_keys_grad: float32 [768, 1536], P(('section', 'dp'))
- cross_out_grad: float32 [768, 768], P(('section', 'dp'))
Inputs may be any that keep to these rules, and one draw needn't show every extreme that they name: `lengths`: a caption of length n holds its tokens in its first n of 64 slots; the rest is padding.
All inputs are finite; a program needn't handle non-finite values.
Results may differ from a plain program's by a relative error of at most 0.025.
Values may be sent and summed in bfloat16 or wider, within the bound.
No kernel may reach another device: no remote copies, remote signals or barrier semaphores. Data moves between devices by JAX's collectives and lax.ppermute only.
A program may use at most 320 MiB of HBM per device.

v0:
```python
import functools

import jax
import jax.numpy as jnp
from jax import lax
from jax.experimental import pallas as pl
from jax.experimental.pallas import tpu as pltpu
from jax.sharding import PartitionSpec as P

HEAD_DIM = 64
PAIR = 2 * HEAD_DIM
QUAD = 4 * HEAD_DIM
EPS = 1e-05
MASKED = -1000000000.0
SCALE = HEAD_DIM**-0.5
F32 = jnp.float32
BF16 = jnp.bfloat16
MIB = 1 << 20


def swap(value):
    return lax.ppermute(value, "section", [(0, 1), (1, 0)])


def pick(section, first, later):
    return jnp.where(section == 0, first, later)


def side(own, other, section, axis):
    return jnp.concatenate([pick(section, own, other), pick(section, other, own)], axis)


def low(values):
    return values.astype(BF16)


def ring_chip(place, chips):
    return jnp.where(place < chips // 2, 2 * place, 2 * (chips - 1 - place) + 1)


def ring_order():
    chips = lax.axis_size("dp") // 2
    return list(range(0, chips, 2)) + list(range(chips - 1, 0, -2))


def ring_steps(shift):
    order = ring_order()
    chips = len(order)
    return [(2 * order[i] + core, 2 * order[(i + shift) % chips] + core) for i in range(chips) for core in range(2)]


def ring_move(value, shift):
    return lax.ppermute(value, "dp", ring_steps(shift))


def core_swap(value):
    return lax.ppermute(value, "dp", [(i, i ^ 1) for i in range(lax.axis_size("dp"))])


def my_place():
    chips = lax.axis_size("dp") // 2
    me = lax.axis_index("dp")
    chip, core = me // 2, me % 2
    return jnp.where(chip % 2 == 0, chip // 2, chips - 1 - chip // 2), core


def pack_kernel(cut, spots, *refs):
    *sources, out = refs
    chips = out.shape[0]
    for i, source in enumerate(sources[: chips - 1]):
        out[spots[i]] = source[...]
    out[spots[chips - 1], :, :cut] = sources[chips - 1][...]
    out[spots[chips - 1], :, cut:] = sources[chips][...]


def join_kernel(place, mine, other, out):
    core = place[1]
    for chip in range(mine.shape[0]):
        out[2 * chip + core] = mine[chip]
        out[2 * chip + 1 - core] = other[chip]


def reorder_kernel(order, parts, place, source, *outs):
    rows = source.shape[0] // len(order)
    width = sum(out.shape[1] for out in outs)
    for part in range(parts):
        offset = part * width
        for out in outs:
            for i, spot in enumerate(order):
                begin = part * source.shape[0] + spot * rows
                out[begin : begin + rows, :] = source[i * rows : (i + 1) * rows, offset : offset + out.shape[1]]
            offset += out.shape[1]


class Gather:
    def __init__(self, shard):
        self.chips = lax.axis_size("dp") // 2
        self.steps = self.chips // 2
        self.rows, self.width = shard.shape
        self.cut = self.width // 256 * 128
        self.got = {0: shard}
        self.step = 0
        self.last = ()

    def front(self):
        return self.last or (self.got[-self.step], self.got[self.step])

    def put_front(self, values):
        if self.last:
            self.last = values
        else:
            self.got[-self.step], self.got[self.step] = values

    def move(self):
        self.step += 1
        up, down = self.got[1 - self.step], self.got[self.step - 1]
        if self.step < self.steps:
            self.got[-self.step], self.got[self.step] = ring_move(up, 1), ring_move(down, -1)
        else:
            self.last = (ring_move(up[:, : self.cut], 1), ring_move(down[:, self.cut :], -1))

    def pack(self):
        chips, half = self.chips, self.steps
        steps = list(range(1 - half, half + 1))
        place, _ = my_place()
        spots = jnp.stack([ring_chip((place + step + chips) % chips, chips) for step in steps]).astype(jnp.int32)
        (self.mine,) = call(
            functools.partial(pack_kernel, self.cut), spots, [self.got[step] for step in steps[:-1]] + list(self.last), [((chips, self.rows, self.width), BF16)], name="pack"
        )
        self.other = core_swap(self.mine)

    def result(self, place):
        rows = 2 * self.chips * self.rows
        if self.rows % 16 == 0:
            (full,) = call(join_kernel, place, [self.mine, self.other], [((2 * self.chips, self.rows, self.width), BF16)], name="join")
            return full.reshape(rows, self.width)
        first, later = pick(place[1], self.mine, self.other), pick(place[1], self.other, self.mine)
        return jnp.stack([first, later], 1).reshape(rows, self.width)


def together(*values):
    return lax.optimization_barrier(values)


def meet(rings, *values):
    fronts = [ring.front() for ring in rings]
    flat = together(*[v for front in fronts for v in front], *values)
    for i, ring in enumerate(rings):
        ring.put_front((flat[2 * i], flat[2 * i + 1]))
    return flat[2 * len(rings) :]


class Scatter:
    def __init__(self, mine, sent):
        self.mine, self.sent = mine, sent
        self.chips, self.rows, self.width = mine.shape
        self.steps = self.left = self.chips // 2
        self.cut = self.width // 256 * 128
        self.place, _ = my_place()

    def begin(self):
        self.got = core_swap(self.sent)

    def own(self, step, begin=0, end=None):
        chip = ring_chip((self.place + step + self.chips) % self.chips, self.chips)
        cut_out = lambda v: lax.dynamic_index_in_dim(v, chip, 0, False)[:, begin:end].astype(F32)
        return cut_out(self.mine) + cut_out(self.got)

    def front(self):
        return self.up, self.down

    def put_front(self, values):
        self.up, self.down = values

    def step(self, *pins):
        left, cut = self.left, self.cut
        if left == self.steps:
            up, down = self.own(left, 0, cut), self.own(-left, cut)
        else:
            up, down = self.added()
            up, down = self.own(left) + up, self.own(-left) + down
        up, down, *pins = together(low(up), low(down), *pins)
        self.up, self.down = ring_move(up, 1), ring_move(down, -1)
        self.left -= 1
        return pins

    def added(self):
        up, down = self.up.astype(F32), self.down.astype(F32)
        if self.left == self.steps - 1:
            up = jnp.concatenate([up, jnp.zeros((self.rows, self.width - self.cut), F32)], 1)
            down = jnp.concatenate([jnp.zeros((self.rows, self.cut), F32), down], 1)
        return up, down

    def after_here(self, *values):
        self.mine, self.got, *_ = together(self.mine, self.got, *values)

    def result(self):
        up, down = self.added()
        return self.own(0) + up + down


def norm_unit(values):
    centred = values - jnp.mean(values, -1, keepdims=True)
    scale = lax.rsqrt(jnp.mean(centred * centred, -1, keepdims=True) + EPS)
    return centred * scale, scale


def norm_back(values, gain, grad):
    unit, scale = norm_unit(values)
    wide = grad * gain
    inner = wide - jnp.mean(wide, -1, keepdims=True) - unit * jnp.mean(wide * unit, -1, keepdims=True)
    return inner * scale, jnp.sum(grad * unit, 0, keepdims=True), jnp.sum(grad, 0, keepdims=True)


def dot(left, right):
    return jnp.dot(left, right, preferred_element_type=F32)


def dot_tn(left, right):
    return lax.dot_general(left, right, (((0,), (0,)), ((), ())), preferred_element_type=F32)


def dot_nt(left, right):
    return lax.dot_general(left, right, (((1,), (1,)), ((), ())), preferred_element_type=F32)


def heads_of(shape):
    return lax.broadcasted_iota(jnp.int32, shape, 1) // HEAD_DIM


def stacked(block):
    head = heads_of(block.shape)
    zero = jnp.zeros_like(block)
    return jnp.concatenate([jnp.where(head == h, block, zero) for h in range(block.shape[1] // HEAD_DIM)], 0)


def unstacked(rows):
    heads = rows.shape[1] // HEAD_DIM
    slots = rows.shape[0] // heads
    head = heads_of((slots, rows.shape[1]))
    out = rows[:slots]
    for h in range(1, heads):
        out = jnp.where(head == h, rows[h * slots : (h + 1) * slots], out)
    return out


def row_sums(values):
    high = low(values)
    rest = low(values - high.astype(F32))
    ones = jnp.ones((8, values.shape[1]), BF16)
    return (dot_nt(ones, high) + dot_nt(ones, rest))[0:1]


def keep_mask(length, slots):
    query = lax.broadcasted_iota(jnp.int32, (2 * slots, slots), 0) % slots
    key = lax.broadcasted_iota(jnp.int32, (2 * slots, slots), 1)
    return (key <= query) & (key < length)


def self_chances(queries, keys, keep):
    scores = jnp.where(keep, dot_nt(queries, keys) * SCALE, MASKED)
    raised = jnp.exp(scores - jnp.max(scores, -1, keepdims=True))
    return raised / jnp.sum(raised, -1, keepdims=True)


def keep_mask_turned(length, slots):
    key = lax.broadcasted_iota(jnp.int32, (slots, 2 * slots), 0)
    query = lax.broadcasted_iota(jnp.int32, (slots, 2 * slots), 1) % slots
    return (key <= query) & (key < length)


def self_chances_turned(queries, keys, keep):
    scores = jnp.where(keep, dot_nt(keys, queries) * SCALE, MASKED)
    raised = jnp.exp(scores - jnp.max(scores, 0, keepdims=True))
    return raised / jnp.sum(raised, 0, keepdims=True)


class Late:
    def __init__(self, source, scratch, sems, blocks):
        self.scratch, self.shape = scratch, scratch.shape
        self.copies = {}
        for i, (begin, end) in enumerate(blocks or [(0, None)]):
            here = (slice(None), slice(begin, end)) if blocks else Ellipsis
            copy = pltpu.make_async_copy(source.at[here] if blocks else source, scratch.at[here] if blocks else scratch, sems.at[i])
            copy.start()
            self.copies[(begin, end)] = copy

    def __getitem__(self, index):
        wanted = index[-1] if isinstance(index, tuple) and len(self.shape) == 2 else slice(None)
        low_end, high_end = wanted.start or 0, wanted.stop or self.shape[-1]
        for block in list(self.copies):
            if block[0] < high_end and (block[1] is None or block[1] > low_end):
                self.copies.pop(block).wait()
        return self.scratch[index]


class Save:
    def __init__(self, buffer, target, sems):
        self.buffer, self.target, self.sems, self.shape = buffer, target, sems, buffer.shape
        self.copies, self.whole = [], False

    def __getitem__(self, index):
        return self.buffer[index]

    def __setitem__(self, index, value):
        self.buffer[index] = value

    def flush(self, cols=None):
        if self.whole:
            return
        self.whole = cols is None
        here = (slice(None),) * (len(self.shape) - 1) + (cols,)
        copy = pltpu.make_async_copy(self.buffer if cols is None else self.buffer.at[here], self.target if cols is None else self.target.at[here], self.sems.at[len(self.copies)])
        copy.start()
        self.copies.append(copy)


def flush(ref, cols=None):
    if isinstance(ref, Save):
        ref.flush(cols)


def late(array, *blocks):
    return (array, blocks)


def save(shape, dtype):
    return (shape, dtype, "save")


def both(shape, dtype):
    return (shape, dtype, "both")


FLUSHES = 10


def run_kernel(kernel, in_kinds, out_kinds, kept, n_over, n_fetch, n_results, *refs):
    n_ins = 1 + len(in_kinds) + n_over + n_fetch
    ins, results, scratch = refs[1:n_ins], list(refs[n_ins : n_ins + n_results]), list(refs[n_ins + n_results :])
    given = []
    for ref, blocks in zip(ins, in_kinds):
        given.append(ref if blocks is None else Late(ref, scratch.pop(0), scratch.pop(0), blocks))
    saves, outs = [], []
    for i in kept:
        saves.append(Save(ins[i], results.pop(), scratch.pop(0)))
        saves[-1].flush()
    fetches = []
    for i in range(n_fetch):
        copy = pltpu.make_async_copy(refs[n_ins - n_fetch + i], results[len(results) - n_fetch + i], scratch.pop(0).at[0])
        copy.start()
        fetches.append(copy)
    results = results[: len(results) - n_fetch]
    for kind in out_kinds:
        if kind == "near":
            outs.append(results.pop(0))
            continue
        buffer = scratch.pop(0) if kind == "save" else results.pop(0)
        saves.append(Save(buffer, results.pop(0), scratch.pop(0)))
        outs.append(saves[-1])
    kernel(refs[0], *given, *outs, *scratch)
    for item in saves:
        if not item.copies:
            item.flush()
    for item in saves:
        for copy in item.copies:
            copy.wait()
    for copy in fetches:
        copy.wait()


def call(kernel, place, ins, outs, scratch=(), vmem=14, name=None, flops=0, keep=(), over=(), fetch=()):
    smem, near, far = pl.BlockSpec(memory_space=pltpu.SMEM), pl.BlockSpec(memory_space=pltpu.VMEM), pl.BlockSpec(memory_space=pl.ANY)
    in_specs, arrays, in_kinds, buffers = [smem], [place], [], []
    for entry in ins:
        if isinstance(entry, tuple):
            array, blocks = entry
            array = pltpu.with_memory_space_constraint(array, pltpu.HBM)
            in_specs.append(far)
            in_kinds.append(tuple(blocks))
            buffers += [pltpu.VMEM(array.shape, array.dtype), pltpu.SemaphoreType.DMA((max(1, len(blocks)),))]
        else:
            array = entry
            in_specs.append(smem if array.dtype == jnp.int32 else near)
            in_kinds.append(None)
        arrays.append(array)
    for array in over:
        in_specs.append(far)
        arrays.append(pltpu.with_memory_space_constraint(array, pltpu.HBM))
    for array in fetch:
        in_specs.append(far)
        arrays.append(pltpu.with_memory_space_constraint(array, pltpu.HBM))
    buffers += [pltpu.SemaphoreType.DMA((1,)) for _ in list(keep) + list(fetch)]
    out_specs, out_shapes, out_kinds = [], [], []
    for entry in outs:
        shape, dtype, kind = entry if len(entry) == 3 else entry + ("near",)
        out_kinds.append(kind)
        if kind != "save":
            out_specs.append(near)
            out_shapes.append(jax.ShapeDtypeStruct(shape, dtype))
        else:
            buffers.append(pltpu.VMEM(shape, dtype))
        if kind != "near":
            out_specs.append(far)
            out_shapes.append(pltpu.HBM(shape, dtype))
            buffers.append(pltpu.SemaphoreType.DMA((FLUSHES,)))
    for array in fetch:
        out_specs.append(near)
        out_shapes.append(jax.ShapeDtypeStruct(array.shape, array.dtype))
    for i in reversed(keep):
        out_specs.append(far)
        out_shapes.append(pltpu.HBM(ins[i].shape, ins[i].dtype))
    moved = sum(a.size * a.dtype.itemsize for a in arrays)
    return pl.pallas_call(
        functools.partial(run_kernel, kernel, tuple(in_kinds), tuple(out_kinds), tuple(keep), len(over), len(fetch), len(out_shapes)),
        in_specs=in_specs,
        out_specs=out_specs,
        out_shape=out_shapes,
        scratch_shapes=buffers + list(scratch),
        input_output_aliases={1 + len(ins) + i: i for i in range(len(over))},
        compiler_params=pltpu.CompilerParams(vmem_limit_bytes=vmem * MIB),
        cost_estimate=pl.CostEstimate(flops=flops, bytes_accessed=moved, transcendentals=0),
        name=name,
    )(*arrays)


def prepare_kernel(count, place, into, out, up, down, vectors, up_bias, cross_gain, cross_shift, sent, own_attn, own_feed, own_vecs):
    rows, width = out.shape
    half = width // 2
    section = place[0]

    def choose(make):
        first, later = make(0), make(1)
        return jnp.where(section == 0, first, later), jnp.where(section == 0, later, first)

    def feed_of(side_index):
        parts = []
        for fold in range(FOLDS):
            for device in range(count):
                begin = ((device * 2 + side_index) * FOLDS + fold) * rows
                parts.append(up[:, begin : begin + rows])
        parts += [down[(side_index * FOLDS + fold) * rows : (side_index * FOLDS + fold + 1) * rows, :] for fold in range(FOLDS)]
        return jnp.concatenate(parts, 1)

    attn, attn_other = choose(lambda i: jnp.concatenate([into[:, (2 * j + i) * half : (2 * j + i + 1) * half] for j in range(3)], 1))
    feed, feed_other = choose(feed_of)
    wide = lambda v: jnp.concatenate([v, jnp.zeros((v.shape[0], 128 - v.shape[1]), F32)], 1)
    lines = [wide(vectors[...].astype(F32))] + [wide(up_bias[:, i * rows : (i + 1) * rows].astype(F32)) for i in range(2 * FOLDS)]
    lines += [wide(cross_gain[...].astype(F32)), wide(cross_shift[...].astype(F32))]
    vecs = low(jnp.concatenate(lines + [jnp.zeros((128 - LAYER_VECS - 2, 128), F32)], 0).T[:rows])
    own_attn[:, :width] = out[...]
    own_attn[:, width:] = attn
    own_feed[...] = feed
    own_vecs[...] = vecs
    cols = width + 3 * half
    sent[:, :width] = out[...]
    sent[:, width:cols] = attn_other
    sent[:, cols : cols + 128] = vecs
    sent[:, cols + 128 :] = feed_other


def merge_kernel(place, got, own_attn, own_feed, own_vecs, attn_first, attn_last, feed_first, feed_last):
    section = place[0]
    cols = own_attn.shape[1]
    first, last = (lambda own, other: jnp.where(section == 0, own, other)), (lambda own, other: jnp.where(section == 0, other, own))
    attn, attn_other = own_attn[...], got[:, :cols]
    attn_first[:, :cols] = first(attn, attn_other)
    attn_last[...] = last(attn, attn_other)
    feed, feed_other = own_feed[...], got[:, cols + 128 :]
    feed_first[...] = first(feed, feed_other)
    feed_last[...] = last(feed, feed_other)
    vecs, vecs_other = own_vecs[...].astype(F32), got[:, cols : cols + 128].astype(F32)
    vecs_0, vecs_1 = first(vecs, vecs_other), last(vecs, vecs_other)
    half = vecs.shape[0] // 2
    cross = jnp.concatenate([vecs_0[:half], vecs_1[:half]], 0)
    lane = lax.broadcasted_iota(jnp.int32, vecs.shape, 1)
    turned = lambda v: pltpu.roll(v, LAYER_VECS, 1)
    attn_first[:, cols:] = low(jnp.where(lane < LAYER_VECS, vecs_0, jnp.where(lane < 2 * LAYER_VECS, turned(vecs_1), turned(cross))))


SELF_GAIN, SELF_SHIFT, FEED_GAIN, FEED_SHIFT, DOWN_BIAS, UP_BIAS = range(6)
FOLDS = 2
LAYER_VECS = 5 + 2 * FOLDS
CROSS_GAIN, CROSS_SHIFT = 2 * LAYER_VECS, 2 * LAYER_VECS + 1
VECS = 24


def woven(first, later, blocks):
    parts = [v.reshape(blocks, v.shape[0] // blocks, v.shape[1]) for v in (first, later)]
    return jnp.concatenate(parts, 1).reshape(2 * first.shape[0], first.shape[1])


def unwoven(value, blocks):
    parts = value.reshape(blocks, value.shape[0] // blocks, value.shape[1])
    half = parts.shape[1] // 2
    return jnp.concatenate([parts[:, :half].reshape(-1, value.shape[1]), parts[:, half:].reshape(-1, value.shape[1])], 0)


def side_in(section, own, other):
    first = jnp.where(section == 0, own, other)
    return jnp.concatenate([first, jnp.where(section == 0, other, own)], 1)


def half_in(section, values):
    half = values.shape[1] // 2
    return jnp.where(section == 0, values[:, :half], values[:, half:])


def vec(ref, row):
    return ref[row : row + 1, :]


def up_bias_of(vecs, layer, section, fold):
    return vecs[pl.ds(LAYER_VECS * layer + UP_BIAS + FOLDS * section + fold, 1), :]


def self_part(values, layer, lengths, vecs, weights, normed_ref, projected, mixed_ref):
    base = LAYER_VECS * layer
    unit, _ = norm_unit(values)
    normed = low(unit * vec(vecs, base + SELF_GAIN) + vec(vecs, base + SELF_SHIFT))
    normed_ref[...] = normed
    flush(normed_ref)
    half = mixed_ref.shape[1]
    width = values.shape[1]
    projected[...] = low(dot(normed, weights[:, width : width + 3 * half]))
    flush(projected)
    captions = lengths.shape[0]
    slots = values.shape[0] // captions
    for c in range(captions):
        keep = keep_mask(lengths[c], slots)
        here = slice(c * slots, (c + 1) * slots)
        for j in range(half // PAIR):
            q, k, v = (projected[here, i * half + j * PAIR : i * half + (j + 1) * PAIR] for i in range(3))
            chances = self_chances(stacked(q), k, keep)
            mixed_ref[here, j * PAIR : (j + 1) * PAIR] = low(unstacked(dot(low(chances), v)))


def self_first_kernel(aligned, place, lengths, text, weights, vecs, normed, projected, mixed):
    columns = weights[:, weights.shape[1] - 128 :].astype(F32)
    if aligned:
        lane = lax.broadcasted_iota(jnp.int32, columns.shape, 1)
        columns = jnp.where(lane < CROSS_GAIN, columns, unwoven(columns, weights.shape[0] // 48))
    vecs[...] = columns.T[: vecs.shape[0]]
    flush(vecs)
    self_part(text[...].astype(F32), 0, lengths, vecs, weights, normed, projected, mixed)


def self_second_kernel(place, lengths, middle, own, other, vecs, weights, hidden, normed, projected, mixed):
    total = middle[...] + (own[...].astype(F32) + other[...].astype(F32)) + vec(vecs, DOWN_BIAS)
    hidden[...] = low(total)
    flush(hidden)
    self_part(hidden[...].astype(F32), 1, lengths, vecs, weights, normed, projected, mixed)


def heads_rows(weights, section):
    width = weights.shape[0]
    return weights[pl.ds(pl.multiple_of(section * (width // 2), width // 2), width // 2), :width]


def add_heads_out(values, mixed, weights):
    return values + dot(mixed[...], weights[:, : values.shape[1]])


def feed_part(middle, layer, section, vecs, feed, normed_ref, slope_ref, active_ref):
    base = LAYER_VECS * layer
    width = middle.shape[1]
    unit, _ = norm_unit(middle)
    normed = low(unit * vec(vecs, base + FEED_GAIN) + vec(vecs, base + FEED_SHIFT))
    normed_ref[...] = normed
    flush(normed_ref)
    total = jnp.zeros_like(middle)
    for i in range(FOLDS):
        here = slice(i * width, (i + 1) * width)
        raised = dot(normed, feed[:, here]) + up_bias_of(vecs, layer, section, i)
        chance = 0.5 * (1.0 + lax.erf(raised * 0.5**0.5))
        slope_ref[:, here] = low(chance + raised * jnp.exp(-0.5 * raised * raised) * 0.3989422804014327)
        active = low(raised * chance)
        active_ref[:, here] = active
        flush(slope_ref, here)
        flush(active_ref, here)
        total += dot(active, feed[:, (FOLDS + i) * width : (FOLDS + i + 1) * width])
    return low(total)


def feed_first_kernel(place, text, own, other, vecs, weights, feed, mixed_all, middle, normed, slope, active, part):
    mixed_all[...] = side_in(place[0], own[...], other[...])
    flush(mixed_all)
    values = add_heads_out(text[...].astype(F32), mixed_all, weights)
    middle[...] = values
    flush(middle)
    part[...] = feed_part(values, 0, place[0], vecs, feed, normed, slope, active)


def by_caption(kernel, array, weights, out, name, flops):
    block = lambda shape: pl.BlockSpec((1,) + shape[1:], lambda i: (i, 0, 0))
    moved = array.size * array.dtype.itemsize + out.size * out.dtype.itemsize
    return pl.pallas_call(
        kernel,
        grid=(array.shape[0],),
        in_specs=[block(array.shape), pl.BlockSpec(weights.shape, lambda i: (0, 0))],
        out_specs=block(out.shape),
        out_shape=pltpu.HBM(out.shape, out.dtype),
        compiler_params=pltpu.CompilerParams(vmem_limit_bytes=24 * MIB),
        cost_estimate=pl.CostEstimate(flops=flops, bytes_accessed=moved, transcendentals=0),
        name=name,
    )(array, weights)


def pairs_kernel(place, image, keys, pairs):
    for c in range(image.shape[0]):
        pairs[c] = low(dot(image[c], keys[...]))


def image_grad_kernel(grad_pairs, keys, grad):
    grad[0] = dot_nt(grad_pairs[0], keys[...])


def cross_kernel(place, hidden, own, other, vecs, weights, query, pairs, mixed_all, first, normed_ref, queries, part, stats):
    mixed_all[...] = side_in(place[0], own[...], other[...])
    flush(mixed_all)
    values = add_heads_out(hidden[...].astype(F32), mixed_all, weights)
    first[...] = values
    flush(first)
    unit, _ = norm_unit(values)
    normed = low(unit * vec(vecs, CROSS_GAIN) + vec(vecs, CROSS_SHIFT))
    normed_ref[...] = normed
    flush(normed_ref)
    rows, width = values.shape
    queries[...] = low(dot(normed, query[...]))
    flush(queries)
    captions = pairs.shape[0]
    slots = rows // captions
    quads = width // QUAD
    for c in range(captions):
        here = slice(c * slots, (c + 1) * slots)
        for j in range(quads):
            cols = slice(j * QUAD, (j + 1) * QUAD)
            k, v = pairs[c, :, cols], pairs[c, :, width + j * QUAD : width + (j + 1) * QUAD]
            scores = dot_nt(k, stacked(queries[here, cols])) * SCALE
            top = jnp.max(scores, 0, keepdims=True)
            raised = jnp.exp(scores - top)
            part[here, cols] = low(unstacked(dot_tn(low(raised), v)))
            row = c * quads + j
            stats[row : row + 1, :] = top
            stats[STATS + row : STATS + row + 1, :] = jnp.sum(raised, 0, keepdims=True)


STATS = 16


def feed_second_kernel(place, first, own, other, own_stats, other_stats, vecs, out, feed, middle, mixed, factor, normed, slope, active, part):
    rows, width = first.shape
    quads = width // QUAD
    top, top_other = own_stats[:STATS], other_stats[:STATS]
    best = jnp.maximum(top, top_other)
    own_weight, other_weight = jnp.exp(top - best), jnp.exp(top_other - best)
    inverse = 1.0 / (own_stats[STATS:] * own_weight + other_stats[STATS:] * other_weight)
    own_factor, other_factor = own_weight * inverse, other_weight * inverse
    factor[...] = own_factor
    flush(factor)
    columns = jnp.concatenate([own_factor, other_factor, jnp.zeros((PAIR - 2 * STATS, QUAD), F32)], 0).T
    slots = QUAD // 4
    head = heads_of((slots, QUAD))
    for c in range(rows // slots):
        here = slice(c * slots, (c + 1) * slots)
        for j in range(quads):
            cols = slice(j * QUAD, (j + 1) * QUAD)

            def spread(column):
                out = columns[:slots, column : column + 1]
                for h in range(1, 4):
                    out = jnp.where(head == h, columns[h * slots : (h + 1) * slots, column : column + 1], out)
                return out

            row = c * quads + j
            mixed[here, cols] = low(spread(row) * own[here, cols].astype(F32) + spread(STATS + row) * other[here, cols].astype(F32))
    flush(mixed)
    values = first[...] + dot(mixed[...], out[...])
    middle[...] = values
    flush(middle)
    part[...] = feed_part(values, 1, place[0], vecs, feed, normed, slope, active)


def feed_back(grad, vecs, feed, slope, bias_grad, down_bias_grad, slope_ref, part):
    width = grad.shape[1]
    grad_low = low(grad)
    down_bias_grad[...] = jnp.sum(grad, 0, keepdims=True)
    total = jnp.zeros(grad.shape, F32)
    for i in range(FOLDS):
        here = slice(i * width, (i + 1) * width)
        down = feed[:, (FOLDS + i) * width : (FOLDS + i + 1) * width]
        grad_raised = low(dot_nt(grad_low, down) * slope[:, here].astype(F32))
        slope_ref[:, here] = grad_raised
        bias_grad[i : i + 1, :] = jnp.sum(grad_raised.astype(F32), 0, keepdims=True)
        total += dot_nt(grad_raised, feed[:, here])
    part[...] = low(total)


def feed_back_last_kernel(place, cot, vecs, feed, slope, bias_grad, down_bias_grad, grad_raised, part):
    feed_back(cot[...].astype(F32), vecs, feed, slope, bias_grad, down_bias_grad, grad_raised, part)


def cross_back_kernel(place, cot, own, other, middle, vecs, out, queries, pairs, stats, factor, mixed, grad_ref, low_ref, vec_grad, query_part, grad_pairs, grad_mixed):
    rows, width = middle.shape
    inner = own[...].astype(F32) + other[...].astype(F32)
    step, gain_grad, shift_grad = norm_back(middle[...], vec(vecs, LAYER_VECS + FEED_GAIN), inner)
    vec_grad[0:1, :] = gain_grad
    vec_grad[1:2, :] = shift_grad
    grad = step + cot[...].astype(F32)
    grad_ref[...] = grad
    low_ref[...] = low(grad)
    grad_mixed[...] = low(dot_nt(low(grad), out[...]))
    captions = pairs.shape[0]
    slots = rows // captions
    quads = width // QUAD
    for c in range(captions):
        here = slice(c * slots, (c + 1) * slots)
        for j in range(quads):
            cols = slice(j * QUAD, (j + 1) * QUAD)
            later = slice(width + j * QUAD, width + (j + 1) * QUAD)
            row = slice(c * quads + j, c * quads + j + 1)
            k, v = pairs[c, :, cols], pairs[c, :, later]
            q = stacked(queries[here, cols])
            grad_block = grad_mixed[here, cols]
            grads = stacked(grad_block)
            delta = row_sums(stacked(grad_block.astype(F32) * mixed[here, cols].astype(F32)))
            chances = jnp.exp(dot_nt(k, q) * SCALE - stats[row, :]) * factor[row, :]
            slope = low(chances * (dot_nt(v, grads) - delta))
            query_part[here, cols] = low(unstacked(dot_tn(slope, k)) * SCALE)
            grad_pairs[c, :, cols] = low(dot(slope, q) * SCALE)
            grad_pairs[c, :, later] = low(dot(low(chances), grads))


def self_back(grad, section, lengths, weights, projected, low_ref, grad_projected, grad_mixed):
    half = grad_mixed.shape[1]
    low_ref[...] = low(grad)
    flush(low_ref)
    grad_mixed[...] = low(dot_nt(low(grad), heads_rows(weights, section)))
    captions = lengths.shape[0]
    slots = grad.shape[0] // captions
    for c in range(captions):
        keep = keep_mask_turned(lengths[c], slots)
        here = slice(c * slots, (c + 1) * slots)
        for j in range(half // PAIR):
            cols = [slice(i * half + j * PAIR, i * half + (j + 1) * PAIR) for i in range(3)]
            q, k, v = (projected[here, cols[i]] for i in range(3))
            q = stacked(q)
            chances = self_chances_turned(q, k, keep)
            grads = stacked(grad_mixed[here, cols[0]])
            grad_chances = dot_nt(v, grads)
            slope = low(chances * (grad_chances - jnp.sum(grad_chances * chances, 0, keepdims=True)))
            grad_projected[here, cols[0]] = low(unstacked(dot_tn(slope, k)) * SCALE)
            grad_projected[here, cols[1]] = low(dot(slope, q) * SCALE)
            grad_projected[here, cols[2]] = low(dot(low(chances), grads))
    width = grad.shape[1]
    return dot_nt(grad_projected[...], weights[:, width : width + 3 * half])


def self_back_second_kernel(place, lengths, grad_middle, own, other, first, vecs, query, weights, projected, grad_ref, low_ref, grad_queries, grad_projected, part, vec_grad, grad_mixed):
    total = low(own[...].astype(F32) + other[...].astype(F32))
    grad_queries[...] = total
    inner = dot_nt(total, query[...])
    step, gain_grad, shift_grad = norm_back(first[...], vec(vecs, CROSS_GAIN), inner)
    vec_grad[0:1, :] = gain_grad
    vec_grad[1:2, :] = shift_grad
    grad = step + grad_middle[...]
    grad_ref[...] = grad
    part[...] = low(self_back(grad, place[0], lengths, weights, projected, low_ref, grad_projected, grad_mixed))


def feed_back_first_kernel(place, grad_first, own, other, hidden, vecs, feed, slope, grad_ref, low_ref, vec_grad, bias_grad, down_bias_grad, grad_raised, part):
    inner = own[...].astype(F32) + other[...].astype(F32)
    step, gain_grad, shift_grad = norm_back(hidden[...].astype(F32), vec(vecs, LAYER_VECS + SELF_GAIN), inner)
    vec_grad[0:1, :] = gain_grad
    vec_grad[1:2, :] = shift_grad
    low_ref[...] = low(step + grad_first[...])
    grad = low_ref[...].astype(F32)
    grad_ref[...] = grad
    feed_back(grad, vecs, feed, slope, bias_grad, down_bias_grad, grad_raised, part)


def self_back_first_kernel(place, lengths, grad_hidden, own, other, middle, text, vecs, weights, projected, grad_ref, low_ref, grad_projected, part, vec_grad, grad_mixed):
    inner = own[...].astype(F32) + other[...].astype(F32)
    step, gain_grad, shift_grad = norm_back(middle[...], vec(vecs, FEED_GAIN), inner)
    vec_grad[0:1, :] = gain_grad
    vec_grad[1:2, :] = shift_grad
    grad = step + grad_hidden[...]
    grad_ref[...] = grad
    total = self_back(grad, place[0], lengths, weights, projected, low_ref, grad_projected, grad_mixed)
    part[...] = low(total)
    unit, _ = norm_unit(text[...].astype(F32))
    vec_grad[2:3, :] = jnp.sum(total * unit, 0, keepdims=True)
    vec_grad[3:4, :] = jnp.sum(total, 0, keepdims=True)


def text_grad_kernel(place, grad_middle, own, other, text, vecs, out):
    inner = own[...].astype(F32) + other[...].astype(F32)
    step, _, _ = norm_back(text[...].astype(F32), vec(vecs, SELF_GAIN), inner)
    total = step + grad_middle[...]
    half = out.shape[1]
    out[...] = jnp.where(place[0] == 0, total[:, :half], total[:, half:])


BLOCK = 384


def weight_grads(pieces, refs, put):
    offset = 0
    rows = min(refs[left].shape[1] for left, _ in pieces)
    for left, right in pieces:
        for i in range(refs[left].shape[1] // rows):
            for j in range(refs[right].shape[1] // BLOCK):
                put(offset, dot_tn(refs[left][:, i * rows : (i + 1) * rows], refs[right][:, j * BLOCK : (j + 1) * BLOCK]))
                offset += BLOCK
    return offset


def put_in_order(order, out, cols, value):
    rows = value.shape[0] // len(order)
    for i, device in enumerate(order):
        out[i * rows : (i + 1) * rows, cols] = low(value[device * rows : (device + 1) * rows])
    flush(out, cols)


def products_kernel(order, pieces, place, *refs):
    weight_grads(pieces, refs, lambda offset, value: put_in_order(order, refs[-1], slice(offset, offset + value.shape[1]), value))


def put_by_core(core, mine, sent):
    chips, rows, _ = mine.shape

    def put(offset, value):
        cols = slice(offset, offset + value.shape[1])
        for chip in range(chips):
            first = value[2 * chip * rows : (2 * chip + 1) * rows]
            later = value[(2 * chip + 1) * rows : (2 * chip + 2) * rows]
            mine[chip, :, cols] = low(jnp.where(core == 0, first, later))
            sent[chip, :, cols] = low(jnp.where(core == 0, later, first))
        flush(mine, cols)
        flush(sent, cols)

    return put


def ring_products_kernel(pieces, place, *refs):
    weight_grads(pieces, refs, put_by_core(place[1], *refs[-2:]))


def last_products_kernel(
    blocks, place, normed, grad_projected, mixed_0, mixed_1, low_0, low_1, vecs_0, self_vecs_1, feed_vecs_1, cross_vecs, down_0, down_1, bias_0, bias_1, mine, sent
):
    section = place[0]
    put = put_by_core(place[1], mine, sent)
    width = normed.shape[1]
    offset = weight_grads(((0, 1),), (normed, grad_projected), put)
    mixed = jnp.where(section == 0, mixed_0[...], mixed_1[...])
    head_low = jnp.where(section == 0, low_0[...], low_1[...])
    for j in range(width // BLOCK):
        put(offset, dot_tn(mixed, head_low[:, j * BLOCK : (j + 1) * BLOCK]))
        offset += BLOCK
    rows = [
        vecs_0[2:4, :],
        jnp.where(section == 0, 0.0, self_vecs_1[0:2, :]),
        jnp.where(section == 0, vecs_0[0:2, :], feed_vecs_1[0:2, :]),
        jnp.where(section == 0, down_0[...], down_1[...]),
        bias_0[...],
        bias_1[...],
        cross_vecs[0:2, :],
    ]
    used = 7 + 2 * FOLDS
    columns = jnp.concatenate(rows + [jnp.zeros((128 - used - 2, width), F32)], 0).T
    if blocks:
        lane = lax.broadcasted_iota(jnp.int32, columns.shape, 1)
        columns = jnp.where(lane < used, columns, woven(columns[: width // 2], columns[width // 2 :], blocks))
    put(offset, columns)


def keys_products_kernel(blocks, offset, place, image, grad_pairs, mine, sent):
    put = put_by_core(place[1], mine, sent)
    half = image.shape[2] // 2
    for j in range(grad_pairs.shape[2] // BLOCK):
        value = sum(dot_tn(image[c], grad_pairs[c, :, j * BLOCK : (j + 1) * BLOCK]) for c in range(image.shape[0]))
        put(offset + j * BLOCK, woven(value[:half], value[half:], blocks))


def second_products_kernel(blocks, place, normed, grad_queries, mixed, grad_low, self_normed, grad_projected, mine, sent):
    put = put_by_core(place[1], mine, sent)
    offset = weight_grads(((0, 1),), (self_normed, grad_projected), put)
    own_normed, own_mixed = half_in(place[0], normed[...]), half_in(place[0], mixed[...])
    for j in range(grad_queries.shape[1] // BLOCK):
        cols = slice(j * BLOCK, (j + 1) * BLOCK)
        put(offset, woven(dot_tn(own_normed, grad_queries[:, cols]), dot_tn(own_mixed, grad_low[:, cols]), blocks))
        offset += BLOCK


def in_order(section, own, other):
    own, other = own.astype(F32), other.astype(F32)
    return jnp.where(section == 0, own, other), jnp.where(section == 0, other, own)


def finish_feed_kernel(count, place, own, other, up, down):
    rows, width = own.shape[0], down.shape[1]
    halves = in_order(place[0], own[...], other[...])
    parts = []
    for device in range(count):
        for half in halves:
            for fold in range(FOLDS):
                begin = fold * width + device * rows
                parts.append(half[:, begin : begin + rows])
    up[...] = jnp.concatenate(parts, 1)
    for i, half in enumerate(halves):
        for fold in range(FOLDS):
            begin = (i * FOLDS + fold) * rows
            down[begin : begin + rows, :] = half[:, (FOLDS + fold) * width : (FOLDS + fold + 1) * width]


def finish_cross_kernel(place, heads, keys, keys_other, query_grad, keys_grad, out_grad):
    rows = query_grad.shape[0]
    heads32, keys32 = heads[...].astype(F32), keys[...].astype(F32)
    query_grad[...] = heads32[:rows]
    out_grad[...] = heads32[rows:]
    keys_grad[...] = jnp.where(place[0] == 0, keys32[:rows], keys32[rows:]) + keys_other[...].astype(F32)


def finish_heads_kernel(cross_rows, place, sums, own, other, into, out, gain, shift, feed_gain, feed_shift, down_bias, cross_gain, cross_shift, up_bias):
    rows, width = out.shape
    half = width // 2
    section = place[0]
    halves = in_order(section, own[...], other[:, : 3 * half])
    for i in range(3):
        for j, part in enumerate(halves):
            into[:, (2 * i + j) * half : (2 * i + j + 1) * half] = part[:, i * half : (i + 1) * half]
    out[...] = sums[:, 3 * half : 3 * half + width]
    flipped = lambda v: jnp.concatenate([v.astype(F32), jnp.zeros((128 - rows, 128), F32)], 0).T[:, :rows]
    own_vec, other_vec = flipped(sums[:, 3 * half + width :]), flipped(other[:, 3 * half :])
    mine = lambda v, first, later: jnp.where(section == 0, v[first : first + 1], v[later : later + 1])
    gain[...] = mine(own_vec, 0, 2) + mine(other_vec, 0, 2)
    shift[...] = mine(own_vec, 1, 3) + mine(other_vec, 1, 3)
    feed_gain[...] = own_vec[4:5]
    feed_shift[...] = own_vec[5:6]
    down_bias[...] = own_vec[6:7]
    bias = [[mine(v, 7 + i, 7 + FOLDS + i) for i in range(FOLDS)] for v in (own_vec, other_vec)]
    ordered = [jnp.where(section == 0, a, b) for a, b in zip(*bias)] + [jnp.where(section == 0, b, a) for a, b in zip(*bias)]
    up_bias[...] = jnp.concatenate(ordered, 1)
    for i, ref in enumerate((cross_gain, cross_shift)):
        row = own_vec[7 + 2 * FOLDS + i : 8 + 2 * FOLDS + i]
        ref[...] = jnp.where(section == 0, row[:, :cross_rows], row[:, cross_rows:])


def body(
    text,
    image,
    lengths,
    self_gain,
    self_shift,
    heads_in,
    heads_out,
    feed_gain,
    feed_shift,
    up_weight,
    up_bias,
    down_weight,
    down_bias,
    cross_gain,
    cross_shift,
    cross_query,
    cross_keys,
    cross_out,
    cotangent,
):
    section = lax.axis_index("section")
    count = lax.axis_size("dp")
    core = lax.axis_index("dp") % 2
    place = jnp.stack([section, core]).astype(jnp.int32)
    captions, half_image, width = image.shape
    rows = text.shape[0]
    piece = heads_in.shape[1]
    cross_piece = cross_query.shape[0]
    half = width // 2
    half_ff = FOLDS * width
    aligned = piece % 16 == 0
    order = [2 * chip + i for chip in ring_order() for i in range(2)] if aligned else list(range(count))
    groups = [order]

    def both_layers(first, later):
        own, got = pick(section, first, later), swap(pick(section, later, first))
        return pick(section, own, got), pick(section, got, own)

    core_cols = width + 3 * half
    cross_own = jnp.concatenate([cross_keys, cross_query, cross_out], 1)
    if aligned:
        vectors = jnp.concatenate([self_gain, self_shift, feed_gain, feed_shift, down_bias], 0)
        sent, own_attn, own_feed, own_vecs = call(
            functools.partial(prepare_kernel, count),
            place,
            [late(v) for v in (heads_in[0], heads_out[0], up_weight[0], down_weight[0], vectors, up_bias, cross_gain[None], cross_shift[None])],
            [((piece, cols), BF16) for cols in (core_cols + 128 + 2 * half_ff, core_cols, 2 * half_ff, 128)],
            name="prepare",
        )
        attn_rows_0, attn_1, feed_0, feed_1 = call(
            merge_kernel, place, [swap(sent), own_attn, own_feed, own_vecs], [((piece, cols), BF16) for cols in (core_cols + 128, core_cols, 2 * half_ff, 2 * half_ff)], name="merge"
        )
    else:
        up = up_weight[0].reshape(piece, count, 2, FOLDS, piece).transpose(2, 0, 3, 1, 4).reshape(2, piece, half_ff)
        down = down_weight[0].reshape(2, FOLDS, piece, width)
        feed_own = [jnp.concatenate([up[i]] + [down[i, j] for j in range(FOLDS)], 1) for i in range(2)]
        into = heads_in[0].reshape(piece, 3, 2, half)
        attn_own = [jnp.concatenate([heads_out[0], into[:, :, i].reshape(piece, 3 * half)], 1) for i in range(2)]
        own_vecs = jnp.concatenate([self_gain, self_shift, feed_gain, feed_shift, down_bias, up_bias.reshape(2 * FOLDS, piece)], 0)
        own_cross_vecs = jnp.concatenate([cross_gain[None], cross_shift[None]], 0)
        sent_vecs = jnp.concatenate([own_vecs, jnp.pad(own_cross_vecs, ((0, 0), (0, piece - cross_piece)))], 0)
        feed_0, feed_1 = both_layers(*feed_own)
        feed_0, feed_1, sent_vecs, *attn_own = together(feed_0, feed_1, sent_vecs, *attn_own)
        attn_0, attn_1 = both_layers(*attn_own)
        got_vecs = swap(sent_vecs)
        cross_vec_rows = side(own_cross_vecs, got_vecs[LAYER_VECS:, :cross_piece], section, 1)
        vec_cols = jnp.concatenate([pick(section, own_vecs, got_vecs[:LAYER_VECS]), pick(section, got_vecs[:LAYER_VECS], own_vecs), cross_vec_rows], 0)
        vec_cols = jnp.pad(vec_cols, ((0, 128 - vec_cols.shape[0]), (0, 0))).T
        attn_rows_0 = jnp.concatenate([attn_0, vec_cols], 1)
    ring_f = Gather(feed_0)
    ring_f.move()

    def gather(value):
        return lax.all_gather(value, "dp", axis=0, tiled=True, axis_index_groups=groups)

    def reordered(value, blocks, parts, widths):
        rows_out = value.shape[0] * parts
        if aligned:
            return call(functools.partial(reorder_kernel, blocks, parts), place, [value], [((rows_out, w), BF16) for w in widths], name="reorder")
        whole = value.reshape(value.shape[0], parts, sum(widths)).transpose(1, 0, 2).reshape(rows_out, sum(widths))
        ends = [sum(widths[: i + 1]) for i in range(len(widths))]
        return [whole[:, end - w : end] for end, w in zip(ends, widths)]

    attn_first = gather(attn_rows_0)
    attn_1, feed_1, cross_own, text_own, cot_own = meet([ring_f], attn_1, feed_1, cross_own, text, cotangent)
    cross_all = gather(side(cross_own, swap(cross_own), section, 1))
    text_all = side(text, swap(text_own), section, 1)
    feed_last = gather(feed_1)
    cot_all = side(cotangent, swap(cot_own), section, 1)
    ring_d = Gather(attn_1)
    for i in range(ring_f.steps - 2):
        ring_f.move()
        ring_d.move()
        if i < ring_f.steps - 3:
            meet([ring_f, ring_d])
    (attn_first,) = meet([ring_f, ring_d], attn_first)
    ring_f.move()
    ring_d.move()
    (weights_0,) = reordered(attn_first, order, 1, [core_cols + 128])

    shape_f = ((rows, width), F32)
    shape_b = ((rows, width), BF16)
    shape_half = ((rows, half), BF16)
    shape_qkv = ((rows, 3 * half), BF16)
    shape_active = ((rows, half_ff), BF16)
    shape_stats = ((2 * STATS, QUAD), F32)
    shape_factor = ((STATS, QUAD), F32)
    shape_pairs = ((captions, half_image, 2 * width), BF16)
    shape_vec = ((8, width), F32)
    shape_bias = ((FOLDS, width), F32)
    shape_one = ((1, width), F32)
    half_scratch = [pltpu.VMEM((rows, half), BF16)]
    self_flops, feed_flops, pair_flops = 6 * rows * width * half, 4 * rows * width * half_ff, 4 * captions * half_image * width * width
    feed_blocks = [(i * width, (i + 1) * width) for i in (2, 0, 3, 1)]
    attn_blocks = [(0, width), (width, core_cols)]

    vecs, vecs_far, normed_a0, qkv_0, mixed_0, weights_0_far = call(
        functools.partial(self_first_kernel, aligned),
        place,
        [lengths, text_all, weights_0],
        [both((VECS, width), F32), save(*shape_b), save(*shape_qkv), shape_half],
        name="self_0",
        flops=self_flops,
        keep=(2,),
    )
    if not aligned:
        straight = lambda v: jnp.concatenate([v[:CROSS_GAIN], v[CROSS_GAIN : CROSS_GAIN + 2].reshape(2, count, 2, cross_piece).transpose(0, 2, 1, 3).reshape(2, width), v[CROSS_GAIN + 2 :]], 0)
        vecs, vecs_far = straight(vecs), straight(vecs_far)
    other_0 = swap(mixed_0)
    (mixed_0,) = meet([ring_f, ring_d], mixed_0)
    ring_f.pack()
    while ring_d.step < ring_d.steps:
        ring_d.move()
    other_0, ring_f.other = together(other_0, ring_f.other)
    feed_w0 = ring_f.result(place)
    keys, query, cross_out_w = reordered(cross_all, ring_order() if aligned else [0], 2, [2 * width, width, width])
    mixed_all_0, middle_0, normed_f0, slope_f0, active_0, part_0, feed_w0_far = call(
        feed_first_kernel,
        place,
        [text_all, mixed_0, other_0, vecs, weights_0, feed_w0],
        [save(*shape_b), save(*shape_f), save(*shape_b), save(*shape_active), save(*shape_active), shape_b],
        name="feed_0",
        flops=feed_flops,
        keep=(5,),
    )
    part_0_other = swap(part_0)
    (part_0,) = meet([ring_d], part_0)
    ring_d.pack()
    weights_1 = ring_d.result(place)
    hidden, hidden_far, normed_a1, qkv_1, mixed_1 = call(
        self_second_kernel,
        place,
        [lengths, late(middle_0), part_0, part_0_other, vecs, weights_1],
        [both(*shape_b), save(*shape_b), save(*shape_qkv), shape_half],
        name="self_1",
        flops=self_flops,
    )
    other_1 = swap(mixed_1)
    pairs, keys_far = call(pairs_kernel, place, [late(image), keys], [shape_pairs], name="pairs", flops=pair_flops, keep=(1,))
    other_1, pairs = together(other_1, pairs)
    mixed_all_1, first_1, normed_c, queries, cross_part, stats, stats_far, query_far, weights_1_far = call(
        cross_kernel,
        place,
        [hidden, mixed_1, other_1, vecs, weights_1, query, pairs],
        [save(*shape_b), save(*shape_f), save(*shape_b), save(*shape_b), shape_b, both(*shape_stats)],
        name="cross_1",
        flops=4 * rows * width * width,
        keep=(4, 5),
    )
    cross_part_other, stats_other = swap(cross_part), swap(stats)
    (feed_w1,) = reordered(feed_last, order, 1, [2 * half_ff])
    middle_1_far, cross_mixed_far, factor, normed_f1, slope_f1, active_1, part_1, cross_out_far = call(
        feed_second_kernel,
        place,
        [late(first_1), cross_part, cross_part_other, stats, stats_other, vecs, cross_out_w, feed_w1],
        [save(*shape_f), save(*shape_b), save(*shape_factor), shape_b, shape_active, shape_active, shape_b],
        name="feed_1",
        flops=feed_flops,
        keep=(6,),
    )
    own_cols = lambda v: pick(section, v[..., :half], v[..., half:])

    def meet_sums(rings, *values):
        flat = together(*[v for ring in rings for v in ring.front()], *values)
        for i, ring in enumerate(rings):
            ring.put_front(flat[2 * i : 2 * i + 2])
        return flat[2 * len(rings) :]

    def scatter(value):
        return lax.psum_scatter(value, "dp", scatter_dimension=0, tiled=True, axis_index_groups=groups)

    bias_grad_1, down_bias_grad_1, slope_1, back_1 = call(
        feed_back_last_kernel, place, [cot_all, vecs, feed_w1, slope_f1], [save(*shape_bias), save(*shape_one), shape_active, shape_b], name="feed_back_1", flops=feed_flops
    )
    back_1_other = swap(back_1)
    (feed_grad_1,) = call(
        functools.partial(products_kernel, order, ((0, 1), (2, 3))),
        place,
        [normed_f1, slope_1, active_1, cot_all],
        [save((width, 2 * half_ff), BF16)],
        name="feed_grads_1",
        flops=feed_flops,
    )
    back_1_other, feed_grad_1 = together(back_1_other, feed_grad_1)
    feed_got_1 = scatter(feed_grad_1)
    grad_middle_1, grad_low_1, feed_vec_1, query_part, grad_pairs = call(
        cross_back_kernel,
        place,
        [late(cot_all), back_1, back_1_other, late(middle_1_far), late(vecs_far), late(cross_out_far), late(queries), pairs, late(stats_far), late(factor), late(cross_mixed_far)],
        [shape_f, shape_b, save(*shape_vec), shape_b, shape_pairs],
        scratch=[pltpu.VMEM((rows, width), BF16)],
        name="cross_back",
        flops=4 * rows * width * width,
    )
    query_part_other = swap(query_part)
    ring_shape = lambda cols: ((count // 2, piece, cols), BF16)
    second_cols = 3 * half + 3 * width
    if aligned:
        *keys_grads, first_now, query_now, weights_now, qkv_now = call(
            functools.partial(keys_products_kernel, count, 3 * half + width),
            place,
            [late(image), grad_pairs],
            [save(*ring_shape(second_cols)), save(*ring_shape(second_cols))],
            vmem=20,
            name="keys_grads",
            flops=pair_flops,
            fetch=(first_1, query_far, weights_1_far, qkv_1),
        )
        query_part_other, *keys_grads = together(query_part_other, *keys_grads)
    else:
        first_now, query_now, weights_now, qkv_now = first_1, query_far, weights_1_far, qkv_1
    grad_first_1, head_low_1, grad_queries, grad_qkv_1, self_back_1, cross_vec_1 = call(
        self_back_second_kernel,
        place,
        [lengths, grad_middle_1, query_part, query_part_other, first_now, late(vecs_far), query_now, weights_now, qkv_now],
        [shape_f, save(*shape_b), shape_b, shape_qkv, shape_b, save(*shape_vec)],
        scratch=half_scratch,
        name="self_back_1",
        flops=2 * self_flops,
    )
    self_back_1_other = swap(self_back_1)
    if aligned:
        second_grads = call(
            functools.partial(second_products_kernel, count),
            place,
            [late(normed_c), grad_queries, late(cross_mixed_far), grad_low_1, late(normed_a1), grad_qkv_1],
            [save(*ring_shape(second_cols)), save(*ring_shape(second_cols))],
            vmem=20,
            name="second_grads",
            flops=2 * rows * width * (width + 3 * half),
            over=keys_grads,
        )
    else:
        pair_rows = lambda v: v.reshape(2, count, cross_piece, v.shape[1]).transpose(1, 0, 2, 3).reshape(width, v.shape[1])
        flat = lambda v: v.reshape(captions * half_image, v.shape[2])
        heads = pair_rows(jnp.concatenate([dot_tn(own_cols(normed_c), grad_queries), dot_tn(own_cols(cross_mixed_far), grad_low_1)], 0))
        second_grad = low(jnp.concatenate([dot_tn(normed_a1, grad_qkv_1), heads, pair_rows(dot_tn(flat(image), flat(grad_pairs)))], 1))
        parts = second_grad.reshape(count // 2, 2, piece, second_cols)
        second_grads = pick(core, parts[:, 0], parts[:, 1]), pick(core, parts[:, 1], parts[:, 0])
    self_back_1_other, *second_grads = together(self_back_1_other, *second_grads)
    ring_second = Scatter(*second_grads)
    ring_second.begin()
    (self_back_1_other,) = ring_second.step(self_back_1_other)
    grad_hidden, grad_hidden_low, self_vec_1, bias_grad_0, down_bias_grad_0, slope_0, back_0 = call(
        feed_back_first_kernel,
        place,
        [grad_first_1, self_back_1, self_back_1_other, late(hidden_far), late(vecs_far), late(feed_w0_far, *feed_blocks), late(slope_f0)],
        [shape_f, shape_b, save(*shape_vec), save(*shape_bias), save(*shape_one), shape_active, shape_b],
        name="feed_back_0",
        flops=feed_flops,
    )
    back_0_other = swap(back_0)
    (back_0,) = meet_sums([ring_second], back_0)
    (slope_0,) = ring_second.step(slope_0)
    (feed_grad_0,) = call(
        functools.partial(products_kernel, order, ((0, 1), (2, 3))),
        place,
        [late(normed_f0), slope_0, late(active_0), grad_hidden_low],
        [save((width, 2 * half_ff), BF16)],
        name="feed_grads_0",
        flops=feed_flops,
    )
    back_0_other, feed_grad_0, up, down = together(back_0_other, feed_grad_0, *ring_second.front())
    ring_second.put_front((up, down))
    feed_got_0 = scatter(feed_grad_0)
    (back_0_other,) = ring_second.step(back_0_other)
    grad_middle_0, head_low_0, grad_qkv_0, self_back_0, vecs_grad_0 = call(
        self_back_first_kernel,
        place,
        [lengths, grad_hidden, back_0, back_0_other, late(middle_0), text_all, late(vecs_far), late(weights_0_far, *attn_blocks), late(qkv_0)],
        [shape_f, shape_b, shape_qkv, shape_b, shape_vec],
        scratch=half_scratch,
        name="self_back_0",
        flops=2 * self_flops,
    )
    self_back_0_other = swap(self_back_0)
    (grad_qkv_0,) = meet_sums([ring_second], grad_qkv_0)
    (grad_qkv_0,) = ring_second.step(grad_qkv_0)
    cross_vec_woven = cross_vec_1
    if not aligned:
        cross_vec_woven = cross_vec_1.reshape(8, 2, count, cross_piece).transpose(0, 2, 1, 3).reshape(8, width)
    last_grads = call(
        functools.partial(last_products_kernel, count if aligned else 0),
        place,
        [late(normed_a0), grad_qkv_0, late(mixed_all_0), late(mixed_all_1), head_low_0, late(head_low_1), vecs_grad_0]
        + [late(v) for v in (self_vec_1, feed_vec_1, cross_vec_woven, down_bias_grad_0, down_bias_grad_1, bias_grad_0, bias_grad_1)],
        [save(*ring_shape(core_cols + 128)), ring_shape(core_cols + 128)],
        name="last_grads",
        flops=2 * rows * width * core_cols,
    )
    *last_grads, feed_got_1, self_back_0_other = meet_sums([ring_second], *last_grads, feed_got_1, self_back_0_other)
    ring_last = Scatter(*last_grads)
    ring_last.begin()
    (grad_middle_0,) = ring_last.step(grad_middle_0)
    second_got = low(ring_second.result())
    (text_grad,) = call(text_grad_kernel, place, [grad_middle_0, self_back_0, self_back_0_other, text_all, late(vecs_far)], [((rows, half), F32)], name="text_grad")
    text_grad, second_got = meet_sums([ring_last], text_grad, second_got)
    (grad_pairs,) = ring_last.step(grad_pairs)
    image_grad = by_caption(image_grad_kernel, grad_pairs, keys_far, jax.ShapeDtypeStruct((captions, half_image, width), F32), "image_grad", pair_flops)
    (image_grad,) = meet_sums([ring_last], image_grad)
    ring_last.step()

    def other_half(first, later):
        return swap(pick(section, low(later), low(first)))

    (feed_got_0,) = meet_sums([ring_last], feed_got_0)
    feed_other = other_half(feed_got_0, feed_got_1)
    ring_last.step()
    got_part = swap(pick(section, part_1[:, half:], part_1[:, :half]))
    layer_out = own_cols(middle_1_far) + (own_cols(part_1).astype(F32) + got_part.astype(F32)) + own_cols(vecs_far[LAYER_VECS + DOWN_BIAS])
    cross_got = second_got[:, 3 * half : 3 * half + width]
    keys_got = second_got[:, 3 * half + width :]
    keys_other = swap(pick(section, keys_got[cross_piece:], keys_got[:cross_piece]))
    feed_own = pick(section, feed_got_0, feed_got_1)
    into_got_1 = second_got[:, : 3 * half]
    if aligned:
        up_grad, down_grad = call(
            functools.partial(finish_feed_kernel, count),
            place,
            [feed_own, feed_other],
            [((piece, 2 * half_ff), F32), ((2 * FOLDS * piece, width), F32)],
            name="finish_feed",
        )
        cross_query_grad, cross_keys_grad, cross_out_grad = call(
            finish_cross_kernel,
            place,
            [cross_got, keys_got, keys_other],
            [((cross_piece, width), F32), ((cross_piece, 2 * width), F32), ((cross_piece, width), F32)],
            name="finish_cross",
        )
        keys_other, cross_query_grad = together(keys_other, cross_query_grad)
    else:
        feed_parts = [v.astype(F32) for v in (pick(section, feed_own, feed_other), pick(section, feed_other, feed_own))]
        up_parts = [v[:, :half_ff].reshape(piece, FOLDS, count, piece).transpose(0, 2, 1, 3) for v in feed_parts]
        up_grad = jnp.stack(up_parts, 2).reshape(piece, 2 * half_ff)
        down_parts = [v[:, half_ff:].reshape(piece, FOLDS, width).transpose(1, 0, 2) for v in feed_parts]
        down_grad = jnp.stack(down_parts, 0).reshape(2 * FOLDS * piece, width)
        cross_query_grad, cross_out_grad = cross_got[:cross_piece].astype(F32), cross_got[cross_piece:].astype(F32)
        own_keys = pick(section, keys_got[:cross_piece], keys_got[cross_piece:])
        cross_keys_grad = own_keys.astype(F32) + keys_other.astype(F32)
    last_got = ring_last.result()
    vec_got = last_got[:, core_cols:]
    last_other = swap(low(jnp.concatenate([pick(section, into_got_1.astype(F32), last_got[:, : 3 * half]), vec_got], 1)))
    into_own = pick(section, last_got[:, : 3 * half], into_got_1.astype(F32))
    if aligned:
        shape_row = ((1, piece), F32)
        heads_in_grad, heads_out_grad, *rows_out, up_bias_grad = call(
            functools.partial(finish_heads_kernel, cross_piece),
            place,
            [last_got, into_own, last_other],
            [((piece, 6 * half), F32), ((piece, width), F32)] + [shape_row] * 5 + [((1, cross_piece), F32)] * 2 + [((1, 2 * FOLDS * piece), F32)],
            name="finish_heads",
        )
        cross_gain_grad, cross_shift_grad = rows_out[5][0], rows_out[6][0]
    else:
        into_other = last_other[:, : 3 * half].astype(F32)
        into_parts = pick(section, into_own, into_other), pick(section, into_other, into_own)
        heads_in_grad = jnp.stack([v.reshape(piece, 3, half) for v in into_parts], 2).reshape(piece, 6 * half)
        heads_out_grad = last_got[:, 3 * half : core_cols]
        own_vec, other_vec = vec_got.T, last_other[:, 3 * half :].astype(F32).T
        mine = lambda v, begin, size: pick(section, v[begin : begin + size], v[begin + size : begin + 2 * size])
        self_vec = mine(own_vec, 0, 2) + mine(other_vec, 0, 2)
        rows_out = [self_vec[0:1], self_vec[1:2], own_vec[4:5], own_vec[5:6], own_vec[6:7]]
        bias = mine(own_vec, 7, FOLDS), mine(other_vec, 7, FOLDS)
        up_bias_grad = jnp.concatenate([pick(section, *bias), pick(section, *bias[::-1])], 0).reshape(1, 2 * FOLDS * piece)
        cross_vec = pick(section, own_vec[7 + 2 * FOLDS : 9 + 2 * FOLDS, :cross_piece], own_vec[7 + 2 * FOLDS : 9 + 2 * FOLDS, cross_piece:])
        cross_gain_grad, cross_shift_grad = cross_vec[0], cross_vec[1]
    return (
        layer_out,
        text_grad,
        image_grad,
        rows_out[0],
        rows_out[1],
        heads_in_grad[None],
        heads_out_grad[None],
        rows_out[2],
        rows_out[3],
        up_grad[None],
        up_bias_grad,
        down_grad[None],
        rows_out[4],
        cross_gain_grad,
        cross_shift_grad,
        cross_query_grad,
        cross_keys_grad,
        cross_out_grad,
    )


def solution(mesh):
    placed = (
        P("dp", "section"),
        P("dp", "section", None),
        P("dp"),
        P("section", "dp"),
        P("section", "dp"),
        P("section", "dp", None),
        P("section", "dp", None),
        P("section", "dp"),
        P("section", "dp"),
        P("section", "dp", None),
        P("section", "dp"),
        P("section", "dp", None),
        P("section", "dp"),
        P(("section", "dp")),
        P(("section", "dp")),
        P(("section", "dp"), None),
        P(("section", "dp"), None),
        P(("section", "dp"), None),
        P("dp", "section"),
    )
    return jax.shard_map(
        body,
        mesh=mesh,
        in_specs=placed,
        out_specs=(P("dp", "section"), P("dp", "section"), P("dp", "section", None)) + placed[3:18],
        check_vma=False,
    )
```

profile of v0, /device:TPU:0, one launch (start us, length us, event | category | flops | bytes accessed | tf_op | source)
XLA Modules:
  0.0 320.0 jit_solution(18240366975721569544)
XLA Ops:
  8.6 2.3 prepare.1
  11.0 3.0 collective-permute-start
  14.0 11.2 %collective-permute-done.refs_1_ = bf16[48,5120]{1,0:T(8,128)(2,1)S(1)} collective-permute-done((bf16[48,5120]{1,0:T(8,128)(2,1)S(1)}, bf16[48,5120]{1,0:T(8,128)(2,1)S(1)}, u32[]{:S(2)}, u32[]{:S(2)}) %collective-permute-start) | collective-permute-done | bytes 491552 | tf_op jit(solution)/shard_map/ppermute | solution.py:22
  26.7 1.8 collective-permute-start.2
  29.7 5.2 %collective-permute-done.2.refs_5_ = bf16[48,3072]{1,0:T(8,128)(2,1)S(1)} collective-permute-done((bf16[48,3072]{1,0:T(8,128)(2,1)S(1)}, bf16[48,3072]{1,0:T(8,128)(2,1)S(1)}, u32[]{:S(2)}, u32[]{:S(2)}) %collective-permute-start.2) | collective-permute-done | bytes 294944 | tf_op jit(solution)/shard_map/ppermute | solution.py:53
  36.1 1.5 collective-permute-start.23
  37.6 3.7 %collective-permute-done.23 = bf16[24,3072]{1,0:T(8,128)(2,1)S(1)} collective-permute-done((bf16[24,3072]{1,0:T(8,128)(2,1)S(1)}, bf16[24,3072]{1,0:T(8,128)(2,1)S(1)}, u32[]{:S(2)}, u32[]{:S(2)}) %collective-permute-start.23) | collective-permute-done | bytes 147488 | tf_op jit(solution)/shard_map/ppermute | solution.py:22
  43.5 1.5 collective-permute-start.5
  44.9 1.6 collective-permute-start.7
  46.9 16.6 %collective-permute-done.7.refs_5_ = bf16[48,1920]{1,0:T(8,128)(2,1)S(1)} collective-permute-done((bf16[48,1920]{1,0:T(8,128)(2,1)S(1)}, bf16[48,1920]{1,0:T(8,128)(2,1)S(1)}, u32[]{:S(2)}, u32[]{:S(2)}) %collective-permute-start.7) | collective-permute-done | bytes 184352 | tf_op jit(solution)/shard_map/ppermute | solution.py:53
  63.5 1.8 collective-permute-start.8
  66.9 1.9 collective-permute-start.10
  69.0 4.7 %collective-permute-done.10.refs_2_ = bf16[48,1920]{1,0:T(8,128)(2,1)S(1)} collective-permute-done((bf16[48,1920]{1,0:T(8,128)(2,1)S(1)}, bf16[48,1920]{1,0:T(8,128)(2,1)S(1)}, u32[]{:S(2)}, u32[]{:S(2)}) %collective-permute-start.10) | collective-permute-done | bytes 184352 | tf_op jit(solution)/shard_map/ppermute | solution.py:53
  73.7 1.6 collective-permute-done.11.refs_6_
  75.3 1.8 collective-permute-start.14
  78.8 1.7 collective-permute-start.12
  80.5 1.9 copy-done.7
  83.2 2.8 self_0.1
  86.1 7.2 %collective-permute-done.13.refs_9_ = bf16[48,1536]{1,0:T(8,128)(2,1)S(1)} collective-permute-done((bf16[48,1536]{1,0:T(8,128)(2,1)S(1)}, bf16[48,1536]{1,0:T(8,128)(2,1)S(1)}, u32[]{:S(2)}, u32[]{:S(2)}) %collective-permute-start.13) | collective-permute-done | bytes 147488 | tf_op jit(solution)/shard_map/ppermute | solution.py:53
  94.1 1.5 collective-permute-start.16
  97.9 3.5 %collective-permute-done.16.refs_3_ = bf16[256,384]{1,0:T(8,128)(2,1)S(1)} collective-permute-done((bf16[256,384]{1,0:T(8,128)(2,1)S(1)}, bf16[256,384]{1,0:T(8,128)(2,1)S(1)}, u32[]{:S(2)}, u32[]{:S(2)}) %collective-permute-start.16) | collective-permute-done | bytes 196640 | tf_op jit(solution)/shard_map/ppermute | solution.py:22
  102.3 4.2 %feed_0.1 = (bf16[256,768]{1,0:T(8,128)(2,1)}, f32[256,768]{1,0:T(8,128)}, bf16[256,768]{1,0:T(8,128)(2,1)}, bf16[256,1536]{1,0:T(8,128)(2,1)}, bf16[256,1536]{1...) custom-call(s32[2]{0:T(128)S(1)} %pad_add_fusion.refs_0_, ...), custom_call_target="tpu_custom_call" | custom-call | flops 1207959552 | bytes 8724488 | tf_op jit(solution)/shard_map/feed_0/pallas_call | solution.py:414
  107.2 1.5 collective-permute-start.20
  109.3 1.4 all-gather.6.cloned.1.call-done.refs_1_
  110.7 2.3 copy-done.4
  115.7 3.6 %collective-permute-done.20.refs_4_ = bf16[256,768]{1,0:T(8,128)(2,1)} collective-permute-done((bf16[256,768]{1,0:T(8,128)(2,1)S(1)}, bf16[256,768]{1,0:T(8,128)(2,1)}, u32[]{:S(2)}, u32[]{:S(2)}) %collective-permute-start.20) | collective-permute-done | bytes 393248 | tf_op jit(solution)/shard_map/ppermute | solution.py:22
  119.3 4.3 %self_1.1 = (bf16[256,768]{1,0:T(8,128)(2,1)S(1)}, bf16[256,768]{1,0:T(8,128)(2,1)}, bf16[256,768]{1,0:T(8,128)(2,1)}, bf16[256,1152]{1,0:T(8,128)(2,1)}, bf16[256,384]{1,0:T(8,128)(2,1)S(1)}) custom-call(s32[2]{0:T(128)S(1)} %pad_add_fusion.refs_0_, s32[4]{0:T(128)S(1)} %copy-done.17, f32[256,768]{1,0:T(8,128)} %get-tuple-element.231.refs_2_.refs_5_, ...), custom_call_target="tpu_custom_call" | custom-call | flops 452984832 | bytes 4595736 | tf_op jit(solution)/shard_map/self_1/pallas_call | solution.py:414
  123.6 1.5 collective-permute-start.22
  125.2 5.8 %pairs.1 = (bf16[4,288,1536]{2,1,0:T(8,128)(2,1)S(1)}, bf16[768,1536]{1,0:T(8,128)(2,1)}) custom-call(s32[2]{0:T(128)S(1)} %pad_add_fusion.refs_0_, bf16[4,288,768]{2,1,0:T(8,128)(2,1)} %refs_1_.9, bf16[768,1536]{1,0:T(8,128)(2,1)S(1)} %get-tuple-element.241.refs_2_), custom_call_target="tpu_custom_call" | custom-call | flops 2717908992 | bytes 4128776 | tf_op jit(solution)/shard_map/pairs/pallas_call | solution.py:414
  131.1 6.2 %cross_1.1 = (bf16[256,768]{1,0:T(8,128)(2,1)}, f32[256,768]{1,0:T(8,128)}, bf16[256,768]{1,0:T(8,128)(2,1)}, bf16[256,768]{1,0:T(8,128)(2,1)}, bf16[256,768]{1,...) custom-call(s32[2]{0:T(128)S(1)} %pad_add_fusion.refs_0_, ...), custom_call_target="tpu_custom_call" | custom-call | flops 603979776 | bytes 8527880 | tf_op jit(solution)/shard_map/cross_1/pallas_call | solution.py:414
  138.9 1.6 collective-permute-start.25
  141.3 5.4 %all-gather.8.cloned.1.call-done.refs_1_ = bf16[768,3072]{1,0:T(8,128)(2,1)} async-done(((bf16[48,3072]{1,0:T(8,128)(2,1)}), bf16[768,3072]{1,0:T(8,128)(2,1)}) %all-gather.8.cloned.1.call-update) | async-done | bytes 4718608 | tf_op jit(solution)/shard_map/all_gather | solution.py:1024
  146.7 2.3 copy-done.3
  150.4 5.8 %feed_1.1 = (f32[256,768]{1,0:T(8,128)}, bf16[256,768]{1,0:T(8,128)(2,1)}, f32[16,256]{1,0:T(8,128)}, bf16[256,768]{1,0:T(8,128)(2,1)S(1)}, bf16[256,1536]{1,0:T...) custom-call(s32[2]{0:T(128)S(1)} %pad_add_fusion.refs_0_, ...), custom_call_target="tpu_custom_call" | custom-call | flops 1207959552 | bytes 7610376 | tf_op jit(solution)/shard_map/feed_1/pallas_call | solution.py:414
  156.2 3.7 %feed_back_1.1 = (f32[2,768]{1,0:T(2,128)}, f32[1,768]{1,0:T(1,128)}, bf16[256,1536]{1,0:T(8,128)(2,1)S(1)}, bf16[256,768]{1,0:T(8,128)(2,1)}) custom-call(s32[2]{0:T(128)S(1)} %pad_add_fusion.refs_0_, bf16[256,768]{1,0:T(8,128)(2,1)S(1)} %copy-done.2, f32[24,768]{1,0:T(8,128)S(1)} %copy-done.10, bf16[768,3072]{1,0:T(8,128)(2,1)S(1)} %reorder.5.refs_8_.refs_3_, ...), custom_call_target="tpu_custom_call" | custom-call | flops 1207959552 | bytes 5971976 | tf_op jit(solution)/shard_map/feed_back_1/pallas_call | solution.py:414
  159.9 1.5 collective-permute-start.28
  161.4 3.4 %feed_grads_1.1 = bf16[768,3072]{1,0:T(8,128)(2,1)} custom-call(s32[2]{0:T(128)S(1)} %pad_add_fusion.refs_0_, bf16[256,768]{1,0:T(8,128)(2,1)S(1)} %get-tuple-element.257.refs_1_, bf16[256,1536]{1,0:T(8,128)(2,1)S(1)} %get-tuple-element.258.refs_2_, bf16[256,1536]{1,0:T(8,128)(2,1)S(1)} %get-tuple-element.259.refs_3_, bf16[256,768]{1,0:T(8,128)(2,1)S(1)} %copy-done.2), custom_call_target="tpu_custom_call" | custom-call | flops 1207959552 | bytes 2359304 | tf_op jit(solution)/shard_map/feed_grads_1/pallas_call | solution.py:414
  164.8 6.7 %collective-permute-done.28.refs_3_ = bf16[256,768]{1,0:T(8,128)(2,1)} collective-permute-done((bf16[256,768]{1,0:T(8,128)(2,1)}, bf16[256,768]{1,0:T(8,128)(2,1)}, u32[]{:S(2)}, u32[]{:S(2)}) %collective-permute-start.28) | collective-permute-done | bytes 393248 | tf_op jit(solution)/shard_map/ppermute | solution.py:22
  171.6 10.1 %cross_back.1 = (f32[256,768]{1,0:T(8,128)S(1)}, bf16[256,768]{1,0:T(8,128)(2,1)S(1)}, f32[8,768]{1,0:T(8,128)}, bf16[256,768]{1,0:T(8,128)(2,1)S(1)}, bf16[4,288,1536]{2,1,0:T(8,128)(2,1)S(1)}) custom-call(s32[2]{0:T(128)S(1)} %pad_add_fusion.refs_0_, bf16[256,768]{1,0:T(8,128)(2,1)} %pad_maximum_fusion.1.refs_1_.refs_4_, ...), custom_call_target="tpu_custom_call" | custom-call | flops 603979776 | bytes 7593992 | tf_op jit(solution)/shard_map/cross_back/pallas_call | solution.py:414
  181.7 1.6 collective-permute-start.29
  183.2 9.3 %keys_grads.1 = (bf16[8,48,3456]{2,1,0:T(8,128)(2,1)}, bf16[8,48,3456]{2,1,0:T(8,128)(2,1)}, f32[256,768]{1,0:T(8,128)S(1)}, bf16[768,768]{1,0:T(8,128)(2,1)S(1)...) custom-call(s32[2]{0:T(128)S(1)} %pad_add_fusion.refs_0_, bf16[4,288,768]{2,1,0:T(8,128)(2,1)} %refs_1_.9, ...), custom_call_target="tpu_custom_call" | custom-call | flops 2717908992 | bytes 10813448 | tf_op jit(solution)/shard_map/keys_grads/pallas_call | solution.py:414
  192.5 7.3 %self_back_1.1 = (f32[256,768]{1,0:T(8,128)S(1)}, bf16[256,768]{1,0:T(8,128)(2,1)}, bf16[256,768]{1,0:T(8,128)(2,1)S(1)}, bf16[256,1152]{1,0:T(8,128)(2,1)S(1)},...) custom-call(s32[2]{0:T(128)S(1)} %pad_add_fusion.refs_0_, s32[4]{0:T(128)S(1)} %copy-done.17, ...), custom_call_target="tpu_custom_call" | custom-call | flops 905969664 | bytes 7151640 | tf_op jit(solution)/shard_map/self_back_1/pallas_call | solution.py:414
  201.0 4.3 %second_grads.1 = (bf16[8,48,3456]{2,1,0:T(8,128)(2,1)}, bf16[8,48,3456]{2,1,0:T(8,128)(2,1)}) custom-call(s32[2]{0:T(128)S(1)} %pad_add_fusion.refs_0_, bf16[256,768]{1,0:T(8,128)(2,1)} %get-tuple-element.280.refs_1_, bf16[256,768]{1,0:T(8,128)(2,1)S(1)} %get-tuple-element.281.refs_2_, ...), custom_call_target="tpu_custom_call", output_to_operand_aliasing={{0}: (7, {}), {1}: (8, {})} | custom-call | flops 754974720 | bytes 7864328 | tf_op jit(solution)/shard_map/second_grads/pallas_call | solution.py:414
  205.3 4.7 %collective-permute-done.30.refs_3_ = bf16[256,768]{1,0:T(8,128)(2,1)S(1)} collective-permute-done((bf16[256,768]{1,0:T(8,128)(2,1)S(1)}, bf16[256,768]{1,0:T(8,128)(2,1)S(1)}, u32[]{:S(2)}, u32[]{:S(2)}) %collective-permute-start.30) | collective-permute-done | bytes 393248 | tf_op jit(solution)/shard_map/ppermute | solution.py:22
  211.2 4.3 %collective-permute-done.31 = bf16[8,48,3456]{2,1,0:T(8,128)(2,1)} collective-permute-done((bf16[8,48,3456]{2,1,0:T(8,128)(2,1)}, bf16[8,48,3456]{2,1,0:T(8,128)(2,1)}, u32[]{:S(2)}, u32[]{:S(2)}) %collective-permute-start.31) | collective-permute-done | bytes 2654240 | tf_op jit(solution)/shard_map/ppermute | solution.py:57
  218.8 6.2 %feed_back_0.1 = (f32[256,768]{1,0:T(8,128)S(1)}, bf16[256,768]{1,0:T(8,128)(2,1)S(1)}, f32[8,768]{1,0:T(8,128)}, f32[2,768]{1,0:T(2,128)}, f32[1,768]{1,0:T(1,1...) custom-call(s32[2]{0:T(128)S(1)} %pad_add_fusion.refs_0_, f32[256,768]{1,0:T(8,128)S(1)} %get-tuple-element.291.refs_1_, ...), custom_call_target="tpu_custom_call" | custom-call | flops 1207959552 | bytes 7544840 | tf_op jit(solution)/shard_map/feed_back_0/pallas_call | solution.py:414
  226.4 1.5 fusion.4
  230.0 4.6 %feed_grads_0.1 = bf16[768,3072]{1,0:T(8,128)(2,1)} custom-call(s32[2]{0:T(128)S(1)} %pad_add_fusion.refs_0_, bf16[256,768]{1,0:T(8,128)(2,1)} %get-tuple-element.298.refs_1_, bf16[256,1536]{1,0:T(8,128)(2,1)S(1)} %get-tuple-element.304.refs_2_, bf16[256,1536]{1,0:T(8,128)(2,1)} %get-tuple-element.305.refs_3_, bf16[256,768]{1,0:T(8,128)(2,1)S(1)} %get-tuple-element.306.refs_4_), custom_call_target="tpu_custom_call" | custom-call | flops 1207959552 | bytes 2359304 | tf_op jit(solution)/shard_map/feed_grads_0/pallas_call | solution.py:414
  237.8 2.2 fusion.3
  242.3 7.4 %self_back_0.1 = (f32[256,768]{1,0:T(8,128)S(1)}, bf16[256,768]{1,0:T(8,128)(2,1)S(1)}, bf16[256,1152]{1,0:T(8,128)(2,1)S(1)}, bf16[256,768]{1,0:T(8,128)(2,1)S(1)}, f32[8,768]{1,0:T(8,128)S(1)}) custom-call(s32[2]{0:T(128)S(1)} %pad_add_fusion.refs_0_, s32[4]{0:T(128)S(1)} %copy-done.17, f32[256,768]{1,0:T(8,128)S(1)} %get-tuple-element.314.refs_2_, ...), custom_call_target="tpu_custom_call" | custom-call | flops 905969664 | bytes 6561816 | tf_op jit(solution)/shard_map/self_back_0/pallas_call | solution.py:414
  252.1 1.8 fusion.2
  253.9 1.5 collective-permute-start.39
  255.9 4.1 %last_grads.1 = (bf16[8,48,2048]{2,1,0:T(8,128)(2,1)}, bf16[8,48,2048]{2,1,0:T(8,128)(2,1)S(1)}) custom-call(s32[2]{0:T(128)S(1)} %pad_add_fusion.refs_0_, bf16[256,768]{1,0:T(8,128)(2,1)} %get-tuple-element.325.refs_1_, bf16[256,1152]{1,0:T(8,128)(2,1)S(1)} %get-tuple-element.326.refs_2_, bf16[256,768]{1,0:T(8,128)(2,1)} %get-tuple-element.327.refs_3_, ...), custom_call_target="tpu_custom_call" | custom-call | flops 754974720 | bytes 2672648 | tf_op jit(solution)/shard_map/last_grads/pallas_call | solution.py:414
  261.2 4.3 %collective-permute-done.39 = bf16[48,3456]{1,0:T(8,128)(2,1)S(1)} collective-permute-done((bf16[48,3456]{1,0:T(8,128)(2,1)S(1)}, bf16[48,3456]{1,0:T(8,128)(2,1)S(1)}, u32[]{:S(2)}, u32[]{:S(2)}) %collective-permute-start.39) | collective-permute-done | bytes 331808 | tf_op jit(solution)/shard_map/ppermute | solution.py:53
  273.3 1.5 fusion.1
  274.8 2.7 text_grad.1
  280.7 1.5 collective-permute-start.46
  282.3 4.5 %image_grad.1 = f32[4,288,768]{2,1,0:T(8,128)} custom-call(bf16[4,288,1536]{2,1,0:T(8,128)(2,1)S(1)} %copy-done.6, bf16[768,1536]{1,0:T(8,128)(2,1)S(1)} %copy-done.19), custom_call_target="tpu_custom_call" | custom-call | flops 2717908992 | bytes 7077888 | tf_op jit(solution)/shard_map/image_grad/pallas_call | solution.py:597
  286.8 2.2 collective-permute-done.45
  291.0 1.5 collective-permute-start.48
  294.6 2.2 collective-permute-done.47
  306.9 2.0 collective-permute-start.51
  309.9 1.9 finish_feed.1
  311.8 1.4 finish_heads.1
  (181 shorter events, 68.7 us)
Async XLA Ops:
  7.2 58.4 %copy-start.24 = (bf16[256,384]{1,0:T(8,128)(2,1)S(1)}, bf16[256,384]{1,0:T(8,128)(2,1)}, u32[]{:S(2)}) copy-start(bf16[256,384]{1,0:T(8,128)(2,1)} %param.19) | copy-start | bytes 589828
  7.2 68.1 %all-gather.4.cloned.1.call-start = ((), (), s32[]{:S(2)}) async-start(), calls=%async_computation.2 | async-start | bytes 3342336 | tf_op jit(solution)/shard_map/all_gather | solution.py:1024
  11.0 14.2 %collective-permute-start = (bf16[48,5120]{1,0:T(8,128)(2,1)S(1)}, bf16[48,5120]{1,0:T(8,128)(2,1)S(1)}, u32[]{:S(2)}, u32[]{:S(2)}) collective-permute-start(bf16[48,5120]{1,0:T(8,128)(2,1)S(1)} %get-tuple-element.203), channel_id=1, source_target_pairs={{0,16},{16,0},{1,17},{17,1},{2,18},{18,2},{3,19},{19,3},{4,20},{20... | collective-permute-start | bytes 1474568 | tf_op jit(solution)/shard_map/ppermute | solution.py:22
  26.7 84.1 %all-gather.6.cloned.1.call-start = ((), (), s32[]{:S(2)}) async-start(), calls=%async_computation.3 | async-start | bytes 5013504 | tf_op jit(solution)/shard_map/all_gather | solution.py:1024
  26.7 8.2 %collective-permute-start.2 = (bf16[48,3072]{1,0:T(8,128)(2,1)S(1)}, bf16[48,3072]{1,0:T(8,128)(2,1)S(1)}, u32[]{:S(2)}, u32[]{:S(2)}) collective-permute-start(bf16[48,3072]{1,0:T(8,128)(2,1)S(1)} %get-tuple-element.207.refs_4_), channel_id=1, source_target_pairs={{0,2},{1,3},{4,0},{5,1},{8,4},{9,5},{12,8},{13,9},{14,12},{15,13},... | collective-permute-start | bytes 884744 | tf_op jit(solution)/shard_map/ppermute | solution.py:53
  28.5 7.6 %collective-permute-start.1 = (bf16[48,3072]{1,0:T(8,128)(2,1)S(1)}, bf16[48,3072]{1,0:T(8,128)(2,1)S(1)}, u32[]{:S(2)}, u32[]{:S(2)}) collective-permute-start(bf16[48,3072]{1,0:T(8,128)(2,1)S(1)} %get-tuple-element.207.refs_4_), channel_id=1, source_target_pairs={{0,4},{1,5},{4,8},{5,9},{8,12},{9,13},{12,14},{13,15},{14,10},{15,... | collective-permute-start | bytes 884744 | tf_op jit(solution)/shard_map/ppermute | solution.py:53
  36.1 5.1 %collective-permute-start.23 = (bf16[24,3072]{1,0:T(8,128)(2,1)S(1)}, bf16[24,3072]{1,0:T(8,128)(2,1)S(1)}, u32[]{:S(2)}, u32[]{:S(2)}) collective-permute-start(bf16[24,3072]{1,0:T(8,128)(2,1)S(1)} %pad_maximum_fusion.3), channel_id=1, source_target_pairs={{0,16},{16,0},{1,17},{17,1},{2,18},{18,2},{3,19},{19,3},{4,20},{20... | collective-permute-start | bytes 442376 | tf_op jit(solution)/shard_map/ppermute | solution.py:22
  42.1 104.6 %all-gather.8.cloned.1.call-start = ((), (), s32[]{:S(2)}) async-start(), calls=%async_computation.4 | async-start | bytes 5013504 | tf_op jit(solution)/shard_map/all_gather | solution.py:1024
  42.8 223.4 %reduce-scatter.3.cloned.1.call-start = ((), (), s32[]{:S(2)}) async-start(), calls=%async_computation.5 | async-start | bytes 5013504 | tf_op jit(solution)/shard_map/reduce_scatter | solution.py:1140
  42.8 20.7 %collective-permute-start.4 = (bf16[48,3072]{1,0:T(8,128)(2,1)S(1)}, bf16[48,3072]{1,0:T(8,128)(2,1)S(1)}, u32[]{:S(2)}, u32[]{:S(2)}) collective-permute-start(bf16[48,3072]{1,0:T(8,128)(2,1)S(1)} %collective-permute-done.1.refs_3_), channel_id=1, source_target_pairs={{0,4},{1,5},{4,8},{5,9},{8,12},{9,13},{12,14},{13,15},{14,10},{15,... | collective-permute-start | bytes 884744 | tf_op jit(solution)/shard_map/ppermute | solution.py:53
  43.5 20.0 %collective-permute-start.5 = (bf16[48,3072]{1,0:T(8,128)(2,1)S(1)}, bf16[48,3072]{1,0:T(8,128)(2,1)S(1)}, u32[]{:S(2)}, u32[]{:S(2)}) collective-permute-start(bf16[48,3072]{1,0:T(8,128)(2,1)S(1)} %collective-permute-done.2.refs_5_), channel_id=1, source_target_pairs={{0,2},{1,3},{4,0},{5,1},{8,4},{9,5},{12,8},{13,9},{14,12},{15,13},... | collective-permute-start | bytes 884744 | tf_op jit(solution)/shard_map/ppermute | solution.py:53
  44.9 18.6 %collective-permute-start.7 = (bf16[48,1920]{1,0:T(8,128)(2,1)S(1)}, bf16[48,1920]{1,0:T(8,128)(2,1)S(1)}, u32[]{:S(2)}, u32[]{:S(2)}) collective-permute-start(bf16[48,1920]{1,0:T(8,128)(2,1)S(1)} %get-tuple-element.213.refs_4_), channel_id=1, source_target_pairs={{0,2},{1,3},{4,0},{5,1},{8,4},{9,5},{12,8},{13,9},{14,12},{15,13},... | collective-permute-start | bytes 552968 | tf_op jit(solution)/shard_map/ppermute | solution.py:53
  46.5 17.0 %collective-permute-start.6 = (bf16[48,1920]{1,0:T(8,128)(2,1)S(1)}, bf16[48,1920]{1,0:T(8,128)(2,1)S(1)}, u32[]{:S(2)}, u32[]{:S(2)}) collective-permute-start(bf16[48,1920]{1,0:T(8,128)(2,1)S(1)} %get-tuple-element.213.refs_4_), channel_id=1, source_target_pairs={{0,4},{1,5},{4,8},{5,9},{8,12},{9,13},{12,14},{13,15},{14,10},{15,... | collective-permute-start | bytes 552968 | tf_op jit(solution)/shard_map/ppermute | solution.py:53
  63.5 11.8 %collective-permute-start.8 = (bf16[48,3072]{1,0:T(8,128)(2,1)S(1)}, bf16[48,3072]{1,0:T(8,128)(2,1)S(1)}, u32[]{:S(2)}, u32[]{:S(2)}) collective-permute-start(bf16[48,3072]{1,0:T(8,128)(2,1)S(1)} %collective-permute-done.4.refs_2_), channel_id=1, source_target_pairs={{0,4},{1,5},{4,8},{5,9},{8,12},{9,13},{12,14},{13,15},{14,10},{15,... | collective-permute-start | bytes 884744 | tf_op jit(solution)/shard_map/ppermute | solution.py:53
  65.3 10.0 %collective-permute-start.9 = (bf16[48,3072]{1,0:T(8,128)(2,1)S(1)}, bf16[48,3072]{1,0:T(8,128)(2,1)S(1)}, u32[]{:S(2)}, u32[]{:S(2)}) collective-permute-start(bf16[48,3072]{1,0:T(8,128)(2,1)S(1)} %collective-permute-done.5.refs_6_), channel_id=1, source_target_pairs={{0,2},{1,3},{4,0},{5,1},{8,4},{9,5},{12,8},{13,9},{14,12},{15,13},... | collective-permute-start | bytes 884744 | tf_op jit(solution)/shard_map/ppermute | solution.py:53
  65.6 11.8 %collective-permute-start.3 = (bf16[256,384]{1,0:T(8,128)(2,1)S(1)}, bf16[256,384]{1,0:T(8,128)(2,1)}, u32[]{:S(2)}, u32[]{:S(2)}) collective-permute-start(bf16[256,384]{1,0:T(8,128)(2,1)S(1)} %copy-done.24), channel_id=1, source_target_pairs={{0,16},{16,0},{1,17},{17,1},{2,18},{18,2},{3,19},{19,3},{4,20},{20... | collective-permute-start | bytes 589832 | tf_op jit(solution)/shard_map/ppermute | solution.py:22
  66.9 6.8 %collective-permute-start.10 = (bf16[48,1920]{1,0:T(8,128)(2,1)S(1)}, bf16[48,1920]{1,0:T(8,128)(2,1)S(1)}, u32[]{:S(2)}, u32[]{:S(2)}) collective-permute-start(bf16[48,1920]{1,0:T(8,128)(2,1)S(1)} %collective-permute-done.6.refs_3_), channel_id=1, source_target_pairs={{0,4},{1,5},{4,8},{5,9},{8,12},{9,13},{12,14},{13,15},{14,10},{15,... | collective-permute-start | bytes 552968 | tf_op jit(solution)/shard_map/ppermute | solution.py:53
  68.8 6.5 %collective-permute-start.11 = (bf16[48,1920]{1,0:T(8,128)(2,1)S(1)}, bf16[48,1920]{1,0:T(8,128)(2,1)S(1)}, u32[]{:S(2)}, u32[]{:S(2)}) collective-permute-start(bf16[48,1920]{1,0:T(8,128)(2,1)S(1)} %collective-permute-done.7.refs_5_), channel_id=1, source_target_pairs={{0,2},{1,3},{4,0},{5,1},{8,4},{9,5},{12,8},{13,9},{14,12},{15,13},... | collective-permute-start | bytes 552968 | tf_op jit(solution)/shard_map/ppermute | solution.py:53
  75.3 18.0 %collective-permute-start.14 = (bf16[48,1920]{1,0:T(8,128)(2,1)S(1)}, bf16[48,1920]{1,0:T(8,128)(2,1)S(1)}, u32[]{:S(2)}, u32[]{:S(2)}) collective-permute-start(bf16[48,1920]{1,0:T(8,128)(2,1)S(1)} %collective-permute-done.10.refs_2_), channel_id=1, source_target_pairs={{0,4},{1,5},{4,8},{5,9},{8,12},{9,13},{12,14},{13,15},{14,10},{15,... | collective-permute-start | bytes 552968 | tf_op jit(solution)/shard_map/ppermute | solution.py:53
  77.1 16.2 %collective-permute-start.15 = (bf16[48,1920]{1,0:T(8,128)(2,1)S(1)}, bf16[48,1920]{1,0:T(8,128)(2,1)S(1)}, u32[]{:S(2)}, u32[]{:S(2)}) collective-permute-start(bf16[48,1920]{1,0:T(8,128)(2,1)S(1)} %collective-permute-done.11.refs_6_), channel_id=1, source_target_pairs={{0,2},{1,3},{4,0},{5,1},{8,4},{9,5},{12,8},{13,9},{14,12},{15,13},... | collective-permute-start | bytes 552968 | tf_op jit(solution)/shard_map/ppermute | solution.py:53
  78.4 14.9 %collective-permute-start.13 = (bf16[48,1536]{1,0:T(8,128)(2,1)S(1)}, bf16[48,1536]{1,0:T(8,128)(2,1)S(1)}, u32[]{:S(2)}, u32[]{:S(2)}) collective-permute-start(bf16[48,1536]{1,0:T(8,128)(2,1)S(1)} %slice.87), channel_id=1, source_target_pairs={{0,2},{1,3},{4,0},{5,1},{8,4},{9,5},{12,8},{13,9},{14,12},{15,13},... | collective-permute-start | bytes 442376 | tf_op jit(solution)/shard_map/ppermute | solution.py:53
  78.8 14.5 %collective-permute-start.12 = (bf16[48,1536]{1,0:T(8,128)(2,1)S(1)}, bf16[48,1536]{1,0:T(8,128)(2,1)S(1)}, u32[]{:S(2)}, u32[]{:S(2)}) collective-permute-start(bf16[48,1536]{1,0:T(8,128)(2,1)S(1)} %slice.86), channel_id=1, source_target_pairs={{0,4},{1,5},{4,8},{5,9},{8,12},{9,13},{12,14},{13,15},{14,10},{15,... | collective-permute-start | bytes 442376 | tf_op jit(solution)/shard_map/ppermute | solution.py:53
  82.5 19.8 %copy-start = (bf16[256,768]{1,0:T(8,128)(2,1)}, bf16[256,768]{1,0:T(8,128)(2,1)S(1)}, u32[]{:S(2)}) copy-start(bf16[256,768]{1,0:T(8,128)(2,1)S(1)} %pad_maximum_fusion.refs_2_.refs_1_.refs_6_.refs_4_) | copy-start | bytes 1179652
  86.1 33.2 %copy-start.8 = (f32[24,768]{1,0:T(8,128)}, f32[24,768]{1,0:T(8,128)S(1)}, u32[]{:S(2)}) copy-start(f32[24,768]{1,0:T(8,128)S(1)} %get-tuple-element.229.refs_4_.refs_5_.refs_6_.refs_2_) | copy-start | bytes 221188
  94.0 7.4 %collective-permute-start.17 = (bf16[8,48,3072]{2,1,0:T(8,128)(2,1)S(1)}, bf16[8,48,3072]{2,1,0:T(8,128)(2,1)S(1)}, u32[]{:S(2)}, u32[]{:S(2)}) collective-permute-start(bf16[8,48,3072]{2,1,0:T(8,128)(2,1)S(1)} %pack.2.refs_1_), channel_id=1, source_target_pairs={{0,1},{1,0},{2,3},{3,2},{4,5},{5,4},{6,7},{7,6},{8,9},{9,8},{10,11... | collective-permute-start | bytes 7077896 | tf_op jit(solution)/shard_map/ppermute | solution.py:57
  94.1 7.3 %collective-permute-start.16 = (bf16[256,384]{1,0:T(8,128)(2,1)S(1)}, bf16[256,384]{1,0:T(8,128)(2,1)S(1)}, u32[]{:S(2)}, u32[]{:S(2)}) collective-permute-start(bf16[256,384]{1,0:T(8,128)(2,1)S(1)} %get-tuple-element.225.refs_2_), channel_id=1, source_target_pairs={{0,16},{16,0},{1,17},{17,1},{2,18},{18,2},{3,19},{19,3},{4,20},{20... | collective-permute-start | bytes 589832 | tf_op jit(solution)/shard_map/ppermute | solution.py:22
  95.6 10.8 %collective-permute-start.18 = (bf16[48,896]{1,0:T(8,128)(2,1)S(1)}, bf16[48,896]{1,0:T(8,128)(2,1)S(1)}, u32[]{:S(2)}, u32[]{:S(2)}) collective-permute-start(bf16[48,896]{1,0:T(8,128)(2,1)S(1)} %slice.88), channel_id=1, source_target_pairs={{0,4},{1,5},{4,8},{5,9},{8,12},{9,13},{12,14},{13,15},{14,10},{15,... | collective-permute-start | bytes 258056 | tf_op jit(solution)/shard_map/ppermute | solution.py:53
  96.8 9.6 %collective-permute-start.19 = (bf16[48,1024]{1,0:T(8,128)(2,1)S(1)}, bf16[48,1024]{1,0:T(8,128)(2,1)S(1)}, u32[]{:S(2)}, u32[]{:S(2)}) collective-permute-start(bf16[48,1024]{1,0:T(8,128)(2,1)S(1)} %slice.89), channel_id=1, source_target_pairs={{0,2},{1,3},{4,0},{5,1},{8,4},{9,5},{12,8},{13,9},{14,12},{15,13},... | collective-permute-start | bytes 294920 | tf_op jit(solution)/shard_map/ppermute | solution.py:53
  107.1 7.8 %collective-permute-start.21 = (bf16[8,48,1920]{2,1,0:T(8,128)(2,1)S(1)}, bf16[8,48,1920]{2,1,0:T(8,128)(2,1)S(1)}, u32[]{:S(2)}, u32[]{:S(2)}) collective-permute-start(bf16[8,48,1920]{2,1,0:T(8,128)(2,1)S(1)} %pack.3.refs_1_), channel_id=1, source_target_pairs={{0,1},{1,0},{2,3},{3,2},{4,5},{5,4},{6,7},{7,6},{8,9},{9,8},{10,11... | collective-permute-start | bytes 4423688 | tf_op jit(solution)/shard_map/ppermute | solution.py:57
  107.2 12.1 %collective-permute-start.20 = (bf16[256,768]{1,0:T(8,128)(2,1)S(1)}, bf16[256,768]{1,0:T(8,128)(2,1)}, u32[]{:S(2)}, u32[]{:S(2)}) collective-permute-start(bf16[256,768]{1,0:T(8,128)(2,1)S(1)} %get-tuple-element.235.refs_3_), channel_id=1, source_target_pairs={{0,16},{16,0},{1,17},{17,1},{2,18},{18,2},{3,19},{19,3},{4,20},{20... | collective-permute-start | bytes 1179656 | tf_op jit(solution)/shard_map/ppermute | solution.py:22
  108.7 29.1 %collective-permute-start.27 = (bf16[256,384]{1,0:T(8,128)(2,1)}, bf16[256,384]{1,0:T(8,128)(2,1)}, u32[]{:S(2)}, u32[]{:S(2)}) collective-permute-start(bf16[256,384]{1,0:T(8,128)(2,1)} %param.37), channel_id=1, source_target_pairs={{0,16},{16,0},{1,17},{17,1},{2,18},{18,2},{3,19},{19,3},{4,20},{20... | collective-permute-start | bytes 589832 | tf_op jit(solution)/shard_map/ppermute | solution.py:22
  123.6 7.4 %collective-permute-start.22 = (bf16[256,384]{1,0:T(8,128)(2,1)S(1)}, bf16[256,384]{1,0:T(8,128)(2,1)S(1)}, u32[]{:S(2)}, u32[]{:S(2)}) collective-permute-start(bf16[256,384]{1,0:T(8,128)(2,1)S(1)} %get-tuple-element.239.refs_2_), channel_id=1, source_target_pairs={{0,16},{16,0},{1,17},{17,1},{2,18},{18,2},{3,19},{19,3},{4,20},{20... | collective-permute-start | bytes 589832 | tf_op jit(solution)/shard_map/ppermute | solution.py:22
  137.2 12.7 %collective-permute-start.24 = (bf16[256,768]{1,0:T(8,128)(2,1)}, bf16[256,768]{1,0:T(8,128)(2,1)}, u32[]{:S(2)}, u32[]{:S(2)}) collective-permute-start(bf16[256,768]{1,0:T(8,128)(2,1)} %get-tuple-element.247.refs_2_), channel_id=1, source_target_pairs={{0,16},{16,0},{1,17},{17,1},{2,18},{18,2},{3,19},{19,3},{4,20},{20... | collective-permute-start | bytes 1179656 | tf_op jit(solution)/shard_map/ppermute | solution.py:22
  138.9 11.0 %collective-permute-start.25 = (f32[32,256]{1,0:T(8,128)}, f32[32,256]{1,0:T(8,128)}, u32[]{:S(2)}, u32[]{:S(2)}) collective-permute-start(f32[32,256]{1,0:T(8,128)} %get-tuple-element.248.refs_4_), channel_id=1, source_target_pairs={{0,16},{16,0},{1,17},{17,1},{2,18},{18,2},{3,19},{19,3},{4,20},{20... | collective-permute-start | bytes 98312 | tf_op jit(solution)/shard_map/ppermute | solution.py:22
  159.9 11.6 %collective-permute-start.28 = (bf16[256,768]{1,0:T(8,128)(2,1)}, bf16[256,768]{1,0:T(8,128)(2,1)}, u32[]{:S(2)}, u32[]{:S(2)}) collective-permute-start(bf16[256,768]{1,0:T(8,128)(2,1)} %get-tuple-element.256.refs_2_), channel_id=1, source_target_pairs={{0,16},{16,0},{1,17},{17,1},{2,18},{18,2},{3,19},{19,3},{4,20},{20... | collective-permute-start | bytes 1179656 | tf_op jit(solution)/shard_map/ppermute | solution.py:22
  171.5 126.0 %reduce-scatter.5.cloned.1.call-start = ((), (), s32[]{:S(2)}) async-start(), calls=%async_computation.6 | async-start | bytes 5013504 | tf_op jit(solution)/shard_map/reduce_scatter | solution.py:1140
  181.7 10.8 %collective-permute-start.29 = (bf16[256,768]{1,0:T(8,128)(2,1)S(1)}, bf16[256,768]{1,0:T(8,128)(2,1)S(1)}, u32[]{:S(2)}, u32[]{:S(2)}) collective-permute-start(bf16[256,768]{1,0:T(8,128)(2,1)S(1)} %get-tuple-element.267.refs_3_), channel_id=1, source_target_pairs={{0,16},{16,0},{1,17},{17,1},{2,18},{18,2},{3,19},{19,3},{4,20},{20... | collective-permute-start | bytes 1179656 | tf_op jit(solution)/shard_map/ppermute | solution.py:22
  199.8 10.3 %collective-permute-start.30 = (bf16[256,768]{1,0:T(8,128)(2,1)S(1)}, bf16[256,768]{1,0:T(8,128)(2,1)S(1)}, u32[]{:S(2)}, u32[]{:S(2)}) collective-permute-start(bf16[256,768]{1,0:T(8,128)(2,1)S(1)} %get-tuple-element.279.refs_2_), channel_id=1, source_target_pairs={{0,16},{16,0},{1,17},{17,1},{2,18},{18,2},{3,19},{19,3},{4,20},{20... | collective-permute-start | bytes 1179656 | tf_op jit(solution)/shard_map/ppermute | solution.py:22
  210.0 5.5 %collective-permute-start.31 = (bf16[8,48,3456]{2,1,0:T(8,128)(2,1)}, bf16[8,48,3456]{2,1,0:T(8,128)(2,1)}, u32[]{:S(2)}, u32[]{:S(2)}) collective-permute-start(bf16[8,48,3456]{2,1,0:T(8,128)(2,1)} %get-tuple-element.290), channel_id=1, source_target_pairs={{0,1},{1,0},{2,3},{3,2},{4,5},{5,4},{6,7},{7,6},{8,9},{9,8},{10,11... | collective-permute-start | bytes 7962632 | tf_op jit(solution)/shard_map/ppermute | solution.py:57
  216.8 9.7 %collective-permute-start.34 = (bf16[48,1792]{1,0:T(8,128)(2,1)S(1)}, bf16[48,1792]{1,0:T(8,128)(2,1)S(1)}, u32[]{:S(2)}, u32[]{:S(2)}) collective-permute-start(bf16[48,1792]{1,0:T(8,128)(2,1)S(1)} %add_convert_fusion), channel_id=1, source_target_pairs={{0,2},{1,3},{4,0},{5,1},{8,4},{9,5},{12,8},{13,9},{14,12},{15,13},... | collective-permute-start | bytes 516104 | tf_op jit(solution)/shard_map/ppermute | solution.py:53
  217.8 8.0 %collective-permute-start.33 = (bf16[48,1664]{1,0:T(8,128)(2,1)S(1)}, bf16[48,1664]{1,0:T(8,128)(2,1)S(1)}, u32[]{:S(2)}, u32[]{:S(2)}) collective-permute-start(bf16[48,1664]{1,0:T(8,128)(2,1)S(1)} %add_convert_fusion.1), channel_id=1, source_target_pairs={{0,4},{1,5},{4,8},{5,9},{8,12},{9,13},{12,14},{13,15},{14,10},{15,... | collective-permute-start | bytes 479240 | tf_op jit(solution)/shard_map/ppermute | solution.py:53
  225.0 10.7 %collective-permute-start.32 = (bf16[256,768]{1,0:T(8,128)(2,1)S(1)}, bf16[256,768]{1,0:T(8,128)(2,1)S(1)}, u32[]{:S(2)}, u32[]{:S(2)}) collective-permute-start(bf16[256,768]{1,0:T(8,128)(2,1)S(1)} %get-tuple-element.315.refs_3_), channel_id=1, source_target_pairs={{0,16},{16,0},{1,17},{17,1},{2,18},{18,2},{3,19},{19,3},{4,20},{20... | collective-permute-start | bytes 1179656 | tf_op jit(solution)/shard_map/ppermute | solution.py:22
  227.9 9.1 %collective-permute-start.35 = (bf16[48,3456]{1,0:T(8,128)(2,1)S(1)}, bf16[48,3456]{1,0:T(8,128)(2,1)S(1)}, u32[]{:S(2)}, u32[]{:S(2)}) collective-permute-start(bf16[48,3456]{1,0:T(8,128)(2,1)S(1)} %get-tuple-element.307), channel_id=1, source_target_pairs={{0,4},{1,5},{4,8},{5,9},{8,12},{9,13},{12,14},{13,15},{14,10},{15,... | collective-permute-start | bytes 995336 | tf_op jit(solution)/shard_map/ppermute | solution.py:53
  229.0 8.8 %collective-permute-start.36 = (bf16[48,3456]{1,0:T(8,128)(2,1)S(1)}, bf16[48,3456]{1,0:T(8,128)(2,1)S(1)}, u32[]{:S(2)}, u32[]{:S(2)}) collective-permute-start(bf16[48,3456]{1,0:T(8,128)(2,1)S(1)} %get-tuple-element.308), channel_id=1, source_target_pairs={{0,2},{1,3},{4,0},{5,1},{8,4},{9,5},{12,8},{13,9},{14,12},{15,13},... | collective-permute-start | bytes 995336 | tf_op jit(solution)/shard_map/ppermute | solution.py:53
  240.0 11.1 %collective-permute-start.37 = (bf16[48,3456]{1,0:T(8,128)(2,1)}, bf16[48,3456]{1,0:T(8,128)(2,1)}, u32[]{:S(2)}, u32[]{:S(2)}) collective-permute-start(bf16[48,3456]{1,0:T(8,128)(2,1)} %get-tuple-element.312), channel_id=1, source_target_pairs={{0,4},{1,5},{4,8},{5,9},{8,12},{9,13},{12,14},{13,15},{14,10},{15,... | collective-permute-start | bytes 995336 | tf_op jit(solution)/shard_map/ppermute | solution.py:53
  241.1 11.0 %collective-permute-start.38 = (bf16[48,3456]{1,0:T(8,128)(2,1)S(1)}, bf16[48,3456]{1,0:T(8,128)(2,1)}, u32[]{:S(2)}, u32[]{:S(2)}) collective-permute-start(bf16[48,3456]{1,0:T(8,128)(2,1)S(1)} %get-tuple-element.313), channel_id=1, source_target_pairs={{0,2},{1,3},{4,0},{5,1},{8,4},{9,5},{12,8},{13,9},{14,12},{15,13},... | collective-permute-start | bytes 995336 | tf_op jit(solution)/shard_map/ppermute | solution.py:53
  249.6 10.4 %collective-permute-start.41 = (bf16[256,768]{1,0:T(8,128)(2,1)S(1)}, bf16[256,768]{1,0:T(8,128)(2,1)S(1)}, u32[]{:S(2)}, u32[]{:S(2)}) collective-permute-start(bf16[256,768]{1,0:T(8,128)(2,1)S(1)} %get-tuple-element.342.refs_2_), channel_id=1, source_target_pairs={{0,16},{16,0},{1,17},{17,1},{2,18},{18,2},{3,19},{19,3},{4,20},{20... | collective-permute-start | bytes 1179656 | tf_op jit(solution)/shard_map/ppermute | solution.py:22
  252.1 14.9 %copy-start.12 = (bf16[256,768]{1,0:T(8,128)(2,1)S(1)}, bf16[256,768]{1,0:T(8,128)(2,1)}, u32[]{:S(2)}) copy-start(bf16[256,768]{1,0:T(8,128)(2,1)} %copy-done.11) | copy-start | bytes 1179652
  253.9 11.6 %collective-permute-start.39 = (bf16[48,3456]{1,0:T(8,128)(2,1)S(1)}, bf16[48,3456]{1,0:T(8,128)(2,1)S(1)}, u32[]{:S(2)}, u32[]{:S(2)}) collective-permute-start(bf16[48,3456]{1,0:T(8,128)(2,1)S(1)} %get-tuple-element.323), channel_id=1, source_target_pairs={{0,4},{1,5},{4,8},{5,9},{8,12},{9,13},{12,14},{13,15},{14,10},{15,... | collective-permute-start | bytes 995336 | tf_op jit(solution)/shard_map/ppermute | solution.py:53
  255.3 10.9 %collective-permute-start.40 = (bf16[48,3456]{1,0:T(8,128)(2,1)S(1)}, bf16[48,3456]{1,0:T(8,128)(2,1)}, u32[]{:S(2)}, u32[]{:S(2)}) collective-permute-start(bf16[48,3456]{1,0:T(8,128)(2,1)S(1)} %get-tuple-element.324), channel_id=1, source_target_pairs={{0,2},{1,3},{4,0},{5,1},{8,4},{9,5},{12,8},{13,9},{14,12},{15,13},... | collective-permute-start | bytes 995336 | tf_op jit(solution)/shard_map/ppermute | solution.py:53
  266.2 3.9 %collective-permute-start.42 = (bf16[8,48,2048]{2,1,0:T(8,128)(2,1)}, bf16[8,48,2048]{2,1,0:T(8,128)(2,1)}, u32[]{:S(2)}, u32[]{:S(2)}) collective-permute-start(bf16[8,48,2048]{2,1,0:T(8,128)(2,1)} %copy-done.18), channel_id=1, source_target_pairs={{0,1},{1,0},{2,3},{3,2},{4,5},{5,4},{6,7},{7,6},{8,9},{9,8},{10,11... | collective-permute-start | bytes 4718600 | tf_op jit(solution)/shard_map/ppermute | solution.py:57
  267.0 25.5 %collective-permute-start.26 = (bf16[256,384]{1,0:T(8,128)(2,1)S(1)}, bf16[256,384]{1,0:T(8,128)(2,1)S(1)}, u32[]{:S(2)}, u32[]{:S(2)}) collective-permute-start(bf16[256,384]{1,0:T(8,128)(2,1)S(1)} %broadcast_select_fusion.3), channel_id=1, source_target_pairs={{0,16},{16,0},{1,17},{17,1},{2,18},{18,2},{3,19},{19,3},{4,20},{20... | collective-permute-start | bytes 589832 | tf_op jit(solution)/shard_map/ppermute | solution.py:22
  271.2 6.2 %collective-permute-start.43 = (bf16[48,1024]{1,0:T(8,128)(2,1)S(1)}, bf16[48,1024]{1,0:T(8,128)(2,1)S(1)}, u32[]{:S(2)}, u32[]{:S(2)}) collective-permute-start(bf16[48,1024]{1,0:T(8,128)(2,1)S(1)} %get-tuple-element.346), channel_id=1, source_target_pairs={{0,4},{1,5},{4,8},{5,9},{8,12},{9,13},{12,14},{13,15},{14,10},{15,... | collective-permute-start | bytes 294920 | tf_op jit(solution)/shard_map/ppermute | solution.py:53
  272.1 5.8 %collective-permute-start.44 = (bf16[48,1024]{1,0:T(8,128)(2,1)S(1)}, bf16[48,1024]{1,0:T(8,128)(2,1)S(1)}, u32[]{:S(2)}, u32[]{:S(2)}) collective-permute-start(bf16[48,1024]{1,0:T(8,128)(2,1)S(1)} %get-tuple-element.347), channel_id=1, source_target_pairs={{0,2},{1,3},{4,0},{5,1},{8,4},{9,5},{12,8},{13,9},{14,12},{15,13},... | collective-permute-start | bytes 294920 | tf_op jit(solution)/shard_map/ppermute | solution.py:53
  277.9 15.5 %collective-permute-start.53 = (bf16[24,1536]{1,0:T(8,128)(2,1)S(1)}, bf16[24,1536]{1,0:T(8,128)(2,1)S(1)}, u32[]{:S(2)}, u32[]{:S(2)}) collective-permute-start(bf16[24,1536]{1,0:T(8,128)(2,1)S(1)} %slice_select_fusion), channel_id=1, source_target_pairs={{0,16},{16,0},{1,17},{17,1},{2,18},{18,2},{3,19},{19,3},{4,20},{20... | collective-permute-start | bytes 221192 | tf_op jit(solution)/shard_map/ppermute | solution.py:22
  280.2 8.8 %collective-permute-start.45 = (bf16[48,2048]{1,0:T(8,128)(2,1)S(1)}, bf16[48,2048]{1,0:T(8,128)(2,1)S(1)}, u32[]{:S(2)}, u32[]{:S(2)}) collective-permute-start(bf16[48,2048]{1,0:T(8,128)(2,1)S(1)} %get-tuple-element.355), channel_id=1, source_target_pairs={{0,4},{1,5},{4,8},{5,9},{8,12},{9,13},{12,14},{13,15},{14,10},{15,... | collective-permute-start | bytes 589832 | tf_op jit(solution)/shard_map/ppermute | solution.py:53
  280.7 8.5 %collective-permute-start.46 = (bf16[48,2048]{1,0:T(8,128)(2,1)S(1)}, bf16[48,2048]{1,0:T(8,128)(2,1)S(1)}, u32[]{:S(2)}, u32[]{:S(2)}) collective-permute-start(bf16[48,2048]{1,0:T(8,128)(2,1)S(1)} %get-tuple-element.356), channel_id=1, source_target_pairs={{0,2},{1,3},{4,0},{5,1},{8,4},{9,5},{12,8},{13,9},{14,12},{15,13},... | collective-permute-start | bytes 589832 | tf_op jit(solution)/shard_map/ppermute | solution.py:53
  286.8 14.2 %copy-start.23 = (bf16[48,3072]{1,0:T(8,128)(2,1)S(1)}, bf16[48,3072]{1,0:T(8,128)(2,1)}, u32[]{:S(2)}) copy-start(bf16[48,3072]{1,0:T(8,128)(2,1)} %reduce-scatter.3.cloned.1.call-done) | copy-start | bytes 884740
  290.4 6.5 %collective-permute-start.47 = (bf16[48,2048]{1,0:T(8,128)(2,1)S(1)}, bf16[48,2048]{1,0:T(8,128)(2,1)S(1)}, u32[]{:S(2)}, u32[]{:S(2)}) collective-permute-start(bf16[48,2048]{1,0:T(8,128)(2,1)S(1)} %get-tuple-element.362), channel_id=1, source_target_pairs={{0,4},{1,5},{4,8},{5,9},{8,12},{9,13},{12,14},{13,15},{14,10},{15,... | collective-permute-start | bytes 589832 | tf_op jit(solution)/shard_map/ppermute | solution.py:53
  291.0 6.5 %collective-permute-start.48 = (bf16[48,2048]{1,0:T(8,128)(2,1)S(1)}, bf16[48,2048]{1,0:T(8,128)(2,1)S(1)}, u32[]{:S(2)}, u32[]{:S(2)}) collective-permute-start(bf16[48,2048]{1,0:T(8,128)(2,1)S(1)} %get-tuple-element.363), channel_id=1, source_target_pairs={{0,2},{1,3},{4,0},{5,1},{8,4},{9,5},{12,8},{13,9},{14,12},{15,13},... | collective-permute-start | bytes 589832 | tf_op jit(solution)/shard_map/ppermute | solution.py:53
  298.9 5.7 %collective-permute-start.49 = (bf16[48,2048]{1,0:T(8,128)(2,1)S(1)}, bf16[48,2048]{1,0:T(8,128)(2,1)S(1)}, u32[]{:S(2)}, u32[]{:S(2)}) collective-permute-start(bf16[48,2048]{1,0:T(8,128)(2,1)S(1)} %get-tuple-element.367), channel_id=1, source_target_pairs={{0,4},{1,5},{4,8},{5,9},{8,12},{9,13},{12,14},{13,15},{14,10},{15,... | collective-permute-start | bytes 589832 | tf_op jit(solution)/shard_map/ppermute | solution.py:53
  300.0 5.7 %collective-permute-start.50 = (bf16[48,2048]{1,0:T(8,128)(2,1)S(1)}, bf16[48,2048]{1,0:T(8,128)(2,1)S(1)}, u32[]{:S(2)}, u32[]{:S(2)}) collective-permute-start(bf16[48,2048]{1,0:T(8,128)(2,1)S(1)} %get-tuple-element.368), channel_id=1, source_target_pairs={{0,2},{1,3},{4,0},{5,1},{8,4},{9,5},{12,8},{13,9},{14,12},{15,13},... | collective-permute-start | bytes 589832 | tf_op jit(solution)/shard_map/ppermute | solution.py:53
  302.0 8.0 %collective-permute-start.52 = (bf16[48,3072]{1,0:T(8,128)(2,1)S(1)}, bf16[48,3072]{1,0:T(8,128)(2,1)S(1)}, u32[]{:S(2)}, u32[]{:S(2)}) collective-permute-start(bf16[48,3072]{1,0:T(8,128)(2,1)S(1)} %get-tuple-element.408), channel_id=1, source_target_pairs={{0,16},{16,0},{1,17},{17,1},{2,18},{18,2},{3,19},{19,3},{4,20},{20... | collective-permute-start | bytes 884744 | tf_op jit(solution)/shard_map/ppermute | solution.py:22
  306.9 5.0 %collective-permute-start.51 = (bf16[48,1280]{1,0:T(8,128)(2,1)S(1)}, bf16[48,1280]{1,0:T(8,128)(2,1)S(1)}, u32[]{:S(2)}, u32[]{:S(2)}) collective-permute-start(bf16[48,1280]{1,0:T(8,128)(2,1)S(1)} %pad_maximum_fusion.4), channel_id=1, source_target_pairs={{0,16},{16,0},{1,17},{17,1},{2,18},{18,2},{3,19},{19,3},{4,20},{20... | collective-permute-start | bytes 368648 | tf_op jit(solution)/shard_map/ppermute | solution.py:22
  (21 other events, 105.5 us)
Sparse Core Ops, SparseCore 0:
  26.8 38.9 all-gather.3
  68.0 42.7 all-gather.5
  112.3 34.3 all-gather.7
  171.6 51.4 reduce-scatter.2
  237.9 57.3 reduce-scatter.4
where the time goes:
time: 325 us; the launch traced here: 320 us
  Pallas kernels  110 us (34%)
  waiting for transfers between devices  101 us (31%)
  starting transfers between devices  59.1 us (18%)
  other arithmetic  19.4 us (6%)
  local copies, waits for them, and re-layouts  15.9 us (5%)
  between operations  14.7 us (5%)
    pallas_call x29, Pallas kernels, call(): pl.pallas_call(functools.partial(run_kernel, kernel, tuple(in_kinds), tup...  106 us
    ppermute x32, waiting for transfers between devices, ring_move(): return lax.ppermute(value, 'dp', ring_steps(shift))  52.7 us
    ppermute x18, waiting for transfers between devices, swap(): return lax.ppermute(value, 'section', [(0, 1), (1, 0)])  35.5 us
    ppermute x32, starting transfers between devices, ring_move(): return lax.ppermute(value, 'dp', ring_steps(shift))  33.5 us
    ppermute x18, starting transfers between devices, swap(): return lax.ppermute(value, 'section', [(0, 1), (1, 0)])  25.2 us
    convert_element_type x10, other arithmetic, low(): return values.astype(BF16)  10.8 us
    unnamed x52, local copies, waits for them, and re-layouts  9.92 us
    all_gather x3, waiting for transfers between devices, gather(): lax.all_gather(value, 'dp', axis=0, tiled=True, axis_index_groups=groups)  6.86 us
  transfers between devices with their start and end apart: 59, of which 31 were waited for; matrix products, arithmetic and copies ran while one was open for 7% of the time, Pallas kernels for 30%

commit v1 on v0

--- a/solution.py
+++ b/solution.py
@@ -158,12 +158,20 @@
         self.cut = self.width // 256 * 128
         self.place, _ = my_place()
 
-    def begin(self):
+    def begin(self, early=None):
+        self.first = None
+        if early is not None:
+            self.first = core_swap(lax.dynamic_index_in_dim(early, self.chip(self.steps), 0, False))
         self.got = core_swap(self.sent)
 
+    def chip(self, step):
+        return ring_chip((self.place + step + self.chips) % self.chips, self.chips)
+
     def own(self, step, begin=0, end=None):
-        chip = ring_chip((self.place + step + self.chips) % self.chips, self.chips)
+        chip = self.chip(step)
         cut_out = lambda v: lax.dynamic_index_in_dim(v, chip, 0, False)[:, begin:end].astype(F32)
+        if self.first is not None and abs(step) == self.steps:
+            return cut_out(self.mine) + self.first[:, begin:end].astype(F32)
         return cut_out(self.mine) + cut_out(self.got)
 
     def front(self):
@@ -700,7 +708,7 @@
     feed_back(cot[...].astype(F32), vecs, feed, slope, bias_grad, down_bias_grad, grad_raised, part)
 
 
-def cross_back_kernel(place, cot, own, other, middle, vecs, out, queries, pairs, stats, factor, mixed, grad_ref, low_ref, vec_grad, query_part, grad_pairs, grad_mixed):
+def cross_back_kernel(place, own, other, middle, vecs, cot, out, queries, pairs, stats, factor, mixed, grad_ref, low_ref, vec_grad, query_part, grad_pairs, grad_mixed):
     rows, width = middle.shape
     inner = own[...].astype(F32) + other[...].astype(F32)
     step, gain_grad, shift_grad = norm_back(middle[...], vec(vecs, LAYER_VECS + FEED_GAIN), inner)
@@ -768,7 +776,7 @@
     part[...] = low(self_back(grad, place[0], lengths, weights, projected, low_ref, grad_projected, grad_mixed))
 
 
-def feed_back_first_kernel(place, grad_first, own, other, hidden, vecs, feed, slope, grad_ref, low_ref, vec_grad, bias_grad, down_bias_grad, grad_raised, part):
+def feed_back_first_kernel(place, grad_first, own, other, hidden, vecs, slope, feed, grad_ref, low_ref, vec_grad, bias_grad, down_bias_grad, grad_raised, part):
     inner = own[...].astype(F32) + other[...].astype(F32)
     step, gain_grad, shift_grad = norm_back(hidden[...].astype(F32), vec(vecs, LAYER_VECS + SELF_GAIN), inner)
     vec_grad[0:1, :] = gain_grad
@@ -779,7 +787,7 @@
     feed_back(grad, vecs, feed, slope, bias_grad, down_bias_grad, grad_raised, part)
 
 
-def self_back_first_kernel(place, lengths, grad_hidden, own, other, middle, text, vecs, weights, projected, grad_ref, low_ref, grad_projected, part, vec_grad, grad_mixed):
+def self_back_first_kernel(place, lengths, grad_hidden, own, other, middle, text, vecs, projected, weights, grad_ref, low_ref, grad_projected, part, vec_grad, grad_mixed):
     inner = own[...].astype(F32) + other[...].astype(F32)
     step, gain_grad, shift_grad = norm_back(middle[...], vec(vecs, FEED_GAIN), inner)
     vec_grad[0:1, :] = gain_grad
@@ -1033,7 +1041,7 @@
 
     attn_first = gather(attn_rows_0)
     attn_1, feed_1, cross_own, text_own, cot_own = meet([ring_f], attn_1, feed_1, cross_own, text, cotangent)
-    cross_all = gather(side(cross_own, swap(cross_own), section, 1))
+    cross_got = swap(cross_own)
     text_all = side(text, swap(text_own), section, 1)
     feed_last = gather(feed_1)
     cot_all = side(cotangent, swap(cot_own), section, 1)
@@ -1041,7 +1049,10 @@
     for i in range(ring_f.steps - 2):
         ring_f.move()
         ring_d.move()
-        if i < ring_f.steps - 3:
+        if i == 0:
+            (cross_got,) = meet([ring_f, ring_d], cross_got)
+            cross_all = gather(side(cross_own, cross_got, section, 1))
+        elif i < ring_f.steps - 3:
             meet([ring_f, ring_d])
     (attn_first,) = meet([ring_f, ring_d], attn_first)
     ring_f.move()
@@ -1156,7 +1167,7 @@
     grad_middle_1, grad_low_1, feed_vec_1, query_part, grad_pairs = call(
         cross_back_kernel,
         place,
-        [late(cot_all), back_1, back_1_other, late(middle_1_far), late(vecs_far), late(cross_out_far), late(queries), pairs, late(stats_far), late(factor), late(cross_mixed_far)],
+        [back_1, back_1_other, late(middle_1_far), late(vecs_far), late(cot_all), late(cross_out_far), late(queries), pairs, late(stats_far), late(factor), late(cross_mixed_far)],
         [shape_f, shape_b, save(*shape_vec), shape_b, shape_pairs],
         scratch=[pltpu.VMEM((rows, width), BF16)],
         name="cross_back",
@@ -1207,14 +1218,15 @@
         second_grad = low(jnp.concatenate([dot_tn(normed_a1, grad_qkv_1), heads, pair_rows(dot_tn(flat(image), flat(grad_pairs)))], 1))
         parts = second_grad.reshape(count // 2, 2, piece, second_cols)
         second_grads = pick(core, parts[:, 0], parts[:, 1]), pick(core, parts[:, 1], parts[:, 0])
+    early_grads = second_grads[1]
     self_back_1_other, *second_grads = together(self_back_1_other, *second_grads)
     ring_second = Scatter(*second_grads)
-    ring_second.begin()
+    ring_second.begin(early_grads)
     (self_back_1_other,) = ring_second.step(self_back_1_other)
     grad_hidden, grad_hidden_low, self_vec_1, bias_grad_0, down_bias_grad_0, slope_0, back_0 = call(
         feed_back_first_kernel,
         place,
-        [grad_first_1, self_back_1, self_back_1_other, late(hidden_far), late(vecs_far), late(feed_w0_far, *feed_blocks), late(slope_f0)],
+        [grad_first_1, self_back_1, self_back_1_other, late(hidden_far), late(vecs_far), late(slope_f0, *[(i * width, (i + 1) * width) for i in range(FOLDS)]), late(feed_w0_far, *feed_blocks)],
         [shape_f, shape_b, save(*shape_vec), save(*shape_bias), save(*shape_one), shape_active, shape_b],
         name="feed_back_0",
         flops=feed_flops,
@@ -1237,7 +1249,7 @@
     grad_middle_0, head_low_0, grad_qkv_0, self_back_0, vecs_grad_0 = call(
         self_back_first_kernel,
         place,
-        [lengths, grad_hidden, back_0, back_0_other, late(middle_0), text_all, late(vecs_far), late(weights_0_far, *attn_blocks), late(qkv_0)],
+        [lengths, grad_hidden, back_0, back_0_other, late(middle_0), text_all, late(vecs_far), late(qkv_0), late(weights_0_far, *attn_blocks)],
         [shape_f, shape_b, shape_qkv, shape_b, shape_vec],
         scratch=half_scratch,
         name="self_back_0",
@@ -1245,7 +1257,8 @@
     )
     self_back_0_other = swap(self_back_0)
     (grad_qkv_0,) = meet_sums([ring_second], grad_qkv_0)
-    (grad_qkv_0,) = ring_second.step(grad_qkv_0)
+    grad_qkv_0, grad_pairs = ring_second.step(grad_qkv_0, grad_pairs)
+    image_grad = by_caption(image_grad_kernel, grad_pairs, keys_far, jax.ShapeDtypeStruct((captions, half_image, width), F32), "image_grad", pair_flops)
     cross_vec_woven = cross_vec_1
     if not aligned:
         cross_vec_woven = cross_vec_1.reshape(8, 2, count, cross_piece).transpose(0, 2, 1, 3).reshape(8, width)
@@ -1254,20 +1267,20 @@
         place,
         [late(normed_a0), grad_qkv_0, late(mixed_all_0), late(mixed_all_1), head_low_0, late(head_low_1), vecs_grad_0]
         + [late(v) for v in (self_vec_1, feed_vec_1, cross_vec_woven, down_bias_grad_0, down_bias_grad_1, bias_grad_0, bias_grad_1)],
-        [save(*ring_shape(core_cols + 128)), ring_shape(core_cols + 128)],
+        [save(*ring_shape(core_cols + 128)), save(*ring_shape(core_cols + 128))],
+        vmem=20,
         name="last_grads",
         flops=2 * rows * width * core_cols,
     )
-    *last_grads, feed_got_1, self_back_0_other = meet_sums([ring_second], *last_grads, feed_got_1, self_back_0_other)
+    *last_grads, feed_got_1, self_back_0_other, image_grad = meet_sums([ring_second], *last_grads, feed_got_1, self_back_0_other, image_grad)
     ring_last = Scatter(*last_grads)
     ring_last.begin()
     (grad_middle_0,) = ring_last.step(grad_middle_0)
+    (text_grad,) = call(text_grad_kernel, place, [grad_middle_0, self_back_0, self_back_0_other, text_all, late(vecs_far)], [((rows, half), F32)], name="text_grad")
+    (text_grad,) = meet_sums([ring_last], text_grad)
+    (ring_second.mine,) = ring_last.step(ring_second.mine)
     second_got = low(ring_second.result())
-    (text_grad,) = call(text_grad_kernel, place, [grad_middle_0, self_back_0, self_back_0_other, text_all, late(vecs_far)], [((rows, half), F32)], name="text_grad")
-    text_grad, second_got = meet_sums([ring_last], text_grad, second_got)
-    (grad_pairs,) = ring_last.step(grad_pairs)
-    image_grad = by_caption(image_grad_kernel, grad_pairs, keys_far, jax.ShapeDtypeStruct((captions, half_image, width), F32), "image_grad", pair_flops)
-    (image_grad,) = meet_sums([ring_last], image_grad)
+    (second_got,) = meet_sums([ring_last], second_got)
     ring_last.step()
 
     def other_half(first, later):

time: 325 us -> 324 us (level)
    all_gather x3, waiting for transfers between devices: 6.86 us -> 12.7 us  [gather(): lax.all_gather(value, 'dp', axis=0, tiled=True, axis_index_groups=groups)]
    ppermute x32, waiting for transfers between devices: 52.7 us -> 47.5 us  [ring_move(): return lax.ppermute(value, 'dp', ring_steps(shift))]
    unnamed x52 -> x50, local copies, waits for them, and re-layouts: 9.92 us -> 8.83 us
  transfers between devices with their start and end apart: 59 -> 60, of which waited for: 31 -> 32; matrix products, arithmetic and copies ran while one was open for 7% -> 7% of each run, Pallas kernels for 30% -> 30%
where the time goes in v1:
time: 324 us; the launch traced here: 319 us
  Pallas kernels  111 us (34%)
  waiting for transfers between devices  101 us (31%)
  starting transfers between devices  58 us (18%)
  other arithmetic  19.5 us (6%)
  between operations  14.7 us (5%)
  local copies, waits for them, and re-layouts  14.5 us (4%)
    pallas_call x29, Pallas kernels, call(): pl.pallas_call(functools.partial(run_kernel, kernel, tuple(in_kinds), tup...  106 us
    ppermute x32, waiting for transfers between devices, ring_move(): return lax.ppermute(value, 'dp', ring_steps(shift))  47.5 us
    ppermute x18, waiting for transfers between devices, swap(): return lax.ppermute(value, 'section', [(0, 1), (1, 0)])  35.5 us
    ppermute x32, starting transfers between devices, ring_move(): return lax.ppermute(value, 'dp', ring_steps(shift))  33.4 us
    ppermute x18, starting transfers between devices, swap(): return lax.ppermute(value, 'section', [(0, 1), (1, 0)])  23.7 us
    all_gather x3, waiting for transfers between devices, gather(): lax.all_gather(value, 'dp', axis=0, tiled=True, axis_index_groups=groups)  12.7 us
    convert_element_type x10, other arithmetic, low(): return values.astype(BF16)  10.9 us
    unnamed x50, local copies, waits for them, and re-layouts  8.83 us
  transfers between devices with their start and end apart: 60, of which 32 were waited for; matrix products, arithmetic and copies ran while one was open for 7% of the time, Pallas kernels for 30%

profile of v1, /device:TPU:0, one launch (start us, length us, event | category | flops | bytes accessed | tf_op | source)
XLA Modules:
  0.0 318.6 jit_solution(10438351875013049755)
XLA Ops:
  8.6 2.3 prepare.1
  11.0 3.0 collective-permute-start
  14.0 11.2 %collective-permute-done.refs_1_ = bf16[48,5120]{1,0:T(8,128)(2,1)S(1)} collective-permute-done((bf16[48,5120]{1,0:T(8,128)(2,1)S(1)}, bf16[48,5120]{1,0:T(8,128)(2,1)S(1)}, u32[]{:S(2)}, u32[]{:S(2)}) %collective-permute-start) | collective-permute-done | bytes 491552 | tf_op jit(solution)/shard_map/ppermute | solution.py:22
  25.2 1.4 merge.1
  26.7 1.8 collective-permute-start.2
  29.7 5.2 %collective-permute-done.2.refs_5_ = bf16[48,3072]{1,0:T(8,128)(2,1)S(1)} collective-permute-done((bf16[48,3072]{1,0:T(8,128)(2,1)S(1)}, bf16[48,3072]{1,0:T(8,128)(2,1)S(1)}, u32[]{:S(2)}, u32[]{:S(2)}) %collective-permute-start.2) | collective-permute-done | bytes 294944 | tf_op jit(solution)/shard_map/ppermute | solution.py:53
  36.7 1.5 collective-permute-start.5
  38.1 1.6 collective-permute-start.7
  40.2 1.5 collective-permute-start.8
  41.7 3.7 %collective-permute-done.8 = bf16[24,3072]{1,0:T(8,128)(2,1)S(1)} collective-permute-done((bf16[24,3072]{1,0:T(8,128)(2,1)S(1)}, bf16[24,3072]{1,0:T(8,128)(2,1)S(1)}, u32[]{:S(2)}, u32[]{:S(2)}) %collective-permute-start.8) | collective-permute-done | bytes 147488 | tf_op jit(solution)/shard_map/ppermute | solution.py:22
  45.3 12.6 %collective-permute-done.7.refs_5_ = bf16[48,1920]{1,0:T(8,128)(2,1)S(1)} collective-permute-done((bf16[48,1920]{1,0:T(8,128)(2,1)S(1)}, bf16[48,1920]{1,0:T(8,128)(2,1)S(1)}, u32[]{:S(2)}, u32[]{:S(2)}) %collective-permute-start.7) | collective-permute-done | bytes 184352 | tf_op jit(solution)/shard_map/ppermute | solution.py:53
  59.5 1.8 collective-permute-start.9
  61.6 1.5 collective-permute-start.3
  63.1 2.0 collective-permute-start.11
  65.2 7.3 %collective-permute-done.11.refs_2_ = bf16[48,1920]{1,0:T(8,128)(2,1)S(1)} collective-permute-done((bf16[48,1920]{1,0:T(8,128)(2,1)S(1)}, bf16[48,1920]{1,0:T(8,128)(2,1)S(1)}, u32[]{:S(2)}, u32[]{:S(2)}) %collective-permute-start.11) | collective-permute-done | bytes 184352 | tf_op jit(solution)/shard_map/ppermute | solution.py:53
  73.2 1.5 collective-permute-start.15
  78.4 1.9 copy-done.7
  81.1 2.8 self_0.1
  83.9 6.1 %collective-permute-done.14.refs_9_ = bf16[48,1536]{1,0:T(8,128)(2,1)S(1)} collective-permute-done((bf16[48,1536]{1,0:T(8,128)(2,1)S(1)}, bf16[48,1536]{1,0:T(8,128)(2,1)S(1)}, u32[]{:S(2)}, u32[]{:S(2)}) %collective-permute-start.14) | collective-permute-done | bytes 147488 | tf_op jit(solution)/shard_map/ppermute | solution.py:53
  90.8 1.4 collective-permute-start.17
  94.5 3.6 %collective-permute-done.17.refs_3_ = bf16[256,384]{1,0:T(8,128)(2,1)S(1)} collective-permute-done((bf16[256,384]{1,0:T(8,128)(2,1)S(1)}, bf16[256,384]{1,0:T(8,128)(2,1)S(1)}, u32[]{:S(2)}, u32[]{:S(2)}) %collective-permute-start.17) | collective-permute-done | bytes 196640 | tf_op jit(solution)/shard_map/ppermute | solution.py:22
  99.0 4.2 %feed_0.1 = (bf16[256,768]{1,0:T(8,128)(2,1)}, f32[256,768]{1,0:T(8,128)}, bf16[256,768]{1,0:T(8,128)(2,1)}, bf16[256,1536]{1,0:T(8,128)(2,1)}, bf16[256,1536]{1...) custom-call(s32[2]{0:T(128)S(1)} %pad_add_fusion.refs_0_, ...), custom_call_target="tpu_custom_call" | custom-call | flops 1207959552 | bytes 8724488 | tf_op jit(solution)/shard_map/feed_0/pallas_call | solution.py:422
  103.9 1.4 collective-permute-start.21
  106.0 3.8 %all-gather.6.cloned.1.call-done.refs_1_ = bf16[384,6144]{1,0:T(8,128)(2,1)} async-done(((bf16[24,6144]{1,0:T(8,128)(2,1)}), bf16[384,6144]{1,0:T(8,128)(2,1)}) %all-gather.6.cloned.1.call-update) | async-done | bytes 4718608 | tf_op jit(solution)/shard_map/all_gather | solution.py:1032
  109.8 2.3 copy-done.4
  116.0 4.3 %self_1.1 = (bf16[256,768]{1,0:T(8,128)(2,1)S(1)}, bf16[256,768]{1,0:T(8,128)(2,1)}, bf16[256,768]{1,0:T(8,128)(2,1)}, bf16[256,1152]{1,0:T(8,128)(2,1)}, bf16[256,384]{1,0:T(8,128)(2,1)S(1)}) custom-call(s32[2]{0:T(128)S(1)} %pad_add_fusion.refs_0_, s32[4]{0:T(128)S(1)} %copy-done.17, f32[256,768]{1,0:T(8,128)} %get-tuple-element.234.refs_2_.refs_5_, ...), custom_call_target="tpu_custom_call" | custom-call | flops 452984832 | bytes 4595736 | tf_op jit(solution)/shard_map/self_1/pallas_call | solution.py:422
  120.3 1.5 collective-permute-start.23
  121.8 5.8 %pairs.1 = (bf16[4,288,1536]{2,1,0:T(8,128)(2,1)S(1)}, bf16[768,1536]{1,0:T(8,128)(2,1)}) custom-call(s32[2]{0:T(128)S(1)} %pad_add_fusion.refs_0_, bf16[4,288,768]{2,1,0:T(8,128)(2,1)} %refs_1_.9, bf16[768,1536]{1,0:T(8,128)(2,1)S(1)} %get-tuple-element.244.refs_2_), custom_call_target="tpu_custom_call" | custom-call | flops 2717908992 | bytes 4128776 | tf_op jit(solution)/shard_map/pairs/pallas_call | solution.py:422
  127.7 6.2 %cross_1.1 = (bf16[256,768]{1,0:T(8,128)(2,1)}, f32[256,768]{1,0:T(8,128)}, bf16[256,768]{1,0:T(8,128)(2,1)}, bf16[256,768]{1,0:T(8,128)(2,1)}, bf16[256,768]{1,...) custom-call(s32[2]{0:T(128)S(1)} %pad_add_fusion.refs_0_, ...), custom_call_target="tpu_custom_call" | custom-call | flops 603979776 | bytes 8527880 | tf_op jit(solution)/shard_map/cross_1/pallas_call | solution.py:422
  135.7 1.4 collective-permute-start.25
  137.9 8.9 %all-gather.8.cloned.1.call-done.refs_1_ = bf16[768,3072]{1,0:T(8,128)(2,1)} async-done(((bf16[48,3072]{1,0:T(8,128)(2,1)}), bf16[768,3072]{1,0:T(8,128)(2,1)}) %all-gather.8.cloned.1.call-update) | async-done | bytes 4718608 | tf_op jit(solution)/shard_map/all_gather | solution.py:1032
  146.8 2.3 copy-done.3
  150.4 5.8 %feed_1.1 = (f32[256,768]{1,0:T(8,128)}, bf16[256,768]{1,0:T(8,128)(2,1)}, f32[16,256]{1,0:T(8,128)}, bf16[256,768]{1,0:T(8,128)(2,1)S(1)}, bf16[256,1536]{1,0:T...) custom-call(s32[2]{0:T(128)S(1)} %pad_add_fusion.refs_0_, ...), custom_call_target="tpu_custom_call" | custom-call | flops 1207959552 | bytes 7610376 | tf_op jit(solution)/shard_map/feed_1/pallas_call | solution.py:422
  156.2 3.7 %feed_back_1.1 = (f32[2,768]{1,0:T(2,128)}, f32[1,768]{1,0:T(1,128)}, bf16[256,1536]{1,0:T(8,128)(2,1)S(1)}, bf16[256,768]{1,0:T(8,128)(2,1)}) custom-call(s32[2]{0:T(128)S(1)} %pad_add_fusion.refs_0_, bf16[256,768]{1,0:T(8,128)(2,1)S(1)} %copy-done.2, f32[24,768]{1,0:T(8,128)S(1)} %copy-done.10, bf16[768,3072]{1,0:T(8,128)(2,1)S(1)} %reorder.5.refs_8_.refs_3_, ...), custom_call_target="tpu_custom_call" | custom-call | flops 1207959552 | bytes 5971976 | tf_op jit(solution)/shard_map/feed_back_1/pallas_call | solution.py:422
  161.3 3.3 %feed_grads_1.1 = bf16[768,3072]{1,0:T(8,128)(2,1)} custom-call(s32[2]{0:T(128)S(1)} %pad_add_fusion.refs_0_, bf16[256,768]{1,0:T(8,128)(2,1)S(1)} %get-tuple-element.260.refs_1_, bf16[256,1536]{1,0:T(8,128)(2,1)S(1)} %get-tuple-element.261.refs_2_, bf16[256,1536]{1,0:T(8,128)(2,1)S(1)} %get-tuple-element.262.refs_3_, bf16[256,768]{1,0:T(8,128)(2,1)S(1)} %copy-done.2), custom_call_target="tpu_custom_call" | custom-call | flops 1207959552 | bytes 2359304 | tf_op jit(solution)/shard_map/feed_grads_1/pallas_call | solution.py:422
  164.7 6.9 %collective-permute-done.28.refs_2_ = bf16[256,768]{1,0:T(8,128)(2,1)} collective-permute-done((bf16[256,768]{1,0:T(8,128)(2,1)}, bf16[256,768]{1,0:T(8,128)(2,1)}, u32[]{:S(2)}, u32[]{:S(2)}) %collective-permute-start.28) | collective-permute-done | bytes 393248 | tf_op jit(solution)/shard_map/ppermute | solution.py:22
  171.7 9.9 %cross_back.1 = (f32[256,768]{1,0:T(8,128)S(1)}, bf16[256,768]{1,0:T(8,128)(2,1)S(1)}, f32[8,768]{1,0:T(8,128)}, bf16[256,768]{1,0:T(8,128)(2,1)S(1)}, bf16[4,288,1536]{2,1,0:T(8,128)(2,1)S(1)}) custom-call(s32[2]{0:T(128)S(1)} %pad_add_fusion.refs_0_, bf16[256,768]{1,0:T(8,128)(2,1)} %get-tuple-element.259.refs_1_, ...), custom_call_target="tpu_custom_call" | custom-call | flops 603979776 | bytes 7593992 | tf_op jit(solution)/shard_map/cross_back/pallas_call | solution.py:422
  181.6 1.4 collective-permute-start.29
  183.0 9.3 %keys_grads.1 = (bf16[8,48,3456]{2,1,0:T(8,128)(2,1)}, bf16[8,48,3456]{2,1,0:T(8,128)(2,1)}, f32[256,768]{1,0:T(8,128)S(1)}, bf16[768,768]{1,0:T(8,128)(2,1)S(1)...) custom-call(s32[2]{0:T(128)S(1)} %pad_add_fusion.refs_0_, bf16[4,288,768]{2,1,0:T(8,128)(2,1)} %refs_1_.9, ...), custom_call_target="tpu_custom_call" | custom-call | flops 2717908992 | bytes 10813448 | tf_op jit(solution)/shard_map/keys_grads/pallas_call | solution.py:422
  192.3 7.3 %self_back_1.1 = (f32[256,768]{1,0:T(8,128)S(1)}, bf16[256,768]{1,0:T(8,128)(2,1)}, bf16[256,768]{1,0:T(8,128)(2,1)S(1)}, bf16[256,1152]{1,0:T(8,128)(2,1)S(1)},...) custom-call(s32[2]{0:T(128)S(1)} %pad_add_fusion.refs_0_, s32[4]{0:T(128)S(1)} %copy-done.17, ...), custom_call_target="tpu_custom_call" | custom-call | flops 905969664 | bytes 7151640 | tf_op jit(solution)/shard_map/self_back_1/pallas_call | solution.py:422
  200.8 4.3 %second_grads.1 = (bf16[8,48,3456]{2,1,0:T(8,128)(2,1)}, bf16[8,48,3456]{2,1,0:T(8,128)(2,1)}) custom-call(s32[2]{0:T(128)S(1)} %pad_add_fusion.refs_0_, bf16[256,768]{1,0:T(8,128)(2,1)} %get-tuple-element.283.refs_1_, bf16[256,768]{1,0:T(8,128)(2,1)S(1)} %get-tuple-element.284.refs_2_, ...), custom_call_target="tpu_custom_call", output_to_operand_aliasing={{0}: (7, {}), {1}: (8, {})} | custom-call | flops 754974720 | bytes 7864328 | tf_op jit(solution)/shard_map/second_grads/pallas_call | solution.py:422
  205.1 4.7 %collective-permute-done.30.refs_3_ = bf16[256,768]{1,0:T(8,128)(2,1)S(1)} collective-permute-done((bf16[256,768]{1,0:T(8,128)(2,1)S(1)}, bf16[256,768]{1,0:T(8,128)(2,1)S(1)}, u32[]{:S(2)}, u32[]{:S(2)}) %collective-permute-start.30) | collective-permute-done | bytes 393248 | tf_op jit(solution)/shard_map/ppermute | solution.py:22
  212.5 2.9 collective-permute-done.32
  217.6 6.4 %feed_back_0.1 = (f32[256,768]{1,0:T(8,128)S(1)}, bf16[256,768]{1,0:T(8,128)(2,1)S(1)}, f32[8,768]{1,0:T(8,128)}, f32[2,768]{1,0:T(2,128)}, f32[1,768]{1,0:T(1,1...) custom-call(s32[2]{0:T(128)S(1)} %pad_add_fusion.refs_0_, f32[256,768]{1,0:T(8,128)S(1)} %get-tuple-element.294.refs_1_, ...), custom_call_target="tpu_custom_call" | custom-call | flops 1207959552 | bytes 7544840 | tf_op jit(solution)/shard_map/feed_back_0/pallas_call | solution.py:422
  225.0 1.5 fusion.4
  228.6 4.6 %feed_grads_0.1 = bf16[768,3072]{1,0:T(8,128)(2,1)} custom-call(s32[2]{0:T(128)S(1)} %pad_add_fusion.refs_0_, bf16[256,768]{1,0:T(8,128)(2,1)} %get-tuple-element.301.refs_1_, bf16[256,1536]{1,0:T(8,128)(2,1)S(1)} %get-tuple-element.307.refs_2_, bf16[256,1536]{1,0:T(8,128)(2,1)} %get-tuple-element.308.refs_3_, bf16[256,768]{1,0:T(8,128)(2,1)S(1)} %get-tuple-element.309.refs_4_), custom_call_target="tpu_custom_call" | custom-call | flops 1207959552 | bytes 2359304 | tf_op jit(solution)/shard_map/feed_grads_0/pallas_call | solution.py:422
  233.2 1.5 collective-permute-done.33.refs_4_
  236.3 2.4 fusion.3
  240.9 7.6 %self_back_0.1 = (f32[256,768]{1,0:T(8,128)S(1)}, bf16[256,768]{1,0:T(8,128)(2,1)S(1)}, bf16[256,1152]{1,0:T(8,128)(2,1)S(1)}, bf16[256,768]{1,0:T(8,128)(2,1)S(1)}, f32[8,768]{1,0:T(8,128)S(1)}) custom-call(s32[2]{0:T(128)S(1)} %pad_add_fusion.refs_0_, s32[4]{0:T(128)S(1)} %copy-done.17, f32[256,768]{1,0:T(8,128)S(1)} %get-tuple-element.317.refs_2_, ...), custom_call_target="tpu_custom_call" | custom-call | flops 905969664 | bytes 6561816 | tf_op jit(solution)/shard_map/self_back_0/pallas_call | solution.py:422
  248.4 1.4 collective-permute-start.42
  249.9 1.6 collective-permute-done.39
  251.5 1.9 fusion.2
  255.4 4.3 %last_grads.1 = (bf16[8,48,2048]{2,1,0:T(8,128)(2,1)}, bf16[8,48,2048]{2,1,0:T(8,128)(2,1)}) custom-call(s32[2]{0:T(128)S(1)} %pad_add_fusion.refs_0_, bf16[256,768]{1,0:T(8,128)(2,1)} %get-tuple-element.328.refs_1_, bf16[256,1152]{1,0:T(8,128)(2,1)S(1)} %get-tuple-element.329.refs_2_, bf16[256,768]{1,0:T(8,128)(2,1)} %get-tuple-element.330.refs_3_, ...), custom_call_target="tpu_custom_call" | custom-call | flops 754974720 | bytes 2672648 | tf_op jit(solution)/shard_map/last_grads/pallas_call | solution.py:422
  259.7 4.5 %image_grad.1 = f32[4,288,768]{2,1,0:T(8,128)} custom-call(bf16[4,288,1536]{2,1,0:T(8,128)(2,1)S(1)} %copy-done.6, bf16[768,1536]{1,0:T(8,128)(2,1)S(1)} %copy-done.18), custom_call_target="tpu_custom_call" | custom-call | flops 2717908992 | bytes 7077888 | tf_op jit(solution)/shard_map/image_grad/pallas_call | solution.py:605
  267.6 1.8 collective-permute-done.43
  273.7 2.7 text_grad.1
  279.2 1.6 collective-permute-start.47
  282.2 5.2 %collective-permute-done.46 = bf16[48,2048]{1,0:T(8,128)(2,1)S(1)} collective-permute-done((bf16[48,2048]{1,0:T(8,128)(2,1)S(1)}, bf16[48,2048]{1,0:T(8,128)(2,1)S(1)}, u32[]{:S(2)}, u32[]{:S(2)}) %collective-permute-start.46) | collective-permute-done | bytes 196640 | tf_op jit(solution)/shard_map/ppermute | solution.py:53
  295.9 1.4 fusion.8
  301.6 1.4 collective-permute-done.50
  305.2 1.4 collective-permute-start.52
  306.7 1.8 collective-permute-done.53.refs_2_
  308.5 1.9 finish_feed.1
  310.4 1.4 finish_heads.1
  (181 shorter events, 68.5 us)
Async XLA Ops:
  7.2 54.4 %copy-start.24 = (bf16[256,384]{1,0:T(8,128)(2,1)S(1)}, bf16[256,384]{1,0:T(8,128)(2,1)}, u32[]{:S(2)}) copy-start(bf16[256,384]{1,0:T(8,128)(2,1)} %param.19) | copy-start | bytes 589828
  7.2 66.0 %all-gather.4.cloned.1.call-start = ((), (), s32[]{:S(2)}) async-start(), calls=%async_computation.2 | async-start | bytes 3342336 | tf_op jit(solution)/shard_map/all_gather | solution.py:1032
  11.0 14.2 %collective-permute-start = (bf16[48,5120]{1,0:T(8,128)(2,1)S(1)}, bf16[48,5120]{1,0:T(8,128)(2,1)S(1)}, u32[]{:S(2)}, u32[]{:S(2)}) collective-permute-start(bf16[48,5120]{1,0:T(8,128)(2,1)S(1)} %get-tuple-element.205), channel_id=1, source_target_pairs={{0,16},{16,0},{1,17},{17,1},{2,18},{18,2},{3,19},{19,3},{4,20},{20... | collective-permute-start | bytes 1474568 | tf_op jit(solution)/shard_map/ppermute | solution.py:22
  26.7 83.1 %all-gather.6.cloned.1.call-start = ((), (), s32[]{:S(2)}) async-start(), calls=%async_computation.3 | async-start | bytes 5013504 | tf_op jit(solution)/shard_map/all_gather | solution.py:1032
  26.7 8.2 %collective-permute-start.2 = (bf16[48,3072]{1,0:T(8,128)(2,1)S(1)}, bf16[48,3072]{1,0:T(8,128)(2,1)S(1)}, u32[]{:S(2)}, u32[]{:S(2)}) collective-permute-start(bf16[48,3072]{1,0:T(8,128)(2,1)S(1)} %get-tuple-element.209.refs_4_), channel_id=1, source_target_pairs={{0,2},{1,3},{4,0},{5,1},{8,4},{9,5},{12,8},{13,9},{14,12},{15,13},... | collective-permute-start | bytes 884744 | tf_op jit(solution)/shard_map/ppermute | solution.py:53
  28.5 7.6 %collective-permute-start.1 = (bf16[48,3072]{1,0:T(8,128)(2,1)S(1)}, bf16[48,3072]{1,0:T(8,128)(2,1)S(1)}, u32[]{:S(2)}, u32[]{:S(2)}) collective-permute-start(bf16[48,3072]{1,0:T(8,128)(2,1)S(1)} %get-tuple-element.209.refs_4_), channel_id=1, source_target_pairs={{0,4},{1,5},{4,8},{5,9},{8,12},{9,13},{12,14},{13,15},{14,10},{15,... | collective-permute-start | bytes 884744 | tf_op jit(solution)/shard_map/ppermute | solution.py:53
  36.1 21.8 %collective-permute-start.4 = (bf16[48,3072]{1,0:T(8,128)(2,1)S(1)}, bf16[48,3072]{1,0:T(8,128)(2,1)S(1)}, u32[]{:S(2)}, u32[]{:S(2)}) collective-permute-start(bf16[48,3072]{1,0:T(8,128)(2,1)S(1)} %collective-permute-done.1.refs_3_), channel_id=1, source_target_pairs={{0,4},{1,5},{4,8},{5,9},{8,12},{9,13},{12,14},{13,15},{14,10},{15,... | collective-permute-start | bytes 884744 | tf_op jit(solution)/shard_map/ppermute | solution.py:53
  36.7 21.2 %collective-permute-start.5 = (bf16[48,3072]{1,0:T(8,128)(2,1)S(1)}, bf16[48,3072]{1,0:T(8,128)(2,1)S(1)}, u32[]{:S(2)}, u32[]{:S(2)}) collective-permute-start(bf16[48,3072]{1,0:T(8,128)(2,1)S(1)} %collective-permute-done.2.refs_5_), channel_id=1, source_target_pairs={{0,2},{1,3},{4,0},{5,1},{8,4},{9,5},{12,8},{13,9},{14,12},{15,13},... | collective-permute-start | bytes 884744 | tf_op jit(solution)/shard_map/ppermute | solution.py:53
  38.1 19.8 %collective-permute-start.7 = (bf16[48,1920]{1,0:T(8,128)(2,1)S(1)}, bf16[48,1920]{1,0:T(8,128)(2,1)S(1)}, u32[]{:S(2)}, u32[]{:S(2)}) collective-permute-start(bf16[48,1920]{1,0:T(8,128)(2,1)S(1)} %get-tuple-element.215.refs_4_), channel_id=1, source_target_pairs={{0,2},{1,3},{4,0},{5,1},{8,4},{9,5},{12,8},{13,9},{14,12},{15,13},... | collective-permute-start | bytes 552968 | tf_op jit(solution)/shard_map/ppermute | solution.py:53
  39.7 18.2 %collective-permute-start.6 = (bf16[48,1920]{1,0:T(8,128)(2,1)S(1)}, bf16[48,1920]{1,0:T(8,128)(2,1)S(1)}, u32[]{:S(2)}, u32[]{:S(2)}) collective-permute-start(bf16[48,1920]{1,0:T(8,128)(2,1)S(1)} %get-tuple-element.215.refs_4_), channel_id=1, source_target_pairs={{0,4},{1,5},{4,8},{5,9},{8,12},{9,13},{12,14},{13,15},{14,10},{15,... | collective-permute-start | bytes 552968 | tf_op jit(solution)/shard_map/ppermute | solution.py:53
  40.2 5.1 %collective-permute-start.8 = (bf16[24,3072]{1,0:T(8,128)(2,1)S(1)}, bf16[24,3072]{1,0:T(8,128)(2,1)S(1)}, u32[]{:S(2)}, u32[]{:S(2)}) collective-permute-start(bf16[24,3072]{1,0:T(8,128)(2,1)S(1)} %pad_maximum_fusion.3), channel_id=1, source_target_pairs={{0,16},{16,0},{1,17},{17,1},{2,18},{18,2},{3,19},{19,3},{4,20},{20... | collective-permute-start | bytes 442376 | tf_op jit(solution)/shard_map/ppermute | solution.py:22
  58.7 88.0 %all-gather.8.cloned.1.call-start = ((), (), s32[]{:S(2)}) async-start(), calls=%async_computation.4 | async-start | bytes 5013504 | tf_op jit(solution)/shard_map/all_gather | solution.py:1032
  59.5 206.2 %reduce-scatter.3.cloned.1.call-start = ((), (), s32[]{:S(2)}) async-start(), calls=%async_computation.5 | async-start | bytes 5013504 | tf_op jit(solution)/shard_map/reduce_scatter | solution.py:1151
  59.5 13.6 %collective-permute-start.9 = (bf16[48,3072]{1,0:T(8,128)(2,1)S(1)}, bf16[48,3072]{1,0:T(8,128)(2,1)S(1)}, u32[]{:S(2)}, u32[]{:S(2)}) collective-permute-start(bf16[48,3072]{1,0:T(8,128)(2,1)S(1)} %collective-permute-done.4.refs_2_), channel_id=1, source_target_pairs={{0,4},{1,5},{4,8},{5,9},{8,12},{9,13},{12,14},{13,15},{14,10},{15,... | collective-permute-start | bytes 884744 | tf_op jit(solution)/shard_map/ppermute | solution.py:53
  61.3 11.8 %collective-permute-start.10 = (bf16[48,3072]{1,0:T(8,128)(2,1)S(1)}, bf16[48,3072]{1,0:T(8,128)(2,1)S(1)}, u32[]{:S(2)}, u32[]{:S(2)}) collective-permute-start(bf16[48,3072]{1,0:T(8,128)(2,1)S(1)} %collective-permute-done.5.refs_6_), channel_id=1, source_target_pairs={{0,2},{1,3},{4,0},{5,1},{8,4},{9,5},{12,8},{13,9},{14,12},{15,13},... | collective-permute-start | bytes 884744 | tf_op jit(solution)/shard_map/ppermute | solution.py:53
  61.6 13.7 %collective-permute-start.3 = (bf16[256,384]{1,0:T(8,128)(2,1)S(1)}, bf16[256,384]{1,0:T(8,128)(2,1)}, u32[]{:S(2)}, u32[]{:S(2)}) collective-permute-start(bf16[256,384]{1,0:T(8,128)(2,1)S(1)} %copy-done.24), channel_id=1, source_target_pairs={{0,16},{16,0},{1,17},{17,1},{2,18},{18,2},{3,19},{19,3},{4,20},{20... | collective-permute-start | bytes 589832 | tf_op jit(solution)/shard_map/ppermute | solution.py:22
  63.1 9.4 %collective-permute-start.11 = (bf16[48,1920]{1,0:T(8,128)(2,1)S(1)}, bf16[48,1920]{1,0:T(8,128)(2,1)S(1)}, u32[]{:S(2)}, u32[]{:S(2)}) collective-permute-start(bf16[48,1920]{1,0:T(8,128)(2,1)S(1)} %collective-permute-done.6.refs_3_), channel_id=1, source_target_pairs={{0,4},{1,5},{4,8},{5,9},{8,12},{9,13},{12,14},{13,15},{14,10},{15,... | collective-permute-start | bytes 552968 | tf_op jit(solution)/shard_map/ppermute | solution.py:53
  65.1 8.1 %collective-permute-start.12 = (bf16[48,1920]{1,0:T(8,128)(2,1)S(1)}, bf16[48,1920]{1,0:T(8,128)(2,1)S(1)}, u32[]{:S(2)}, u32[]{:S(2)}) collective-permute-start(bf16[48,1920]{1,0:T(8,128)(2,1)S(1)} %collective-permute-done.7.refs_5_), channel_id=1, source_target_pairs={{0,2},{1,3},{4,0},{5,1},{8,4},{9,5},{12,8},{13,9},{14,12},{15,13},... | collective-permute-start | bytes 552968 | tf_op jit(solution)/shard_map/ppermute | solution.py:53
  73.2 16.8 %collective-permute-start.15 = (bf16[48,1920]{1,0:T(8,128)(2,1)S(1)}, bf16[48,1920]{1,0:T(8,128)(2,1)S(1)}, u32[]{:S(2)}, u32[]{:S(2)}) collective-permute-start(bf16[48,1920]{1,0:T(8,128)(2,1)S(1)} %collective-permute-done.11.refs_2_), channel_id=1, source_target_pairs={{0,4},{1,5},{4,8},{5,9},{8,12},{9,13},{12,14},{13,15},{14,10},{15,... | collective-permute-start | bytes 552968 | tf_op jit(solution)/shard_map/ppermute | solution.py:53
  74.7 15.3 %collective-permute-start.16 = (bf16[48,1920]{1,0:T(8,128)(2,1)S(1)}, bf16[48,1920]{1,0:T(8,128)(2,1)S(1)}, u32[]{:S(2)}, u32[]{:S(2)}) collective-permute-start(bf16[48,1920]{1,0:T(8,128)(2,1)S(1)} %collective-permute-done.12.refs_6_), channel_id=1, source_target_pairs={{0,2},{1,3},{4,0},{5,1},{8,4},{9,5},{12,8},{13,9},{14,12},{15,13},... | collective-permute-start | bytes 552968 | tf_op jit(solution)/shard_map/ppermute | solution.py:53
  76.3 13.7 %collective-permute-start.14 = (bf16[48,1536]{1,0:T(8,128)(2,1)S(1)}, bf16[48,1536]{1,0:T(8,128)(2,1)S(1)}, u32[]{:S(2)}, u32[]{:S(2)}) collective-permute-start(bf16[48,1536]{1,0:T(8,128)(2,1)S(1)} %slice.87), channel_id=1, source_target_pairs={{0,2},{1,3},{4,0},{5,1},{8,4},{9,5},{12,8},{13,9},{14,12},{15,13},... | collective-permute-start | bytes 442376 | tf_op jit(solution)/shard_map/ppermute | solution.py:53
  77.2 12.8 %collective-permute-start.13 = (bf16[48,1536]{1,0:T(8,128)(2,1)S(1)}, bf16[48,1536]{1,0:T(8,128)(2,1)S(1)}, u32[]{:S(2)}, u32[]{:S(2)}) collective-permute-start(bf16[48,1536]{1,0:T(8,128)(2,1)S(1)} %slice.86), channel_id=1, source_target_pairs={{0,4},{1,5},{4,8},{5,9},{8,12},{9,13},{12,14},{13,15},{14,10},{15,... | collective-permute-start | bytes 442376 | tf_op jit(solution)/shard_map/ppermute | solution.py:53
  80.3 18.6 %copy-start = (bf16[256,768]{1,0:T(8,128)(2,1)}, bf16[256,768]{1,0:T(8,128)(2,1)S(1)}, u32[]{:S(2)}) copy-start(bf16[256,768]{1,0:T(8,128)(2,1)S(1)} %pad_maximum_fusion.refs_2_.refs_1_.refs_6_.refs_4_) | copy-start | bytes 1179652
  83.9 32.1 %copy-start.8 = (f32[24,768]{1,0:T(8,128)}, f32[24,768]{1,0:T(8,128)S(1)}, u32[]{:S(2)}) copy-start(f32[24,768]{1,0:T(8,128)S(1)} %get-tuple-element.232.refs_4_.refs_5_.refs_6_.refs_2_) | copy-start | bytes 221188
  90.7 7.4 %collective-permute-start.18 = (bf16[8,48,3072]{2,1,0:T(8,128)(2,1)S(1)}, bf16[8,48,3072]{2,1,0:T(8,128)(2,1)S(1)}, u32[]{:S(2)}, u32[]{:S(2)}) collective-permute-start(bf16[8,48,3072]{2,1,0:T(8,128)(2,1)S(1)} %pack.2.refs_1_), channel_id=1, source_target_pairs={{0,1},{1,0},{2,3},{3,2},{4,5},{5,4},{6,7},{7,6},{8,9},{9,8},{10,11... | collective-permute-start | bytes 7077896 | tf_op jit(solution)/shard_map/ppermute | solution.py:57
  90.8 7.3 %collective-permute-start.17 = (bf16[256,384]{1,0:T(8,128)(2,1)S(1)}, bf16[256,384]{1,0:T(8,128)(2,1)S(1)}, u32[]{:S(2)}, u32[]{:S(2)}) collective-permute-start(bf16[256,384]{1,0:T(8,128)(2,1)S(1)} %get-tuple-element.228.refs_2_), channel_id=1, source_target_pairs={{0,16},{16,0},{1,17},{17,1},{2,18},{18,2},{3,19},{19,3},{4,20},{20... | collective-permute-start | bytes 589832 | tf_op jit(solution)/shard_map/ppermute | solution.py:22
  92.2 11.0 %collective-permute-start.19 = (bf16[48,896]{1,0:T(8,128)(2,1)S(1)}, bf16[48,896]{1,0:T(8,128)(2,1)S(1)}, u32[]{:S(2)}, u32[]{:S(2)}) collective-permute-start(bf16[48,896]{1,0:T(8,128)(2,1)S(1)} %slice.88), channel_id=1, source_target_pairs={{0,4},{1,5},{4,8},{5,9},{8,12},{9,13},{12,14},{13,15},{14,10},{15,... | collective-permute-start | bytes 258056 | tf_op jit(solution)/shard_map/ppermute | solution.py:53
  93.3 9.9 %collective-permute-start.20 = (bf16[48,1024]{1,0:T(8,128)(2,1)S(1)}, bf16[48,1024]{1,0:T(8,128)(2,1)S(1)}, u32[]{:S(2)}, u32[]{:S(2)}) collective-permute-start(bf16[48,1024]{1,0:T(8,128)(2,1)S(1)} %slice.89), channel_id=1, source_target_pairs={{0,2},{1,3},{4,0},{5,1},{8,4},{9,5},{12,8},{13,9},{14,12},{15,13},... | collective-permute-start | bytes 294920 | tf_op jit(solution)/shard_map/ppermute | solution.py:53
  103.8 10.1 %collective-permute-start.22 = (bf16[8,48,1920]{2,1,0:T(8,128)(2,1)S(1)}, bf16[8,48,1920]{2,1,0:T(8,128)(2,1)S(1)}, u32[]{:S(2)}, u32[]{:S(2)}) collective-permute-start(bf16[8,48,1920]{2,1,0:T(8,128)(2,1)S(1)} %pack.3.refs_1_), channel_id=1, source_target_pairs={{0,1},{1,0},{2,3},{3,2},{4,5},{5,4},{6,7},{7,6},{8,9},{9,8},{10,11... | collective-permute-start | bytes 4423688 | tf_op jit(solution)/shard_map/ppermute | solution.py:57
  103.9 12.1 %collective-permute-start.21 = (bf16[256,768]{1,0:T(8,128)(2,1)S(1)}, bf16[256,768]{1,0:T(8,128)(2,1)}, u32[]{:S(2)}, u32[]{:S(2)}) collective-permute-start(bf16[256,768]{1,0:T(8,128)(2,1)S(1)} %get-tuple-element.238.refs_3_), channel_id=1, source_target_pairs={{0,16},{16,0},{1,17},{17,1},{2,18},{18,2},{3,19},{19,3},{4,20},{20... | collective-permute-start | bytes 1179656 | tf_op jit(solution)/shard_map/ppermute | solution.py:22
  105.3 29.2 %collective-permute-start.27 = (bf16[256,384]{1,0:T(8,128)(2,1)}, bf16[256,384]{1,0:T(8,128)(2,1)}, u32[]{:S(2)}, u32[]{:S(2)}) collective-permute-start(bf16[256,384]{1,0:T(8,128)(2,1)} %param.37), channel_id=1, source_target_pairs={{0,16},{16,0},{1,17},{17,1},{2,18},{18,2},{3,19},{19,3},{4,20},{20... | collective-permute-start | bytes 589832 | tf_op jit(solution)/shard_map/ppermute | solution.py:22
  120.3 7.3 %collective-permute-start.23 = (bf16[256,384]{1,0:T(8,128)(2,1)S(1)}, bf16[256,384]{1,0:T(8,128)(2,1)S(1)}, u32[]{:S(2)}, u32[]{:S(2)}) collective-permute-start(bf16[256,384]{1,0:T(8,128)(2,1)S(1)} %get-tuple-element.242.refs_2_), channel_id=1, source_target_pairs={{0,16},{16,0},{1,17},{17,1},{2,18},{18,2},{3,19},{19,3},{4,20},{20... | collective-permute-start | bytes 589832 | tf_op jit(solution)/shard_map/ppermute | solution.py:22
  133.8 16.1 %collective-permute-start.24 = (bf16[256,768]{1,0:T(8,128)(2,1)}, bf16[256,768]{1,0:T(8,128)(2,1)}, u32[]{:S(2)}, u32[]{:S(2)}) collective-permute-start(bf16[256,768]{1,0:T(8,128)(2,1)} %get-tuple-element.250.refs_2_), channel_id=1, source_target_pairs={{0,16},{16,0},{1,17},{17,1},{2,18},{18,2},{3,19},{19,3},{4,20},{20... | collective-permute-start | bytes 1179656 | tf_op jit(solution)/shard_map/ppermute | solution.py:22
  135.7 14.3 %collective-permute-start.25 = (f32[32,256]{1,0:T(8,128)}, f32[32,256]{1,0:T(8,128)}, u32[]{:S(2)}, u32[]{:S(2)}) collective-permute-start(f32[32,256]{1,0:T(8,128)} %get-tuple-element.251.refs_4_), channel_id=1, source_target_pairs={{0,16},{16,0},{1,17},{17,1},{2,18},{18,2},{3,19},{19,3},{4,20},{20... | collective-permute-start | bytes 98312 | tf_op jit(solution)/shard_map/ppermute | solution.py:22
  160.0 11.6 %collective-permute-start.28 = (bf16[256,768]{1,0:T(8,128)(2,1)}, bf16[256,768]{1,0:T(8,128)(2,1)}, u32[]{:S(2)}, u32[]{:S(2)}) collective-permute-start(bf16[256,768]{1,0:T(8,128)(2,1)} %get-tuple-element.259.refs_1_), channel_id=1, source_target_pairs={{0,16},{16,0},{1,17},{17,1},{2,18},{18,2},{3,19},{19,3},{4,20},{20... | collective-permute-start | bytes 1179656 | tf_op jit(solution)/shard_map/ppermute | solution.py:22
  171.6 124.3 %reduce-scatter.5.cloned.1.call-start = ((), (), s32[]{:S(2)}) async-start(), calls=%async_computation.6 | async-start | bytes 5013504 | tf_op jit(solution)/shard_map/reduce_scatter | solution.py:1151
  181.6 10.6 %collective-permute-start.29 = (bf16[256,768]{1,0:T(8,128)(2,1)S(1)}, bf16[256,768]{1,0:T(8,128)(2,1)S(1)}, u32[]{:S(2)}, u32[]{:S(2)}) collective-permute-start(bf16[256,768]{1,0:T(8,128)(2,1)S(1)} %get-tuple-element.270.refs_3_), channel_id=1, source_target_pairs={{0,16},{16,0},{1,17},{17,1},{2,18},{18,2},{3,19},{19,3},{4,20},{20... | collective-permute-start | bytes 1179656 | tf_op jit(solution)/shard_map/ppermute | solution.py:22
  199.6 10.3 %collective-permute-start.30 = (bf16[256,768]{1,0:T(8,128)(2,1)S(1)}, bf16[256,768]{1,0:T(8,128)(2,1)S(1)}, u32[]{:S(2)}, u32[]{:S(2)}) collective-permute-start(bf16[256,768]{1,0:T(8,128)(2,1)S(1)} %get-tuple-element.282.refs_2_), channel_id=1, source_target_pairs={{0,16},{16,0},{1,17},{17,1},{2,18},{18,2},{3,19},{19,3},{4,20},{20... | collective-permute-start | bytes 1179656 | tf_op jit(solution)/shard_map/ppermute | solution.py:22
  209.8 15.2 %collective-permute-start.31 = (bf16[8,48,3456]{2,1,0:T(8,128)(2,1)}, bf16[8,48,3456]{2,1,0:T(8,128)(2,1)}, u32[]{:S(2)}, u32[]{:S(2)}) collective-permute-start(bf16[8,48,3456]{2,1,0:T(8,128)(2,1)} %get-tuple-element.293), channel_id=1, source_target_pairs={{0,1},{1,0},{2,3},{3,2},{4,5},{5,4},{6,7},{7,6},{8,9},{9,8},{10,11... | collective-permute-start | bytes 7962632 | tf_op jit(solution)/shard_map/ppermute | solution.py:57
  210.8 4.6 %collective-permute-start.32 = (bf16[48,3456]{1,0:T(8,128)(2,1)S(1)}, bf16[48,3456]{1,0:T(8,128)(2,1)S(1)}, u32[]{:S(2)}, u32[]{:S(2)}) collective-permute-start(bf16[48,3456]{1,0:T(8,128)(2,1)S(1)} %dynamic-slice_bitcast_fusion.1), channel_id=1, source_target_pairs={{0,1},{1,0},{2,3},{3,2},{4,5},{5,4},{6,7},{7,6},{8,9},{9,8},{10,11... | collective-permute-start | bytes 995336 | tf_op jit(solution)/shard_map/ppermute | solution.py:57
  215.6 9.5 %collective-permute-start.35 = (bf16[48,1792]{1,0:T(8,128)(2,1)S(1)}, bf16[48,1792]{1,0:T(8,128)(2,1)S(1)}, u32[]{:S(2)}, u32[]{:S(2)}) collective-permute-start(bf16[48,1792]{1,0:T(8,128)(2,1)S(1)} %add_convert_fusion), channel_id=1, source_target_pairs={{0,2},{1,3},{4,0},{5,1},{8,4},{9,5},{12,8},{13,9},{14,12},{15,13},... | collective-permute-start | bytes 516104 | tf_op jit(solution)/shard_map/ppermute | solution.py:53
  216.8 8.2 %collective-permute-start.34 = (bf16[48,1664]{1,0:T(8,128)(2,1)S(1)}, bf16[48,1664]{1,0:T(8,128)(2,1)S(1)}, u32[]{:S(2)}, u32[]{:S(2)}) collective-permute-start(bf16[48,1664]{1,0:T(8,128)(2,1)S(1)} %add_convert_fusion.1), channel_id=1, source_target_pairs={{0,4},{1,5},{4,8},{5,9},{8,12},{9,13},{12,14},{13,15},{14,10},{15,... | collective-permute-start | bytes 479240 | tf_op jit(solution)/shard_map/ppermute | solution.py:53
  224.0 10.6 %collective-permute-start.33 = (bf16[256,768]{1,0:T(8,128)(2,1)S(1)}, bf16[256,768]{1,0:T(8,128)(2,1)S(1)}, u32[]{:S(2)}, u32[]{:S(2)}) collective-permute-start(bf16[256,768]{1,0:T(8,128)(2,1)S(1)} %get-tuple-element.318.refs_3_), channel_id=1, source_target_pairs={{0,16},{16,0},{1,17},{17,1},{2,18},{18,2},{3,19},{19,3},{4,20},{20... | collective-permute-start | bytes 1179656 | tf_op jit(solution)/shard_map/ppermute | solution.py:22
  226.5 9.0 %collective-permute-start.36 = (bf16[48,3456]{1,0:T(8,128)(2,1)S(1)}, bf16[48,3456]{1,0:T(8,128)(2,1)S(1)}, u32[]{:S(2)}, u32[]{:S(2)}) collective-permute-start(bf16[48,3456]{1,0:T(8,128)(2,1)S(1)} %get-tuple-element.310), channel_id=1, source_target_pairs={{0,4},{1,5},{4,8},{5,9},{8,12},{9,13},{12,14},{13,15},{14,10},{15,... | collective-permute-start | bytes 995336 | tf_op jit(solution)/shard_map/ppermute | solution.py:53
  227.6 8.7 %collective-permute-start.37 = (bf16[48,3456]{1,0:T(8,128)(2,1)S(1)}, bf16[48,3456]{1,0:T(8,128)(2,1)S(1)}, u32[]{:S(2)}, u32[]{:S(2)}) collective-permute-start(bf16[48,3456]{1,0:T(8,128)(2,1)S(1)} %get-tuple-element.311), channel_id=1, source_target_pairs={{0,2},{1,3},{4,0},{5,1},{8,4},{9,5},{12,8},{13,9},{14,12},{15,13},... | collective-permute-start | bytes 995336 | tf_op jit(solution)/shard_map/ppermute | solution.py:53
  238.7 11.2 %collective-permute-start.38 = (bf16[48,3456]{1,0:T(8,128)(2,1)}, bf16[48,3456]{1,0:T(8,128)(2,1)}, u32[]{:S(2)}, u32[]{:S(2)}) collective-permute-start(bf16[48,3456]{1,0:T(8,128)(2,1)} %get-tuple-element.315), channel_id=1, source_target_pairs={{0,4},{1,5},{4,8},{5,9},{8,12},{9,13},{12,14},{13,15},{14,10},{15,... | collective-permute-start | bytes 995336 | tf_op jit(solution)/shard_map/ppermute | solution.py:53
  239.9 11.6 %collective-permute-start.39 = (bf16[48,3456]{1,0:T(8,128)(2,1)}, bf16[48,3456]{1,0:T(8,128)(2,1)}, u32[]{:S(2)}, u32[]{:S(2)}) collective-permute-start(bf16[48,3456]{1,0:T(8,128)(2,1)} %get-tuple-element.316), channel_id=1, source_target_pairs={{0,2},{1,3},{4,0},{5,1},{8,4},{9,5},{12,8},{13,9},{14,12},{15,13},... | collective-permute-start | bytes 995336 | tf_op jit(solution)/shard_map/ppermute | solution.py:53
  240.9 18.8 %copy-start.18 = (bf16[768,1536]{1,0:T(8,128)(2,1)S(1)}, bf16[768,1536]{1,0:T(8,128)(2,1)}, u32[]{:S(2)}) copy-start(bf16[768,1536]{1,0:T(8,128)(2,1)} %get-tuple-element.347.keys) | copy-start | bytes 7077892
  248.4 15.8 %collective-permute-start.42 = (bf16[256,768]{1,0:T(8,128)(2,1)S(1)}, bf16[256,768]{1,0:T(8,128)(2,1)S(1)}, u32[]{:S(2)}, u32[]{:S(2)}) collective-permute-start(bf16[256,768]{1,0:T(8,128)(2,1)S(1)} %get-tuple-element.345.refs_2_), channel_id=1, source_target_pairs={{0,16},{16,0},{1,17},{17,1},{2,18},{18,2},{3,19},{19,3},{4,20},{20... | collective-permute-start | bytes 1179656 | tf_op jit(solution)/shard_map/ppermute | solution.py:22
  253.4 11.5 %collective-permute-start.40 = (bf16[48,3456]{1,0:T(8,128)(2,1)S(1)}, bf16[48,3456]{1,0:T(8,128)(2,1)S(1)}, u32[]{:S(2)}, u32[]{:S(2)}) collective-permute-start(bf16[48,3456]{1,0:T(8,128)(2,1)S(1)} %get-tuple-element.326), channel_id=1, source_target_pairs={{0,4},{1,5},{4,8},{5,9},{8,12},{9,13},{12,14},{13,15},{14,10},{15,... | collective-permute-start | bytes 995336 | tf_op jit(solution)/shard_map/ppermute | solution.py:53
  254.5 11.2 %collective-permute-start.41 = (bf16[48,3456]{1,0:T(8,128)(2,1)S(1)}, bf16[48,3456]{1,0:T(8,128)(2,1)}, u32[]{:S(2)}, u32[]{:S(2)}) collective-permute-start(bf16[48,3456]{1,0:T(8,128)(2,1)S(1)} %get-tuple-element.327), channel_id=1, source_target_pairs={{0,2},{1,3},{4,0},{5,1},{8,4},{9,5},{12,8},{13,9},{14,12},{15,13},... | collective-permute-start | bytes 995336 | tf_op jit(solution)/shard_map/ppermute | solution.py:53
  265.7 3.8 %collective-permute-start.43 = (bf16[8,48,2048]{2,1,0:T(8,128)(2,1)}, bf16[8,48,2048]{2,1,0:T(8,128)(2,1)}, u32[]{:S(2)}, u32[]{:S(2)}) collective-permute-start(bf16[8,48,2048]{2,1,0:T(8,128)(2,1)} %get-tuple-element.349), channel_id=1, source_target_pairs={{0,1},{1,0},{2,3},{3,2},{4,5},{5,4},{6,7},{7,6},{8,9},{9,8},{10,11... | collective-permute-start | bytes 4718600 | tf_op jit(solution)/shard_map/ppermute | solution.py:57
  270.6 5.8 %collective-permute-start.44 = (bf16[48,1024]{1,0:T(8,128)(2,1)S(1)}, bf16[48,1024]{1,0:T(8,128)(2,1)S(1)}, u32[]{:S(2)}, u32[]{:S(2)}) collective-permute-start(bf16[48,1024]{1,0:T(8,128)(2,1)S(1)} %get-tuple-element.351), channel_id=1, source_target_pairs={{0,4},{1,5},{4,8},{5,9},{8,12},{9,13},{12,14},{13,15},{14,10},{15,... | collective-permute-start | bytes 294920 | tf_op jit(solution)/shard_map/ppermute | solution.py:53
  271.7 5.9 %collective-permute-start.45 = (bf16[48,1024]{1,0:T(8,128)(2,1)S(1)}, bf16[48,1024]{1,0:T(8,128)(2,1)S(1)}, u32[]{:S(2)}, u32[]{:S(2)}) collective-permute-start(bf16[48,1024]{1,0:T(8,128)(2,1)S(1)} %get-tuple-element.352), channel_id=1, source_target_pairs={{0,2},{1,3},{4,0},{5,1},{8,4},{9,5},{12,8},{13,9},{14,12},{15,13},... | collective-permute-start | bytes 294920 | tf_op jit(solution)/shard_map/ppermute | solution.py:53
  272.7 18.8 %collective-permute-start.26 = (bf16[256,384]{1,0:T(8,128)(2,1)S(1)}, bf16[256,384]{1,0:T(8,128)(2,1)S(1)}, u32[]{:S(2)}, u32[]{:S(2)}) collective-permute-start(bf16[256,384]{1,0:T(8,128)(2,1)S(1)} %broadcast_select_fusion.3), channel_id=1, source_target_pairs={{0,16},{16,0},{1,17},{17,1},{2,18},{18,2},{3,19},{19,3},{4,20},{20... | collective-permute-start | bytes 589832 | tf_op jit(solution)/shard_map/ppermute | solution.py:22
  278.8 8.6 %collective-permute-start.46 = (bf16[48,2048]{1,0:T(8,128)(2,1)S(1)}, bf16[48,2048]{1,0:T(8,128)(2,1)S(1)}, u32[]{:S(2)}, u32[]{:S(2)}) collective-permute-start(bf16[48,2048]{1,0:T(8,128)(2,1)S(1)} %get-tuple-element.359), channel_id=1, source_target_pairs={{0,4},{1,5},{4,8},{5,9},{8,12},{9,13},{12,14},{13,15},{14,10},{15,... | collective-permute-start | bytes 589832 | tf_op jit(solution)/shard_map/ppermute | solution.py:53
  279.2 8.4 %collective-permute-start.47 = (bf16[48,2048]{1,0:T(8,128)(2,1)S(1)}, bf16[48,2048]{1,0:T(8,128)(2,1)S(1)}, u32[]{:S(2)}, u32[]{:S(2)}) collective-permute-start(bf16[48,2048]{1,0:T(8,128)(2,1)S(1)} %get-tuple-element.360), channel_id=1, source_target_pairs={{0,2},{1,3},{4,0},{5,1},{8,4},{9,5},{12,8},{13,9},{14,12},{15,13},... | collective-permute-start | bytes 589832 | tf_op jit(solution)/shard_map/ppermute | solution.py:53
  288.8 4.4 %collective-permute-start.54 = (bf16[24,1536]{1,0:T(8,128)(2,1)S(1)}, bf16[24,1536]{1,0:T(8,128)(2,1)S(1)}, u32[]{:S(2)}, u32[]{:S(2)}) collective-permute-start(bf16[24,1536]{1,0:T(8,128)(2,1)S(1)} %slice_select_fusion), channel_id=1, source_target_pairs={{0,16},{16,0},{1,17},{17,1},{2,18},{18,2},{3,19},{19,3},{4,20},{20... | collective-permute-start | bytes 221192 | tf_op jit(solution)/shard_map/ppermute | solution.py:22
  289.5 5.7 %collective-permute-start.48 = (bf16[48,2048]{1,0:T(8,128)(2,1)S(1)}, bf16[48,2048]{1,0:T(8,128)(2,1)S(1)}, u32[]{:S(2)}, u32[]{:S(2)}) collective-permute-start(bf16[48,2048]{1,0:T(8,128)(2,1)S(1)} %get-tuple-element.366), channel_id=1, source_target_pairs={{0,4},{1,5},{4,8},{5,9},{8,12},{9,13},{12,14},{13,15},{14,10},{15,... | collective-permute-start | bytes 589832 | tf_op jit(solution)/shard_map/ppermute | solution.py:53
  290.1 5.8 %collective-permute-start.49 = (bf16[48,2048]{1,0:T(8,128)(2,1)S(1)}, bf16[48,2048]{1,0:T(8,128)(2,1)S(1)}, u32[]{:S(2)}, u32[]{:S(2)}) collective-permute-start(bf16[48,2048]{1,0:T(8,128)(2,1)S(1)} %get-tuple-element.367), channel_id=1, source_target_pairs={{0,2},{1,3},{4,0},{5,1},{8,4},{9,5},{12,8},{13,9},{14,12},{15,13},... | collective-permute-start | bytes 589832 | tf_op jit(solution)/shard_map/ppermute | solution.py:53
  297.3 5.7 %collective-permute-start.50 = (bf16[48,2048]{1,0:T(8,128)(2,1)S(1)}, bf16[48,2048]{1,0:T(8,128)(2,1)S(1)}, u32[]{:S(2)}, u32[]{:S(2)}) collective-permute-start(bf16[48,2048]{1,0:T(8,128)(2,1)S(1)} %get-tuple-element.371), channel_id=1, source_target_pairs={{0,4},{1,5},{4,8},{5,9},{8,12},{9,13},{12,14},{13,15},{14,10},{15,... | collective-permute-start | bytes 589832 | tf_op jit(solution)/shard_map/ppermute | solution.py:53
  298.4 5.7 %collective-permute-start.51 = (bf16[48,2048]{1,0:T(8,128)(2,1)S(1)}, bf16[48,2048]{1,0:T(8,128)(2,1)S(1)}, u32[]{:S(2)}, u32[]{:S(2)}) collective-permute-start(bf16[48,2048]{1,0:T(8,128)(2,1)S(1)} %get-tuple-element.372), channel_id=1, source_target_pairs={{0,2},{1,3},{4,0},{5,1},{8,4},{9,5},{12,8},{13,9},{14,12},{15,13},... | collective-permute-start | bytes 589832 | tf_op jit(solution)/shard_map/ppermute | solution.py:53
  300.4 8.1 %collective-permute-start.53 = (bf16[48,3072]{1,0:T(8,128)(2,1)S(1)}, bf16[48,3072]{1,0:T(8,128)(2,1)S(1)}, u32[]{:S(2)}, u32[]{:S(2)}) collective-permute-start(bf16[48,3072]{1,0:T(8,128)(2,1)S(1)} %get-tuple-element.410), channel_id=1, source_target_pairs={{0,16},{16,0},{1,17},{17,1},{2,18},{18,2},{3,19},{19,3},{4,20},{20... | collective-permute-start | bytes 884744 | tf_op jit(solution)/shard_map/ppermute | solution.py:22
  305.2 5.1 %collective-permute-start.52 = (bf16[48,1280]{1,0:T(8,128)(2,1)S(1)}, bf16[48,1280]{1,0:T(8,128)(2,1)S(1)}, u32[]{:S(2)}, u32[]{:S(2)}) collective-permute-start(bf16[48,1280]{1,0:T(8,128)(2,1)S(1)} %pad_maximum_fusion.4), channel_id=1, source_target_pairs={{0,16},{16,0},{1,17},{17,1},{2,18},{18,2},{3,19},{19,3},{4,20},{20... | collective-permute-start | bytes 368648 | tf_op jit(solution)/shard_map/ppermute | solution.py:22
  (21 other events, 132.9 us)
Sparse Core Ops, SparseCore 0:
  26.8 39.8 all-gather.3
  68.8 40.9 all-gather.5
  111.4 35.3 all-gather.7
  171.7 52.2 reduce-scatter.2
  236.4 56.8 reduce-scatter.4

commit v2 on v1

--- a/solution.py
+++ b/solution.py
@@ -90,6 +90,13 @@
                 begin = part * source.shape[0] + spot * rows
                 out[begin : begin + rows, :] = source[i * rows : (i + 1) * rows, offset : offset + out.shape[1]]
             offset += out.shape[1]
+
+
+def reorder_late_kernel(order, blocks, place, source, out):
+    rows = source.shape[0] // len(order)
+    for begin, end in blocks:
+        for i, spot in enumerate(order):
+            out[spot * rows : (spot + 1) * rows, begin:end] = source[i * rows : (i + 1) * rows, begin:end]
 
 
 class Gather:
@@ -1129,7 +1136,11 @@
         keep=(4, 5),
     )
     cross_part_other, stats_other = swap(cross_part), swap(stats)
-    (feed_w1,) = reordered(feed_last, order, 1, [2 * half_ff])
+    if aligned:
+        col_blocks = [(i * width, (i + 1) * width) for i in range(2 * FOLDS)]
+        (feed_w1,) = call(functools.partial(reorder_late_kernel, order, col_blocks), place, [late(feed_last, *col_blocks)], [((width, 2 * half_ff), BF16)], name="reorder_late")
+    else:
+        (feed_w1,) = reordered(feed_last, order, 1, [2 * half_ff])
     middle_1_far, cross_mixed_far, factor, normed_f1, slope_f1, active_1, part_1, cross_out_far = call(
         feed_second_kernel,
         place,

time: 324 us -> 324 us (level)
    unnamed x50 -> x48, local copies, waits for them, and re-layouts: 8.83 us -> 6.06 us
  transfers between devices with their start and end apart: 60 -> 60, of which waited for: 32 -> 34; matrix products, arithmetic and copies ran while one was open for 7% -> 7% of each run, Pallas kernels for 30% -> 31%
where the time goes in v2:
time: 324 us; the launch traced here: 318 us
  Pallas kernels  113 us (35%)
  waiting for transfers between devices  101 us (31%)
  starting transfers between devices  58.3 us (18%)
  other arithmetic  19.5 us (6%)
  between operations  14.7 us (5%)
  local copies, waits for them, and re-layouts  11.8 us (4%)
    pallas_call x29, Pallas kernels, call(): pl.pallas_call(functools.partial(run_kernel, kernel, tuple(in_kinds), tup...  108 us
    ppermute x32, waiting for transfers between devices, ring_move(): return lax.ppermute(value, 'dp', ring_steps(shift))  47.9 us
    ppermute x18, waiting for transfers between devices, swap(): return lax.ppermute(value, 'section', [(0, 1), (1, 0)])  35.3 us
    ppermute x32, starting transfers between devices, ring_move(): return lax.ppermute(value, 'dp', ring_steps(shift))  33.4 us
    ppermute x18, starting transfers between devices, swap(): return lax.ppermute(value, 'section', [(0, 1), (1, 0)])  23.9 us
    all_gather x3, waiting for transfers between devices, gather(): lax.all_gather(value, 'dp', axis=0, tiled=True, axis_index_groups=groups)  12.7 us
    convert_element_type x10, other arithmetic, low(): return values.astype(BF16)  10.9 us
  transfers between devices with their start and end apart: 60, of which 34 were waited for; matrix products, arithmetic and copies ran while one was open for 7% of the time, Pallas kernels for 31%

profile of v2, /device:TPU:0, one launch (start us, length us, event | category | flops | bytes accessed | tf_op | source)
XLA Modules:
  0.0 318.2 jit_solution(1884318873586692803)
XLA Ops:
  8.6 2.3 prepare.1
  11.0 3.0 collective-permute-start
  14.0 11.2 %collective-permute-done.refs_1_ = bf16[48,5120]{1,0:T(8,128)(2,1)S(1)} collective-permute-done((bf16[48,5120]{1,0:T(8,128)(2,1)S(1)}, bf16[48,5120]{1,0:T(8,128)(2,1)S(1)}, u32[]{:S(2)}, u32[]{:S(2)}) %collective-permute-start) | collective-permute-done | bytes 491552 | tf_op jit(solution)/shard_map/ppermute | solution.py:22
  25.2 1.4 merge.1
  26.7 1.8 collective-permute-start.2
  29.7 5.2 %collective-permute-done.2.refs_5_ = bf16[48,3072]{1,0:T(8,128)(2,1)S(1)} collective-permute-done((bf16[48,3072]{1,0:T(8,128)(2,1)S(1)}, bf16[48,3072]{1,0:T(8,128)(2,1)S(1)}, u32[]{:S(2)}, u32[]{:S(2)}) %collective-permute-start.2) | collective-permute-done | bytes 294944 | tf_op jit(solution)/shard_map/ppermute | solution.py:53
  36.7 1.5 collective-permute-start.5
  38.1 1.6 collective-permute-start.7
  40.2 1.5 collective-permute-start.8
  41.7 3.7 %collective-permute-done.8 = bf16[24,3072]{1,0:T(8,128)(2,1)S(1)} collective-permute-done((bf16[24,3072]{1,0:T(8,128)(2,1)S(1)}, bf16[24,3072]{1,0:T(8,128)(2,1)S(1)}, u32[]{:S(2)}, u32[]{:S(2)}) %collective-permute-start.8) | collective-permute-done | bytes 147488 | tf_op jit(solution)/shard_map/ppermute | solution.py:22
  45.3 12.6 %collective-permute-done.7.refs_5_ = bf16[48,1920]{1,0:T(8,128)(2,1)S(1)} collective-permute-done((bf16[48,1920]{1,0:T(8,128)(2,1)S(1)}, bf16[48,1920]{1,0:T(8,128)(2,1)S(1)}, u32[]{:S(2)}, u32[]{:S(2)}) %collective-permute-start.7) | collective-permute-done | bytes 184352 | tf_op jit(solution)/shard_map/ppermute | solution.py:53
  59.5 1.8 collective-permute-start.9
  61.6 1.5 collective-permute-start.3
  63.1 2.0 collective-permute-start.11
  65.2 7.3 %collective-permute-done.11.refs_2_ = bf16[48,1920]{1,0:T(8,128)(2,1)S(1)} collective-permute-done((bf16[48,1920]{1,0:T(8,128)(2,1)S(1)}, bf16[48,1920]{1,0:T(8,128)(2,1)S(1)}, u32[]{:S(2)}, u32[]{:S(2)}) %collective-permute-start.11) | collective-permute-done | bytes 184352 | tf_op jit(solution)/shard_map/ppermute | solution.py:53
  73.2 1.5 collective-permute-start.15
  78.4 1.9 copy-done.6
  81.1 2.8 self_0.1
  83.9 6.1 %collective-permute-done.14.refs_9_ = bf16[48,1536]{1,0:T(8,128)(2,1)S(1)} collective-permute-done((bf16[48,1536]{1,0:T(8,128)(2,1)S(1)}, bf16[48,1536]{1,0:T(8,128)(2,1)S(1)}, u32[]{:S(2)}, u32[]{:S(2)}) %collective-permute-start.14) | collective-permute-done | bytes 147488 | tf_op jit(solution)/shard_map/ppermute | solution.py:53
  90.8 1.4 collective-permute-start.17
  94.5 3.6 %collective-permute-done.17.refs_3_ = bf16[256,384]{1,0:T(8,128)(2,1)S(1)} collective-permute-done((bf16[256,384]{1,0:T(8,128)(2,1)S(1)}, bf16[256,384]{1,0:T(8,128)(2,1)S(1)}, u32[]{:S(2)}, u32[]{:S(2)}) %collective-permute-start.17) | collective-permute-done | bytes 196640 | tf_op jit(solution)/shard_map/ppermute | solution.py:22
  99.0 4.2 %feed_0.1 = (bf16[256,768]{1,0:T(8,128)(2,1)}, f32[256,768]{1,0:T(8,128)}, bf16[256,768]{1,0:T(8,128)(2,1)}, bf16[256,1536]{1,0:T(8,128)(2,1)}, bf16[256,1536]{1...) custom-call(s32[2]{0:T(128)S(1)} %pad_add_fusion.refs_0_, ...), custom_call_target="tpu_custom_call" | custom-call | flops 1207959552 | bytes 8724488 | tf_op jit(solution)/shard_map/feed_0/pallas_call | solution.py:429
  103.9 1.4 collective-permute-start.21
  106.0 3.8 %all-gather.6.cloned.1.call-done.refs_1_ = bf16[384,6144]{1,0:T(8,128)(2,1)} async-done(((bf16[24,6144]{1,0:T(8,128)(2,1)}), bf16[384,6144]{1,0:T(8,128)(2,1)}) %all-gather.6.cloned.1.call-update) | async-done | bytes 4718608 | tf_op jit(solution)/shard_map/all_gather | solution.py:1039
  109.8 2.3 copy-done.3
  116.0 4.3 %self_1.1 = (bf16[256,768]{1,0:T(8,128)(2,1)S(1)}, bf16[256,768]{1,0:T(8,128)(2,1)}, bf16[256,768]{1,0:T(8,128)(2,1)}, bf16[256,1152]{1,0:T(8,128)(2,1)}, bf16[256,384]{1,0:T(8,128)(2,1)S(1)}) custom-call(s32[2]{0:T(128)S(1)} %pad_add_fusion.refs_0_, s32[4]{0:T(128)S(1)} %copy-done.16, f32[256,768]{1,0:T(8,128)} %get-tuple-element.234.refs_2_.refs_5_, ...), custom_call_target="tpu_custom_call" | custom-call | flops 452984832 | bytes 4595736 | tf_op jit(solution)/shard_map/self_1/pallas_call | solution.py:429
  120.3 1.5 collective-permute-start.23
  121.8 5.8 %pairs.1 = (bf16[4,288,1536]{2,1,0:T(8,128)(2,1)S(1)}, bf16[768,1536]{1,0:T(8,128)(2,1)}) custom-call(s32[2]{0:T(128)S(1)} %pad_add_fusion.refs_0_, bf16[4,288,768]{2,1,0:T(8,128)(2,1)} %refs_1_.9, bf16[768,1536]{1,0:T(8,128)(2,1)S(1)} %get-tuple-element.244.refs_2_), custom_call_target="tpu_custom_call" | custom-call | flops 2717908992 | bytes 4128776 | tf_op jit(solution)/shard_map/pairs/pallas_call | solution.py:429
  127.7 6.2 %cross_1.1 = (bf16[256,768]{1,0:T(8,128)(2,1)}, f32[256,768]{1,0:T(8,128)}, bf16[256,768]{1,0:T(8,128)(2,1)}, bf16[256,768]{1,0:T(8,128)(2,1)}, bf16[256,768]{1,...) custom-call(s32[2]{0:T(128)S(1)} %pad_add_fusion.refs_0_, ...), custom_call_target="tpu_custom_call" | custom-call | flops 603979776 | bytes 8527880 | tf_op jit(solution)/shard_map/cross_1/pallas_call | solution.py:429
  135.6 1.4 collective-permute-start.25
  137.9 8.9 %all-gather.8.cloned.1.call-done.refs_1_ = bf16[768,3072]{1,0:T(8,128)(2,1)} async-done(((bf16[48,3072]{1,0:T(8,128)(2,1)}), bf16[768,3072]{1,0:T(8,128)(2,1)}) %all-gather.8.cloned.1.call-update) | async-done | bytes 4718608 | tf_op jit(solution)/shard_map/all_gather | solution.py:1039
  146.8 3.0 reorder_late.1.refs_8_.refs_3_
  149.8 5.8 %feed_1.1 = (f32[256,768]{1,0:T(8,128)}, bf16[256,768]{1,0:T(8,128)(2,1)}, f32[16,256]{1,0:T(8,128)}, bf16[256,768]{1,0:T(8,128)(2,1)S(1)}, bf16[256,1536]{1,0:T...) custom-call(s32[2]{0:T(128)S(1)} %pad_add_fusion.refs_0_, ...), custom_call_target="tpu_custom_call" | custom-call | flops 1207959552 | bytes 7610376 | tf_op jit(solution)/shard_map/feed_1/pallas_call | solution.py:429
  155.7 3.7 %feed_back_1.1 = (f32[2,768]{1,0:T(2,128)}, f32[1,768]{1,0:T(1,128)}, bf16[256,1536]{1,0:T(8,128)(2,1)S(1)}, bf16[256,768]{1,0:T(8,128)(2,1)}) custom-call(s32[2]{0:T(128)S(1)} %pad_add_fusion.refs_0_, bf16[256,768]{1,0:T(8,128)(2,1)S(1)} %copy-done.2, f32[24,768]{1,0:T(8,128)S(1)} %copy-done.9, bf16[768,3072]{1,0:T(8,128)(2,1)S(1)} %reorder_late.1.refs_8_.refs_3_, ...), custom_call_target="tpu_custom_call" | custom-call | flops 1207959552 | bytes 5971976 | tf_op jit(solution)/shard_map/feed_back_1/pallas_call | solution.py:429
  159.4 1.5 collective-permute-start.28
  160.9 3.4 %feed_grads_1.1 = bf16[768,3072]{1,0:T(8,128)(2,1)} custom-call(s32[2]{0:T(128)S(1)} %pad_add_fusion.refs_0_, bf16[256,768]{1,0:T(8,128)(2,1)S(1)} %get-tuple-element.260.refs_1_, bf16[256,1536]{1,0:T(8,128)(2,1)S(1)} %get-tuple-element.261.refs_2_, bf16[256,1536]{1,0:T(8,128)(2,1)S(1)} %get-tuple-element.262.refs_3_, bf16[256,768]{1,0:T(8,128)(2,1)S(1)} %copy-done.2), custom_call_target="tpu_custom_call" | custom-call | flops 1207959552 | bytes 2359304 | tf_op jit(solution)/shard_map/feed_grads_1/pallas_call | solution.py:429
  164.3 6.8 %collective-permute-done.28.refs_2_ = bf16[256,768]{1,0:T(8,128)(2,1)} collective-permute-done((bf16[256,768]{1,0:T(8,128)(2,1)}, bf16[256,768]{1,0:T(8,128)(2,1)}, u32[]{:S(2)}, u32[]{:S(2)}) %collective-permute-start.28) | collective-permute-done | bytes 393248 | tf_op jit(solution)/shard_map/ppermute | solution.py:22
  171.1 9.9 %cross_back.1 = (f32[256,768]{1,0:T(8,128)S(1)}, bf16[256,768]{1,0:T(8,128)(2,1)S(1)}, f32[8,768]{1,0:T(8,128)}, bf16[256,768]{1,0:T(8,128)(2,1)S(1)}, bf16[4,288,1536]{2,1,0:T(8,128)(2,1)S(1)}) custom-call(s32[2]{0:T(128)S(1)} %pad_add_fusion.refs_0_, bf16[256,768]{1,0:T(8,128)(2,1)} %get-tuple-element.259.refs_1_, ...), custom_call_target="tpu_custom_call" | custom-call | flops 603979776 | bytes 7593992 | tf_op jit(solution)/shard_map/cross_back/pallas_call | solution.py:429
  181.1 1.5 collective-permute-start.29
  182.5 9.3 %keys_grads.1 = (bf16[8,48,3456]{2,1,0:T(8,128)(2,1)}, bf16[8,48,3456]{2,1,0:T(8,128)(2,1)}, f32[256,768]{1,0:T(8,128)S(1)}, bf16[768,768]{1,0:T(8,128)(2,1)S(1)...) custom-call(s32[2]{0:T(128)S(1)} %pad_add_fusion.refs_0_, bf16[4,288,768]{2,1,0:T(8,128)(2,1)} %refs_1_.9, ...), custom_call_target="tpu_custom_call" | custom-call | flops 2717908992 | bytes 10813448 | tf_op jit(solution)/shard_map/keys_grads/pallas_call | solution.py:429
  191.8 7.3 %self_back_1.1 = (f32[256,768]{1,0:T(8,128)S(1)}, bf16[256,768]{1,0:T(8,128)(2,1)}, bf16[256,768]{1,0:T(8,128)(2,1)S(1)}, bf16[256,1152]{1,0:T(8,128)(2,1)S(1)},...) custom-call(s32[2]{0:T(128)S(1)} %pad_add_fusion.refs_0_, s32[4]{0:T(128)S(1)} %copy-done.16, ...), custom_call_target="tpu_custom_call" | custom-call | flops 905969664 | bytes 7151640 | tf_op jit(solution)/shard_map/self_back_1/pallas_call | solution.py:429
  200.3 4.4 %second_grads.1 = (bf16[8,48,3456]{2,1,0:T(8,128)(2,1)}, bf16[8,48,3456]{2,1,0:T(8,128)(2,1)}) custom-call(s32[2]{0:T(128)S(1)} %pad_add_fusion.refs_0_, bf16[256,768]{1,0:T(8,128)(2,1)} %get-tuple-element.283.refs_1_, bf16[256,768]{1,0:T(8,128)(2,1)S(1)} %get-tuple-element.284.refs_2_, ...), custom_call_target="tpu_custom_call", output_to_operand_aliasing={{0}: (7, {}), {1}: (8, {})} | custom-call | flops 754974720 | bytes 7864328 | tf_op jit(solution)/shard_map/second_grads/pallas_call | solution.py:429
  204.7 4.7 %collective-permute-done.30.refs_3_ = bf16[256,768]{1,0:T(8,128)(2,1)S(1)} collective-permute-done((bf16[256,768]{1,0:T(8,128)(2,1)S(1)}, bf16[256,768]{1,0:T(8,128)(2,1)S(1)}, u32[]{:S(2)}, u32[]{:S(2)}) %collective-permute-start.30) | collective-permute-done | bytes 393248 | tf_op jit(solution)/shard_map/ppermute | solution.py:22
  212.1 2.6 collective-permute-done.32
  216.9 6.4 %feed_back_0.1 = (f32[256,768]{1,0:T(8,128)S(1)}, bf16[256,768]{1,0:T(8,128)(2,1)S(1)}, f32[8,768]{1,0:T(8,128)}, f32[2,768]{1,0:T(2,128)}, f32[1,768]{1,0:T(1,1...) custom-call(s32[2]{0:T(128)S(1)} %pad_add_fusion.refs_0_, f32[256,768]{1,0:T(8,128)S(1)} %get-tuple-element.294.refs_1_, ...), custom_call_target="tpu_custom_call" | custom-call | flops 1207959552 | bytes 7544840 | tf_op jit(solution)/shard_map/feed_back_0/pallas_call | solution.py:429
  224.6 1.5 fusion.4
  228.1 4.6 %feed_grads_0.1 = bf16[768,3072]{1,0:T(8,128)(2,1)} custom-call(s32[2]{0:T(128)S(1)} %pad_add_fusion.refs_0_, bf16[256,768]{1,0:T(8,128)(2,1)} %get-tuple-element.301.refs_1_, bf16[256,1536]{1,0:T(8,128)(2,1)S(1)} %get-tuple-element.307.refs_2_, bf16[256,1536]{1,0:T(8,128)(2,1)} %get-tuple-element.308.refs_3_, bf16[256,768]{1,0:T(8,128)(2,1)S(1)} %get-tuple-element.309.refs_4_), custom_call_target="tpu_custom_call" | custom-call | flops 1207959552 | bytes 2359304 | tf_op jit(solution)/shard_map/feed_grads_0/pallas_call | solution.py:429
  232.8 1.4 collective-permute-done.33.refs_4_
  235.8 2.4 fusion.3
  240.3 7.6 %self_back_0.1 = (f32[256,768]{1,0:T(8,128)S(1)}, bf16[256,768]{1,0:T(8,128)(2,1)S(1)}, bf16[256,1152]{1,0:T(8,128)(2,1)S(1)}, bf16[256,768]{1,0:T(8,128)(2,1)S(1)}, f32[8,768]{1,0:T(8,128)S(1)}) custom-call(s32[2]{0:T(128)S(1)} %pad_add_fusion.refs_0_, s32[4]{0:T(128)S(1)} %copy-done.16, f32[256,768]{1,0:T(8,128)S(1)} %get-tuple-element.317.refs_2_, ...), custom_call_target="tpu_custom_call" | custom-call | flops 905969664 | bytes 6561816 | tf_op jit(solution)/shard_map/self_back_0/pallas_call | solution.py:429
  247.9 1.4 collective-permute-start.42
  249.3 1.6 collective-permute-done.39
  251.0 1.9 fusion.2
  255.0 4.3 %last_grads.1 = (bf16[8,48,2048]{2,1,0:T(8,128)(2,1)}, bf16[8,48,2048]{2,1,0:T(8,128)(2,1)}) custom-call(s32[2]{0:T(128)S(1)} %pad_add_fusion.refs_0_, bf16[256,768]{1,0:T(8,128)(2,1)} %get-tuple-element.328.refs_1_, bf16[256,1152]{1,0:T(8,128)(2,1)S(1)} %get-tuple-element.329.refs_2_, bf16[256,768]{1,0:T(8,128)(2,1)} %get-tuple-element.330.refs_3_, ...), custom_call_target="tpu_custom_call" | custom-call | flops 754974720 | bytes 2672648 | tf_op jit(solution)/shard_map/last_grads/pallas_call | solution.py:429
  259.3 4.5 %image_grad.1 = f32[4,288,768]{2,1,0:T(8,128)} custom-call(bf16[4,288,1536]{2,1,0:T(8,128)(2,1)S(1)} %copy-done.5, bf16[768,1536]{1,0:T(8,128)(2,1)S(1)} %copy-done.17), custom_call_target="tpu_custom_call" | custom-call | flops 2717908992 | bytes 7077888 | tf_op jit(solution)/shard_map/image_grad/pallas_call | solution.py:612
  267.2 1.8 collective-permute-done.43
  273.1 2.7 text_grad.1
  281.3 5.3 %collective-permute-done.46 = bf16[48,2048]{1,0:T(8,128)(2,1)S(1)} collective-permute-done((bf16[48,2048]{1,0:T(8,128)(2,1)S(1)}, bf16[48,2048]{1,0:T(8,128)(2,1)S(1)}, u32[]{:S(2)}, u32[]{:S(2)}) %collective-permute-start.46) | collective-permute-done | bytes 196640 | tf_op jit(solution)/shard_map/ppermute | solution.py:53
  296.8 1.5 collective-permute-start.50
  301.1 1.4 collective-permute-done.50
  302.5 1.4 collective-permute-done.51
  306.1 1.9 collective-permute-done.53.refs_2_
  308.1 1.9 finish_feed.1
  310.0 1.4 finish_heads.1
  (179 shorter events, 67.6 us)
Async XLA Ops:
  7.2 54.4 %copy-start.23 = (bf16[256,384]{1,0:T(8,128)(2,1)S(1)}, bf16[256,384]{1,0:T(8,128)(2,1)}, u32[]{:S(2)}) copy-start(bf16[256,384]{1,0:T(8,128)(2,1)} %param.19) | copy-start | bytes 589828
  7.2 66.0 %all-gather.4.cloned.1.call-start = ((), (), s32[]{:S(2)}) async-start(), calls=%async_computation.2 | async-start | bytes 3342336 | tf_op jit(solution)/shard_map/all_gather | solution.py:1039
  11.0 14.2 %collective-permute-start = (bf16[48,5120]{1,0:T(8,128)(2,1)S(1)}, bf16[48,5120]{1,0:T(8,128)(2,1)S(1)}, u32[]{:S(2)}, u32[]{:S(2)}) collective-permute-start(bf16[48,5120]{1,0:T(8,128)(2,1)S(1)} %get-tuple-element.205), channel_id=1, source_target_pairs={{0,16},{16,0},{1,17},{17,1},{2,18},{18,2},{3,19},{19,3},{4,20},{20... | collective-permute-start | bytes 1474568 | tf_op jit(solution)/shard_map/ppermute | solution.py:22
  26.7 83.1 %all-gather.6.cloned.1.call-start = ((), (), s32[]{:S(2)}) async-start(), calls=%async_computation.3 | async-start | bytes 5013504 | tf_op jit(solution)/shard_map/all_gather | solution.py:1039
  26.7 8.2 %collective-permute-start.2 = (bf16[48,3072]{1,0:T(8,128)(2,1)S(1)}, bf16[48,3072]{1,0:T(8,128)(2,1)S(1)}, u32[]{:S(2)}, u32[]{:S(2)}) collective-permute-start(bf16[48,3072]{1,0:T(8,128)(2,1)S(1)} %get-tuple-element.209.refs_4_), channel_id=1, source_target_pairs={{0,2},{1,3},{4,0},{5,1},{8,4},{9,5},{12,8},{13,9},{14,12},{15,13},... | collective-permute-start | bytes 884744 | tf_op jit(solution)/shard_map/ppermute | solution.py:53
  28.5 7.6 %collective-permute-start.1 = (bf16[48,3072]{1,0:T(8,128)(2,1)S(1)}, bf16[48,3072]{1,0:T(8,128)(2,1)S(1)}, u32[]{:S(2)}, u32[]{:S(2)}) collective-permute-start(bf16[48,3072]{1,0:T(8,128)(2,1)S(1)} %get-tuple-element.209.refs_4_), channel_id=1, source_target_pairs={{0,4},{1,5},{4,8},{5,9},{8,12},{9,13},{12,14},{13,15},{14,10},{15,... | collective-permute-start | bytes 884744 | tf_op jit(solution)/shard_map/ppermute | solution.py:53
  36.1 21.8 %collective-permute-start.4 = (bf16[48,3072]{1,0:T(8,128)(2,1)S(1)}, bf16[48,3072]{1,0:T(8,128)(2,1)S(1)}, u32[]{:S(2)}, u32[]{:S(2)}) collective-permute-start(bf16[48,3072]{1,0:T(8,128)(2,1)S(1)} %collective-permute-done.1.refs_3_), channel_id=1, source_target_pairs={{0,4},{1,5},{4,8},{5,9},{8,12},{9,13},{12,14},{13,15},{14,10},{15,... | collective-permute-start | bytes 884744 | tf_op jit(solution)/shard_map/ppermute | solution.py:53
  36.7 21.2 %collective-permute-start.5 = (bf16[48,3072]{1,0:T(8,128)(2,1)S(1)}, bf16[48,3072]{1,0:T(8,128)(2,1)S(1)}, u32[]{:S(2)}, u32[]{:S(2)}) collective-permute-start(bf16[48,3072]{1,0:T(8,128)(2,1)S(1)} %collective-permute-done.2.refs_5_), channel_id=1, source_target_pairs={{0,2},{1,3},{4,0},{5,1},{8,4},{9,5},{12,8},{13,9},{14,12},{15,13},... | collective-permute-start | bytes 884744 | tf_op jit(solution)/shard_map/ppermute | solution.py:53
  38.1 19.8 %collective-permute-start.7 = (bf16[48,1920]{1,0:T(8,128)(2,1)S(1)}, bf16[48,1920]{1,0:T(8,128)(2,1)S(1)}, u32[]{:S(2)}, u32[]{:S(2)}) collective-permute-start(bf16[48,1920]{1,0:T(8,128)(2,1)S(1)} %get-tuple-element.215.refs_4_), channel_id=1, source_target_pairs={{0,2},{1,3},{4,0},{5,1},{8,4},{9,5},{12,8},{13,9},{14,12},{15,13},... | collective-permute-start | bytes 552968 | tf_op jit(solution)/shard_map/ppermute | solution.py:53
  39.7 18.2 %collective-permute-start.6 = (bf16[48,1920]{1,0:T(8,128)(2,1)S(1)}, bf16[48,1920]{1,0:T(8,128)(2,1)S(1)}, u32[]{:S(2)}, u32[]{:S(2)}) collective-permute-start(bf16[48,1920]{1,0:T(8,128)(2,1)S(1)} %get-tuple-element.215.refs_4_), channel_id=1, source_target_pairs={{0,4},{1,5},{4,8},{5,9},{8,12},{9,13},{12,14},{13,15},{14,10},{15,... | collective-permute-start | bytes 552968 | tf_op jit(solution)/shard_map/ppermute | solution.py:53
  40.2 5.1 %collective-permute-start.8 = (bf16[24,3072]{1,0:T(8,128)(2,1)S(1)}, bf16[24,3072]{1,0:T(8,128)(2,1)S(1)}, u32[]{:S(2)}, u32[]{:S(2)}) collective-permute-start(bf16[24,3072]{1,0:T(8,128)(2,1)S(1)} %pad_maximum_fusion.3), channel_id=1, source_target_pairs={{0,16},{16,0},{1,17},{17,1},{2,18},{18,2},{3,19},{19,3},{4,20},{20... | collective-permute-start | bytes 442376 | tf_op jit(solution)/shard_map/ppermute | solution.py:22
  58.7 88.0 %all-gather.8.cloned.1.call-start = ((), (), s32[]{:S(2)}) async-start(), calls=%async_computation.4 | async-start | bytes 5013504 | tf_op jit(solution)/shard_map/all_gather | solution.py:1039
  59.5 205.8 %reduce-scatter.3.cloned.1.call-start = ((), (), s32[]{:S(2)}) async-start(), calls=%async_computation.5 | async-start | bytes 5013504 | tf_op jit(solution)/shard_map/reduce_scatter | solution.py:1162
  59.5 13.6 %collective-permute-start.9 = (bf16[48,3072]{1,0:T(8,128)(2,1)S(1)}, bf16[48,3072]{1,0:T(8,128)(2,1)S(1)}, u32[]{:S(2)}, u32[]{:S(2)}) collective-permute-start(bf16[48,3072]{1,0:T(8,128)(2,1)S(1)} %collective-permute-done.4.refs_2_), channel_id=1, source_target_pairs={{0,4},{1,5},{4,8},{5,9},{8,12},{9,13},{12,14},{13,15},{14,10},{15,... | collective-permute-start | bytes 884744 | tf_op jit(solution)/shard_map/ppermute | solution.py:53
  61.3 11.8 %collective-permute-start.10 = (bf16[48,3072]{1,0:T(8,128)(2,1)S(1)}, bf16[48,3072]{1,0:T(8,128)(2,1)S(1)}, u32[]{:S(2)}, u32[]{:S(2)}) collective-permute-start(bf16[48,3072]{1,0:T(8,128)(2,1)S(1)} %collective-permute-done.5.refs_6_), channel_id=1, source_target_pairs={{0,2},{1,3},{4,0},{5,1},{8,4},{9,5},{12,8},{13,9},{14,12},{15,13},... | collective-permute-start | bytes 884744 | tf_op jit(solution)/shard_map/ppermute | solution.py:53
  61.6 13.7 %collective-permute-start.3 = (bf16[256,384]{1,0:T(8,128)(2,1)S(1)}, bf16[256,384]{1,0:T(8,128)(2,1)}, u32[]{:S(2)}, u32[]{:S(2)}) collective-permute-start(bf16[256,384]{1,0:T(8,128)(2,1)S(1)} %copy-done.23), channel_id=1, source_target_pairs={{0,16},{16,0},{1,17},{17,1},{2,18},{18,2},{3,19},{19,3},{4,20},{20... | collective-permute-start | bytes 589832 | tf_op jit(solution)/shard_map/ppermute | solution.py:22
  63.1 9.4 %collective-permute-start.11 = (bf16[48,1920]{1,0:T(8,128)(2,1)S(1)}, bf16[48,1920]{1,0:T(8,128)(2,1)S(1)}, u32[]{:S(2)}, u32[]{:S(2)}) collective-permute-start(bf16[48,1920]{1,0:T(8,128)(2,1)S(1)} %collective-permute-done.6.refs_3_), channel_id=1, source_target_pairs={{0,4},{1,5},{4,8},{5,9},{8,12},{9,13},{12,14},{13,15},{14,10},{15,... | collective-permute-start | bytes 552968 | tf_op jit(solution)/shard_map/ppermute | solution.py:53
  65.1 8.1 %collective-permute-start.12 = (bf16[48,1920]{1,0:T(8,128)(2,1)S(1)}, bf16[48,1920]{1,0:T(8,128)(2,1)S(1)}, u32[]{:S(2)}, u32[]{:S(2)}) collective-permute-start(bf16[48,1920]{1,0:T(8,128)(2,1)S(1)} %collective-permute-done.7.refs_5_), channel_id=1, source_target_pairs={{0,2},{1,3},{4,0},{5,1},{8,4},{9,5},{12,8},{13,9},{14,12},{15,13},... | collective-permute-start | bytes 552968 | tf_op jit(solution)/shard_map/ppermute | solution.py:53
  73.2 16.8 %collective-permute-start.15 = (bf16[48,1920]{1,0:T(8,128)(2,1)S(1)}, bf16[48,1920]{1,0:T(8,128)(2,1)S(1)}, u32[]{:S(2)}, u32[]{:S(2)}) collective-permute-start(bf16[48,1920]{1,0:T(8,128)(2,1)S(1)} %collective-permute-done.11.refs_2_), channel_id=1, source_target_pairs={{0,4},{1,5},{4,8},{5,9},{8,12},{9,13},{12,14},{13,15},{14,10},{15,... | collective-permute-start | bytes 552968 | tf_op jit(solution)/shard_map/ppermute | solution.py:53
  74.7 15.3 %collective-permute-start.16 = (bf16[48,1920]{1,0:T(8,128)(2,1)S(1)}, bf16[48,1920]{1,0:T(8,128)(2,1)S(1)}, u32[]{:S(2)}, u32[]{:S(2)}) collective-permute-start(bf16[48,1920]{1,0:T(8,128)(2,1)S(1)} %collective-permute-done.12.refs_6_), channel_id=1, source_target_pairs={{0,2},{1,3},{4,0},{5,1},{8,4},{9,5},{12,8},{13,9},{14,12},{15,13},... | collective-permute-start | bytes 552968 | tf_op jit(solution)/shard_map/ppermute | solution.py:53
  76.3 13.7 %collective-permute-start.14 = (bf16[48,1536]{1,0:T(8,128)(2,1)S(1)}, bf16[48,1536]{1,0:T(8,128)(2,1)S(1)}, u32[]{:S(2)}, u32[]{:S(2)}) collective-permute-start(bf16[48,1536]{1,0:T(8,128)(2,1)S(1)} %slice.87), channel_id=1, source_target_pairs={{0,2},{1,3},{4,0},{5,1},{8,4},{9,5},{12,8},{13,9},{14,12},{15,13},... | collective-permute-start | bytes 442376 | tf_op jit(solution)/shard_map/ppermute | solution.py:53
  77.2 12.8 %collective-permute-start.13 = (bf16[48,1536]{1,0:T(8,128)(2,1)S(1)}, bf16[48,1536]{1,0:T(8,128)(2,1)S(1)}, u32[]{:S(2)}, u32[]{:S(2)}) collective-permute-start(bf16[48,1536]{1,0:T(8,128)(2,1)S(1)} %slice.86), channel_id=1, source_target_pairs={{0,4},{1,5},{4,8},{5,9},{8,12},{9,13},{12,14},{13,15},{14,10},{15,... | collective-permute-start | bytes 442376 | tf_op jit(solution)/shard_map/ppermute | solution.py:53
  80.3 18.6 %copy-start = (bf16[256,768]{1,0:T(8,128)(2,1)}, bf16[256,768]{1,0:T(8,128)(2,1)S(1)}, u32[]{:S(2)}) copy-start(bf16[256,768]{1,0:T(8,128)(2,1)S(1)} %pad_maximum_fusion.refs_2_.refs_1_.refs_6_.refs_4_) | copy-start | bytes 1179652
  83.9 32.1 %copy-start.7 = (f32[24,768]{1,0:T(8,128)}, f32[24,768]{1,0:T(8,128)S(1)}, u32[]{:S(2)}) copy-start(f32[24,768]{1,0:T(8,128)S(1)} %get-tuple-element.232.refs_4_.refs_5_.refs_6_.refs_2_) | copy-start | bytes 221188
  90.7 7.4 %collective-permute-start.18 = (bf16[8,48,3072]{2,1,0:T(8,128)(2,1)S(1)}, bf16[8,48,3072]{2,1,0:T(8,128)(2,1)S(1)}, u32[]{:S(2)}, u32[]{:S(2)}) collective-permute-start(bf16[8,48,3072]{2,1,0:T(8,128)(2,1)S(1)} %pack.2.refs_1_), channel_id=1, source_target_pairs={{0,1},{1,0},{2,3},{3,2},{4,5},{5,4},{6,7},{7,6},{8,9},{9,8},{10,11... | collective-permute-start | bytes 7077896 | tf_op jit(solution)/shard_map/ppermute | solution.py:57
  90.8 7.3 %collective-permute-start.17 = (bf16[256,384]{1,0:T(8,128)(2,1)S(1)}, bf16[256,384]{1,0:T(8,128)(2,1)S(1)}, u32[]{:S(2)}, u32[]{:S(2)}) collective-permute-start(bf16[256,384]{1,0:T(8,128)(2,1)S(1)} %get-tuple-element.228.refs_2_), channel_id=1, source_target_pairs={{0,16},{16,0},{1,17},{17,1},{2,18},{18,2},{3,19},{19,3},{4,20},{20... | collective-permute-start | bytes 589832 | tf_op jit(solution)/shard_map/ppermute | solution.py:22
  92.2 11.0 %collective-permute-start.19 = (bf16[48,896]{1,0:T(8,128)(2,1)S(1)}, bf16[48,896]{1,0:T(8,128)(2,1)S(1)}, u32[]{:S(2)}, u32[]{:S(2)}) collective-permute-start(bf16[48,896]{1,0:T(8,128)(2,1)S(1)} %slice.88), channel_id=1, source_target_pairs={{0,4},{1,5},{4,8},{5,9},{8,12},{9,13},{12,14},{13,15},{14,10},{15,... | collective-permute-start | bytes 258056 | tf_op jit(solution)/shard_map/ppermute | solution.py:53
  93.3 9.9 %collective-permute-start.20 = (bf16[48,1024]{1,0:T(8,128)(2,1)S(1)}, bf16[48,1024]{1,0:T(8,128)(2,1)S(1)}, u32[]{:S(2)}, u32[]{:S(2)}) collective-permute-start(bf16[48,1024]{1,0:T(8,128)(2,1)S(1)} %slice.89), channel_id=1, source_target_pairs={{0,2},{1,3},{4,0},{5,1},{8,4},{9,5},{12,8},{13,9},{14,12},{15,13},... | collective-permute-start | bytes 294920 | tf_op jit(solution)/shard_map/ppermute | solution.py:53
  103.8 10.1 %collective-permute-start.22 = (bf16[8,48,1920]{2,1,0:T(8,128)(2,1)S(1)}, bf16[8,48,1920]{2,1,0:T(8,128)(2,1)S(1)}, u32[]{:S(2)}, u32[]{:S(2)}) collective-permute-start(bf16[8,48,1920]{2,1,0:T(8,128)(2,1)S(1)} %pack.3.refs_1_), channel_id=1, source_target_pairs={{0,1},{1,0},{2,3},{3,2},{4,5},{5,4},{6,7},{7,6},{8,9},{9,8},{10,11... | collective-permute-start | bytes 4423688 | tf_op jit(solution)/shard_map/ppermute | solution.py:57
  103.9 12.1 %collective-permute-start.21 = (bf16[256,768]{1,0:T(8,128)(2,1)S(1)}, bf16[256,768]{1,0:T(8,128)(2,1)}, u32[]{:S(2)}, u32[]{:S(2)}) collective-permute-start(bf16[256,768]{1,0:T(8,128)(2,1)S(1)} %get-tuple-element.238.refs_3_), channel_id=1, source_target_pairs={{0,16},{16,0},{1,17},{17,1},{2,18},{18,2},{3,19},{19,3},{4,20},{20... | collective-permute-start | bytes 1179656 | tf_op jit(solution)/shard_map/ppermute | solution.py:22
  105.3 29.2 %collective-permute-start.27 = (bf16[256,384]{1,0:T(8,128)(2,1)}, bf16[256,384]{1,0:T(8,128)(2,1)}, u32[]{:S(2)}, u32[]{:S(2)}) collective-permute-start(bf16[256,384]{1,0:T(8,128)(2,1)} %param.37), channel_id=1, source_target_pairs={{0,16},{16,0},{1,17},{17,1},{2,18},{18,2},{3,19},{19,3},{4,20},{20... | collective-permute-start | bytes 589832 | tf_op jit(solution)/shard_map/ppermute | solution.py:22
  120.3 7.3 %collective-permute-start.23 = (bf16[256,384]{1,0:T(8,128)(2,1)S(1)}, bf16[256,384]{1,0:T(8,128)(2,1)S(1)}, u32[]{:S(2)}, u32[]{:S(2)}) collective-permute-start(bf16[256,384]{1,0:T(8,128)(2,1)S(1)} %get-tuple-element.242.refs_2_), channel_id=1, source_target_pairs={{0,16},{16,0},{1,17},{17,1},{2,18},{18,2},{3,19},{19,3},{4,20},{20... | collective-permute-start | bytes 589832 | tf_op jit(solution)/shard_map/ppermute | solution.py:22
  133.8 16.0 %collective-permute-start.24 = (bf16[256,768]{1,0:T(8,128)(2,1)}, bf16[256,768]{1,0:T(8,128)(2,1)}, u32[]{:S(2)}, u32[]{:S(2)}) collective-permute-start(bf16[256,768]{1,0:T(8,128)(2,1)} %get-tuple-element.250.refs_2_), channel_id=1, source_target_pairs={{0,16},{16,0},{1,17},{17,1},{2,18},{18,2},{3,19},{19,3},{4,20},{20... | collective-permute-start | bytes 1179656 | tf_op jit(solution)/shard_map/ppermute | solution.py:22
  135.6 14.2 %collective-permute-start.25 = (f32[32,256]{1,0:T(8,128)}, f32[32,256]{1,0:T(8,128)}, u32[]{:S(2)}, u32[]{:S(2)}) collective-permute-start(f32[32,256]{1,0:T(8,128)} %get-tuple-element.251.refs_4_), channel_id=1, source_target_pairs={{0,16},{16,0},{1,17},{17,1},{2,18},{18,2},{3,19},{19,3},{4,20},{20... | collective-permute-start | bytes 98312 | tf_op jit(solution)/shard_map/ppermute | solution.py:22
  159.4 11.6 %collective-permute-start.28 = (bf16[256,768]{1,0:T(8,128)(2,1)}, bf16[256,768]{1,0:T(8,128)(2,1)}, u32[]{:S(2)}, u32[]{:S(2)}) collective-permute-start(bf16[256,768]{1,0:T(8,128)(2,1)} %get-tuple-element.259.refs_1_), channel_id=1, source_target_pairs={{0,16},{16,0},{1,17},{17,1},{2,18},{18,2},{3,19},{19,3},{4,20},{20... | collective-permute-start | bytes 1179656 | tf_op jit(solution)/shard_map/ppermute | solution.py:22
  171.0 124.3 %reduce-scatter.5.cloned.1.call-start = ((), (), s32[]{:S(2)}) async-start(), calls=%async_computation.6 | async-start | bytes 5013504 | tf_op jit(solution)/shard_map/reduce_scatter | solution.py:1162
  181.1 10.8 %collective-permute-start.29 = (bf16[256,768]{1,0:T(8,128)(2,1)S(1)}, bf16[256,768]{1,0:T(8,128)(2,1)S(1)}, u32[]{:S(2)}, u32[]{:S(2)}) collective-permute-start(bf16[256,768]{1,0:T(8,128)(2,1)S(1)} %get-tuple-element.270.refs_3_), channel_id=1, source_target_pairs={{0,16},{16,0},{1,17},{17,1},{2,18},{18,2},{3,19},{19,3},{4,20},{20... | collective-permute-start | bytes 1179656 | tf_op jit(solution)/shard_map/ppermute | solution.py:22
  199.1 10.3 %collective-permute-start.30 = (bf16[256,768]{1,0:T(8,128)(2,1)S(1)}, bf16[256,768]{1,0:T(8,128)(2,1)S(1)}, u32[]{:S(2)}, u32[]{:S(2)}) collective-permute-start(bf16[256,768]{1,0:T(8,128)(2,1)S(1)} %get-tuple-element.282.refs_2_), channel_id=1, source_target_pairs={{0,16},{16,0},{1,17},{17,1},{2,18},{18,2},{3,19},{19,3},{4,20},{20... | collective-permute-start | bytes 1179656 | tf_op jit(solution)/shard_map/ppermute | solution.py:22
  209.4 15.2 %collective-permute-start.31 = (bf16[8,48,3456]{2,1,0:T(8,128)(2,1)}, bf16[8,48,3456]{2,1,0:T(8,128)(2,1)}, u32[]{:S(2)}, u32[]{:S(2)}) collective-permute-start(bf16[8,48,3456]{2,1,0:T(8,128)(2,1)} %get-tuple-element.293), channel_id=1, source_target_pairs={{0,1},{1,0},{2,3},{3,2},{4,5},{5,4},{6,7},{7,6},{8,9},{9,8},{10,11... | collective-permute-start | bytes 7962632 | tf_op jit(solution)/shard_map/ppermute | solution.py:57
  210.4 4.3 %collective-permute-start.32 = (bf16[48,3456]{1,0:T(8,128)(2,1)S(1)}, bf16[48,3456]{1,0:T(8,128)(2,1)S(1)}, u32[]{:S(2)}, u32[]{:S(2)}) collective-permute-start(bf16[48,3456]{1,0:T(8,128)(2,1)S(1)} %dynamic-slice_bitcast_fusion.1), channel_id=1, source_target_pairs={{0,1},{1,0},{2,3},{3,2},{4,5},{5,4},{6,7},{7,6},{8,9},{9,8},{10,11... | collective-permute-start | bytes 995336 | tf_op jit(solution)/shard_map/ppermute | solution.py:57
  214.8 9.8 %collective-permute-start.35 = (bf16[48,1792]{1,0:T(8,128)(2,1)S(1)}, bf16[48,1792]{1,0:T(8,128)(2,1)S(1)}, u32[]{:S(2)}, u32[]{:S(2)}) collective-permute-start(bf16[48,1792]{1,0:T(8,128)(2,1)S(1)} %add_convert_fusion), channel_id=1, source_target_pairs={{0,2},{1,3},{4,0},{5,1},{8,4},{9,5},{12,8},{13,9},{14,12},{15,13},... | collective-permute-start | bytes 516104 | tf_op jit(solution)/shard_map/ppermute | solution.py:53
  215.9 8.7 %collective-permute-start.34 = (bf16[48,1664]{1,0:T(8,128)(2,1)S(1)}, bf16[48,1664]{1,0:T(8,128)(2,1)S(1)}, u32[]{:S(2)}, u32[]{:S(2)}) collective-permute-start(bf16[48,1664]{1,0:T(8,128)(2,1)S(1)} %add_convert_fusion.1), channel_id=1, source_target_pairs={{0,4},{1,5},{4,8},{5,9},{8,12},{9,13},{12,14},{13,15},{14,10},{15,... | collective-permute-start | bytes 479240 | tf_op jit(solution)/shard_map/ppermute | solution.py:53
  223.3 10.9 %collective-permute-start.33 = (bf16[256,768]{1,0:T(8,128)(2,1)S(1)}, bf16[256,768]{1,0:T(8,128)(2,1)S(1)}, u32[]{:S(2)}, u32[]{:S(2)}) collective-permute-start(bf16[256,768]{1,0:T(8,128)(2,1)S(1)} %get-tuple-element.318.refs_3_), channel_id=1, source_target_pairs={{0,16},{16,0},{1,17},{17,1},{2,18},{18,2},{3,19},{19,3},{4,20},{20... | collective-permute-start | bytes 1179656 | tf_op jit(solution)/shard_map/ppermute | solution.py:22
  226.1 9.1 %collective-permute-start.36 = (bf16[48,3456]{1,0:T(8,128)(2,1)S(1)}, bf16[48,3456]{1,0:T(8,128)(2,1)S(1)}, u32[]{:S(2)}, u32[]{:S(2)}) collective-permute-start(bf16[48,3456]{1,0:T(8,128)(2,1)S(1)} %get-tuple-element.310), channel_id=1, source_target_pairs={{0,4},{1,5},{4,8},{5,9},{8,12},{9,13},{12,14},{13,15},{14,10},{15,... | collective-permute-start | bytes 995336 | tf_op jit(solution)/shard_map/ppermute | solution.py:53
  227.0 8.7 %collective-permute-start.37 = (bf16[48,3456]{1,0:T(8,128)(2,1)S(1)}, bf16[48,3456]{1,0:T(8,128)(2,1)S(1)}, u32[]{:S(2)}, u32[]{:S(2)}) collective-permute-start(bf16[48,3456]{1,0:T(8,128)(2,1)S(1)} %get-tuple-element.311), channel_id=1, source_target_pairs={{0,2},{1,3},{4,0},{5,1},{8,4},{9,5},{12,8},{13,9},{14,12},{15,13},... | collective-permute-start | bytes 995336 | tf_op jit(solution)/shard_map/ppermute | solution.py:53
  238.1 11.2 %collective-permute-start.38 = (bf16[48,3456]{1,0:T(8,128)(2,1)}, bf16[48,3456]{1,0:T(8,128)(2,1)}, u32[]{:S(2)}, u32[]{:S(2)}) collective-permute-start(bf16[48,3456]{1,0:T(8,128)(2,1)} %get-tuple-element.315), channel_id=1, source_target_pairs={{0,4},{1,5},{4,8},{5,9},{8,12},{9,13},{12,14},{13,15},{14,10},{15,... | collective-permute-start | bytes 995336 | tf_op jit(solution)/shard_map/ppermute | solution.py:53
  239.4 11.6 %collective-permute-start.39 = (bf16[48,3456]{1,0:T(8,128)(2,1)}, bf16[48,3456]{1,0:T(8,128)(2,1)}, u32[]{:S(2)}, u32[]{:S(2)}) collective-permute-start(bf16[48,3456]{1,0:T(8,128)(2,1)} %get-tuple-element.316), channel_id=1, source_target_pairs={{0,2},{1,3},{4,0},{5,1},{8,4},{9,5},{12,8},{13,9},{14,12},{15,13},... | collective-permute-start | bytes 995336 | tf_op jit(solution)/shard_map/ppermute | solution.py:53
  240.3 18.9 %copy-start.17 = (bf16[768,1536]{1,0:T(8,128)(2,1)S(1)}, bf16[768,1536]{1,0:T(8,128)(2,1)}, u32[]{:S(2)}) copy-start(bf16[768,1536]{1,0:T(8,128)(2,1)} %get-tuple-element.347.keys) | copy-start | bytes 7077892
  247.9 15.9 %collective-permute-start.42 = (bf16[256,768]{1,0:T(8,128)(2,1)S(1)}, bf16[256,768]{1,0:T(8,128)(2,1)S(1)}, u32[]{:S(2)}, u32[]{:S(2)}) collective-permute-start(bf16[256,768]{1,0:T(8,128)(2,1)S(1)} %get-tuple-element.345.refs_2_), channel_id=1, source_target_pairs={{0,16},{16,0},{1,17},{17,1},{2,18},{18,2},{3,19},{19,3},{4,20},{20... | collective-permute-start | bytes 1179656 | tf_op jit(solution)/shard_map/ppermute | solution.py:22
  252.9 11.5 %collective-permute-start.40 = (bf16[48,3456]{1,0:T(8,128)(2,1)S(1)}, bf16[48,3456]{1,0:T(8,128)(2,1)S(1)}, u32[]{:S(2)}, u32[]{:S(2)}) collective-permute-start(bf16[48,3456]{1,0:T(8,128)(2,1)S(1)} %get-tuple-element.326), channel_id=1, source_target_pairs={{0,4},{1,5},{4,8},{5,9},{8,12},{9,13},{12,14},{13,15},{14,10},{15,... | collective-permute-start | bytes 995336 | tf_op jit(solution)/shard_map/ppermute | solution.py:53
  253.9 11.3 %collective-permute-start.41 = (bf16[48,3456]{1,0:T(8,128)(2,1)S(1)}, bf16[48,3456]{1,0:T(8,128)(2,1)}, u32[]{:S(2)}, u32[]{:S(2)}) collective-permute-start(bf16[48,3456]{1,0:T(8,128)(2,1)S(1)} %get-tuple-element.327), channel_id=1, source_target_pairs={{0,2},{1,3},{4,0},{5,1},{8,4},{9,5},{12,8},{13,9},{14,12},{15,13},... | collective-permute-start | bytes 995336 | tf_op jit(solution)/shard_map/ppermute | solution.py:53
  265.2 3.8 %collective-permute-start.43 = (bf16[8,48,2048]{2,1,0:T(8,128)(2,1)}, bf16[8,48,2048]{2,1,0:T(8,128)(2,1)}, u32[]{:S(2)}, u32[]{:S(2)}) collective-permute-start(bf16[8,48,2048]{2,1,0:T(8,128)(2,1)} %get-tuple-element.349), channel_id=1, source_target_pairs={{0,1},{1,0},{2,3},{3,2},{4,5},{5,4},{6,7},{7,6},{8,9},{9,8},{10,11... | collective-permute-start | bytes 4718600 | tf_op jit(solution)/shard_map/ppermute | solution.py:57
  270.1 5.8 %collective-permute-start.44 = (bf16[48,1024]{1,0:T(8,128)(2,1)S(1)}, bf16[48,1024]{1,0:T(8,128)(2,1)S(1)}, u32[]{:S(2)}, u32[]{:S(2)}) collective-permute-start(bf16[48,1024]{1,0:T(8,128)(2,1)S(1)} %get-tuple-element.351), channel_id=1, source_target_pairs={{0,4},{1,5},{4,8},{5,9},{8,12},{9,13},{12,14},{13,15},{14,10},{15,... | collective-permute-start | bytes 294920 | tf_op jit(solution)/shard_map/ppermute | solution.py:53
  270.8 5.9 %collective-permute-start.45 = (bf16[48,1024]{1,0:T(8,128)(2,1)S(1)}, bf16[48,1024]{1,0:T(8,128)(2,1)S(1)}, u32[]{:S(2)}, u32[]{:S(2)}) collective-permute-start(bf16[48,1024]{1,0:T(8,128)(2,1)S(1)} %get-tuple-element.352), channel_id=1, source_target_pairs={{0,2},{1,3},{4,0},{5,1},{8,4},{9,5},{12,8},{13,9},{14,12},{15,13},... | collective-permute-start | bytes 294920 | tf_op jit(solution)/shard_map/ppermute | solution.py:53
  272.2 18.7 %collective-permute-start.26 = (bf16[256,384]{1,0:T(8,128)(2,1)S(1)}, bf16[256,384]{1,0:T(8,128)(2,1)S(1)}, u32[]{:S(2)}, u32[]{:S(2)}) collective-permute-start(bf16[256,384]{1,0:T(8,128)(2,1)S(1)} %broadcast_select_fusion.3), channel_id=1, source_target_pairs={{0,16},{16,0},{1,17},{17,1},{2,18},{18,2},{3,19},{19,3},{4,20},{20... | collective-permute-start | bytes 589832 | tf_op jit(solution)/shard_map/ppermute | solution.py:22
  277.9 8.7 %collective-permute-start.46 = (bf16[48,2048]{1,0:T(8,128)(2,1)S(1)}, bf16[48,2048]{1,0:T(8,128)(2,1)S(1)}, u32[]{:S(2)}, u32[]{:S(2)}) collective-permute-start(bf16[48,2048]{1,0:T(8,128)(2,1)S(1)} %get-tuple-element.359), channel_id=1, source_target_pairs={{0,4},{1,5},{4,8},{5,9},{8,12},{9,13},{12,14},{13,15},{14,10},{15,... | collective-permute-start | bytes 589832 | tf_op jit(solution)/shard_map/ppermute | solution.py:53
  278.7 8.2 %collective-permute-start.47 = (bf16[48,2048]{1,0:T(8,128)(2,1)S(1)}, bf16[48,2048]{1,0:T(8,128)(2,1)S(1)}, u32[]{:S(2)}, u32[]{:S(2)}) collective-permute-start(bf16[48,2048]{1,0:T(8,128)(2,1)S(1)} %get-tuple-element.360), channel_id=1, source_target_pairs={{0,2},{1,3},{4,0},{5,1},{8,4},{9,5},{12,8},{13,9},{14,12},{15,13},... | collective-permute-start | bytes 589832 | tf_op jit(solution)/shard_map/ppermute | solution.py:53
  288.1 4.4 %collective-permute-start.54 = (bf16[24,1536]{1,0:T(8,128)(2,1)S(1)}, bf16[24,1536]{1,0:T(8,128)(2,1)S(1)}, u32[]{:S(2)}, u32[]{:S(2)}) collective-permute-start(bf16[24,1536]{1,0:T(8,128)(2,1)S(1)} %slice_select_fusion), channel_id=1, source_target_pairs={{0,16},{16,0},{1,17},{17,1},{2,18},{18,2},{3,19},{19,3},{4,20},{20... | collective-permute-start | bytes 221192 | tf_op jit(solution)/shard_map/ppermute | solution.py:22
  288.9 6.1 %collective-permute-start.48 = (bf16[48,2048]{1,0:T(8,128)(2,1)S(1)}, bf16[48,2048]{1,0:T(8,128)(2,1)S(1)}, u32[]{:S(2)}, u32[]{:S(2)}) collective-permute-start(bf16[48,2048]{1,0:T(8,128)(2,1)S(1)} %get-tuple-element.366), channel_id=1, source_target_pairs={{0,4},{1,5},{4,8},{5,9},{8,12},{9,13},{12,14},{13,15},{14,10},{15,... | collective-permute-start | bytes 589832 | tf_op jit(solution)/shard_map/ppermute | solution.py:53
  289.7 5.7 %collective-permute-start.49 = (bf16[48,2048]{1,0:T(8,128)(2,1)S(1)}, bf16[48,2048]{1,0:T(8,128)(2,1)S(1)}, u32[]{:S(2)}, u32[]{:S(2)}) collective-permute-start(bf16[48,2048]{1,0:T(8,128)(2,1)S(1)} %get-tuple-element.367), channel_id=1, source_target_pairs={{0,2},{1,3},{4,0},{5,1},{8,4},{9,5},{12,8},{13,9},{14,12},{15,13},... | collective-permute-start | bytes 589832 | tf_op jit(solution)/shard_map/ppermute | solution.py:53
  296.8 5.7 %collective-permute-start.50 = (bf16[48,2048]{1,0:T(8,128)(2,1)S(1)}, bf16[48,2048]{1,0:T(8,128)(2,1)S(1)}, u32[]{:S(2)}, u32[]{:S(2)}) collective-permute-start(bf16[48,2048]{1,0:T(8,128)(2,1)S(1)} %get-tuple-element.371), channel_id=1, source_target_pairs={{0,4},{1,5},{4,8},{5,9},{8,12},{9,13},{12,14},{13,15},{14,10},{15,... | collective-permute-start | bytes 589832 | tf_op jit(solution)/shard_map/ppermute | solution.py:53
  298.2 5.7 %collective-permute-start.51 = (bf16[48,2048]{1,0:T(8,128)(2,1)S(1)}, bf16[48,2048]{1,0:T(8,128)(2,1)S(1)}, u32[]{:S(2)}, u32[]{:S(2)}) collective-permute-start(bf16[48,2048]{1,0:T(8,128)(2,1)S(1)} %get-tuple-element.372), channel_id=1, source_target_pairs={{0,2},{1,3},{4,0},{5,1},{8,4},{9,5},{12,8},{13,9},{14,12},{15,13},... | collective-permute-start | bytes 589832 | tf_op jit(solution)/shard_map/ppermute | solution.py:53
  299.8 8.2 %collective-permute-start.53 = (bf16[48,3072]{1,0:T(8,128)(2,1)S(1)}, bf16[48,3072]{1,0:T(8,128)(2,1)S(1)}, u32[]{:S(2)}, u32[]{:S(2)}) collective-permute-start(bf16[48,3072]{1,0:T(8,128)(2,1)S(1)} %get-tuple-element.410), channel_id=1, source_target_pairs={{0,16},{16,0},{1,17},{17,1},{2,18},{18,2},{3,19},{19,3},{4,20},{20... | collective-permute-start | bytes 884744 | tf_op jit(solution)/shard_map/ppermute | solution.py:22
  305.1 4.9 %collective-permute-start.52 = (bf16[48,1280]{1,0:T(8,128)(2,1)S(1)}, bf16[48,1280]{1,0:T(8,128)(2,1)S(1)}, u32[]{:S(2)}, u32[]{:S(2)}) collective-permute-start(bf16[48,1280]{1,0:T(8,128)(2,1)S(1)} %pad_maximum_fusion.4), channel_id=1, source_target_pairs={{0,16},{16,0},{1,17},{17,1},{2,18},{18,2},{3,19},{19,3},{4,20},{20... | collective-permute-start | bytes 368648 | tf_op jit(solution)/shard_map/ppermute | solution.py:22
  (20 other events, 133.9 us)
Sparse Core Ops, SparseCore 0:
  26.8 39.8 all-gather.3
  68.8 40.9 all-gather.5
  111.4 35.3 all-gather.7
  171.2 51.2 reduce-scatter.2
  235.9 57.1 reduce-scatter.4
